TPU v7x, 32 devices: a whole 2x2x4 slice. The times are simulated.
32 devices in a mesh: groups: 2 (over y), seq: 4 (over z), qblk: 2 (over x), sub: 2 (over core).
Axes of the slice: x: 2, y: 2, z: 4, core: 2. Of those that a mesh axis runs over, the one named last changes fastest.
Arguments:
- queries: bfloat16 [8, 512, 32, 128], P(('groups', 'qblk', 'sub'), 'seq'), parts along dimension 0, may hold values from -9 to 9
- keys: bfloat16 [8, 512, 32, 128], P(('groups', 'qblk', 'sub'), 'seq'), parts along dimension 0, may hold values from -9 to 9
- values: bfloat16 [8, 512, 32, 128], P(('groups', 'qblk', 'sub'), 'seq'), parts along dimension 0, may hold values from -6 to 6
- vert_idx: int32 [64, 2], P('groups'), parts along dimension 0, may hold values from 0 to 15, as said below
- vert_cnt: int32 [64], P('groups'), parts along dimension 0, may hold values from 1 to 2, as said below
- slash_off: int32 [64, 2], P('groups'), parts along dimension 0, may hold values from 1 to 4, as said below
- slash_cnt: int32 [64], P('groups'), parts along dimension 0, may hold values from 1 to 2, as said below
Outputs:
- attended: bfloat16 [8, 512, 32, 128], P(('groups', 'qblk', 'sub'), 'seq'), parts along dimension 0
There are 2 independent parts, one for each index of `groups`. A program takes and returns all parts, laid end to end along the dimension named above; each array names one. Nothing has to cross between parts.
Inputs may be any that keep to these rules, and one draw needn't show every extreme that they name: `vert_idx`: per head the first vert_cnt entries are distinct block indices; some head lists block 0 and block 15. `vert_cnt`: some head uses all 2 entries; most heads use one or two. `slash_off`: per head the first slash_cnt entries are distinct; some head lists offset 4. `slash_cnt`: some head uses all 2 entries.
All inputs are finite; a program needn't handle non-finite values.
Results may differ from a plain program's by a relative error of at most 0.0034.
Values may be sent and summed in bfloat16 or wider, within the bound.
No kernel may reach another device: no remote copies, remote signals or barrier semaphores. Data moves between devices by JAX's collectives and lax.ppermute only.
A program may use at most 64 MiB of HBM per device.

v0:
```python
import jax
import jax.numpy as jnp
from jax import lax
from jax.sharding import PartitionSpec as P

BLK = 128


NEG_START = -1e30


def from_behind(value, axis, steps):
    count = lax.axis_size(axis)
    initial, last = (max(0, -steps), min(count, count - steps))
    return lax.ppermute(value, axis, [(source, source + steps) for source in range(initial, last)])


def pick_rows(table, chosen):
    heads = table.shape[0]
    onehot = chosen[:, None] == jnp.arange(heads, dtype=jnp.int32)[None, :]
    if table.ndim == 1:
        return jnp.sum(jnp.where(onehot, table[None, :], 0), axis=1)
    return jnp.sum(jnp.where(onehot[:, :, None], table[None, :, :], 0), axis=1)


def absorb(carry_state, scores, key_mask, tile_vals, einsum_form):
    run_max, run_sum, run_acc = carry_state
    scores = jnp.where(key_mask, scores, -jnp.inf)
    new_max = jnp.maximum(run_max, jnp.max(scores, axis=-1))
    factor = jnp.exp(run_max - new_max)
    weights = jnp.exp(scores - new_max[..., None])
    run_sum = run_sum * factor + jnp.sum(weights, axis=-1)
    run_acc = run_acc * factor[..., None] + jnp.einsum(
        einsum_form, weights.astype(jnp.bfloat16), tile_vals, preferred_element_type=jnp.float32
    )
    return (new_max, run_sum, run_acc)


def attend_head(
    q_head,
    k_head,
    v_head,
    key_prev,
    val_prev,
    sink_k,
    sink_v,
    v_list,
    v_count,
    s_list,
    s_count,
    slash_table,
    first_block,
):
    span_rows, head_width = q_head.shape
    span_blocks = span_rows // BLK
    scaling = head_width ** (-0.5)
    q_blocks = q_head.reshape(span_blocks, BLK, head_width)
    block_ids = first_block + jnp.arange(span_blocks, dtype=jnp.int32)
    carry_state = (
        jnp.full((span_blocks, BLK), NEG_START, jnp.float32),
        jnp.zeros((span_blocks, BLK), jnp.float32),
        jnp.zeros((span_blocks, BLK, head_width), jnp.float32),
    )
    k_blocks = k_head.reshape(span_blocks, BLK, head_width)
    v_blocks = v_head.reshape(span_blocks, BLK, head_width)
    scores = (
        jnp.einsum("pid,pjd->pij", q_blocks, k_blocks, preferred_element_type=jnp.float32) * scaling
    )
    causal = jnp.arange(BLK)[:, None] >= jnp.arange(BLK)[None, :]
    carry_state = absorb(carry_state, scores, causal[None], v_blocks, "pij,pjd->pid")
    ext_k = jnp.concatenate([key_prev, k_head], axis=0)
    ext_v = jnp.concatenate([val_prev, v_head], axis=0)

    def slash_step(turn_index, carry_state):
        offset = s_list[turn_index]
        start_row = span_rows - offset * BLK
        k_tile = lax.dynamic_slice_in_dim(ext_k, start_row, span_rows, 0).reshape(
            span_blocks, BLK, head_width
        )
        v_tile = lax.dynamic_slice_in_dim(ext_v, start_row, span_rows, 0).reshape(
            span_blocks, BLK, head_width
        )
        tile_scores = (
            jnp.einsum("pid,pjd->pij", q_blocks, k_tile, preferred_element_type=jnp.float32)
            * scaling
        )
        key_mask = (block_ids - offset >= 0)[:, None, None]
        return absorb(carry_state, tile_scores, key_mask, v_tile, "pij,pjd->pid")

    carry_state = lax.fori_loop(0, s_count, slash_step, carry_state)

    def vertical_step(turn_index, carry_state):
        column = v_list[turn_index]
        k_tile = sink_k[turn_index]
        v_tile = sink_v[turn_index]
        tile_scores = (
            jnp.einsum("pid,jd->pij", q_blocks, k_tile, preferred_element_type=jnp.float32)
            * scaling
        )
        distance = block_ids - column
        in_slash = (distance <= span_blocks) & slash_table[jnp.clip(distance, 0, span_blocks)]
        key_mask = ((distance > 0) & jnp.logical_not(in_slash))[:, None, None]
        return absorb(carry_state, tile_scores, key_mask, v_tile, "pij,jd->pid")

    carry_state = lax.fori_loop(0, v_count, vertical_step, carry_state)
    run_max, run_sum, run_acc = carry_state
    return (run_acc / run_sum[..., None]).astype(jnp.bfloat16).reshape(span_rows, head_width)


def body(queries, keys, values, vert_idx, vert_cnt, slash_off, slash_cnt):
    n_seq = lax.axis_size("seq")
    heads = queries.shape[2]
    per_dev = heads // n_seq
    head_order = jnp.arange(heads, dtype=jnp.int32)
    q_all, k_all, v_all = (
        lax.all_to_all(queries, "seq", split_axis=2, concat_axis=1, tiled=True),
        lax.all_to_all(keys, "seq", split_axis=2, concat_axis=1, tiled=True),
        lax.all_to_all(values, "seq", split_axis=2, concat_axis=1, tiled=True),
    )
    key_prev, val_prev = from_behind((k_all, v_all), ("qblk", "sub"), 1)
    span_rows = q_all.shape[1]
    head_width = q_all.shape[3]
    span_blocks = span_rows // BLK
    first_block = lax.axis_index(("qblk", "sub")) * span_blocks
    my_heads = lax.dynamic_slice_in_dim(head_order, lax.axis_index("seq") * per_dev, per_dev)
    v_lists = pick_rows(vert_idx, my_heads)
    v_counts = pick_rows(vert_cnt, my_heads)
    s_lists = pick_rows(slash_off, my_heads)
    s_counts = pick_rows(slash_cnt, my_heads)
    local_ids = v_lists - first_block
    owned = (local_ids >= 0) & (local_ids < span_blocks)
    clipped = jnp.clip(local_ids, 0, span_blocks - 1)
    slot_ids = jnp.arange(per_dev, dtype=jnp.int32)[:, None]
    k_grid = k_all[0].reshape(span_blocks, BLK, per_dev, head_width)
    v_grid = v_all[0].reshape(span_blocks, BLK, per_dev, head_width)
    zero_half = jnp.zeros((), jnp.bfloat16)
    picked_k = jnp.where(owned[:, :, None, None], k_grid[clipped, :, slot_ids, :], zero_half)
    picked_v = jnp.where(owned[:, :, None, None], v_grid[clipped, :, slot_ids, :], zero_half)
    sink_k, sink_v = (
        lax.psum(picked_k, ("qblk", "sub")).astype(jnp.float32),
        lax.psum(picked_v, ("qblk", "sub")).astype(jnp.float32),
    )
    sink_k = sink_k.astype(jnp.bfloat16)
    sink_v = sink_v.astype(jnp.bfloat16)
    s_width = slash_off.shape[1]
    s_live = jnp.arange(s_width, dtype=jnp.int32)[None, :] < s_counts[:, None]
    offset_ids = jnp.arange(span_blocks + 1, dtype=jnp.int32)
    slash_tables = jnp.any(
        (s_lists[:, :, None] == offset_ids[None, None, :]) & s_live[:, :, None], axis=1
    )
    results = []
    for slot in range(per_dev):
        results.append(
            attend_head(
                q_all[0, :, slot, :],
                k_all[0, :, slot, :],
                v_all[0, :, slot, :],
                key_prev[0, :, slot, :],
                val_prev[0, :, slot, :],
                sink_k[slot],
                sink_v[slot],
                v_lists[slot],
                v_counts[slot],
                s_lists[slot],
                s_counts[slot],
                slash_tables[slot],
                first_block,
            )
        )
    stacked = jnp.stack(results, axis=1)[None]
    restored = lax.all_to_all(stacked, "seq", split_axis=1, concat_axis=2, tiled=True)
    return restored


def solution(mesh):
    placed = (
        P(("groups", "qblk", "sub"), "seq", None, None),
        P(("groups", "qblk", "sub"), "seq", None, None),
        P(("groups", "qblk", "sub"), "seq", None, None),
        P("groups", None),
        P("groups"),
        P("groups", None),
        P("groups"),
    )
    return jax.shard_map(
        body,
        mesh=mesh,
        in_specs=placed,
        out_specs=P(("groups", "qblk", "sub"), "seq", None, None),
        check_vma=False,
    )
```

profile of v0, /device:TPU:12, one launch (start us, length us, event | category | flops | bytes accessed | tf_op | source)
XLA Modules:
  0.0 337.5 jit_solution(6275686621010512668)
XLA Ops:
  6.5 2.6 copy.191
  9.1 5.4 %all-to-all-start.1 = ((bf16[1,128,32,128]{3,1,0,2:T(8,128)(2,1)}), bf16[1,128,32,128]{3,1,0,2:T(8,128)(2,1)S(1)}, u32[]{:S(2)}, u32[]{:S(2)}) async-start(bf16[1,128,32,128]{3,1,0,2:T(8,128)(2,1)} %copy.191), calls=%async_computation.1 | async-start | bytes 2097152 | tf_op jit(solution)/shard_map/all_to_all | solution.py:117
  16.0 21.1 %all-to-all-done.1 = bf16[1,128,32,128]{3,1,0,2:T(8,128)(2,1)S(1)} async-done(((bf16[1,128,32,128]{3,1,0,2:T(8,128)(2,1)}), bf16[1,128,32,128]{3,1,0,2:T(8,128)(2,1)S(1)}, u32[]{:S(2)}, u32[]{:S(2)}) %all-to-all-start.1) | async-done | bytes 1048608 | tf_op jit(solution)/shard_map/all_to_all | solution.py:117
  37.0 6.8 %all-to-all-start.2 = ((bf16[1,128,32,128]{3,1,0,2:T(8,128)(2,1)}), bf16[1,128,32,128]{3,1,0,2:T(8,128)(2,1)S(1)}, u32[]{:S(2)}, u32[]{:S(2)}) async-start(bf16[1,128,32,128]{3,1,0,2:T(8,128)(2,1)} %copy.193), calls=%async_computation.2 | async-start | bytes 2097152 | tf_op jit(solution)/shard_map/all_to_all | solution.py:118
  46.1 19.6 %all-to-all-done.2 = bf16[1,128,32,128]{3,1,0,2:T(8,128)(2,1)S(1)} async-done(((bf16[1,128,32,128]{3,1,0,2:T(8,128)(2,1)}), bf16[1,128,32,128]{3,1,0,2:T(8,128)(2,1)S(1)}, u32[]{:S(2)}, u32[]{:S(2)}) %all-to-all-start.2) | async-done | bytes 1048608 | tf_op jit(solution)/shard_map/all_to_all | solution.py:118
  65.8 6.8 %all-to-all-start = ((bf16[1,128,32,128]{3,1,0,2:T(8,128)(2,1)}), bf16[1,128,32,128]{3,1,0,2:T(8,128)(2,1)S(1)}, u32[]{:S(2)}, u32[]{:S(2)}) async-start(bf16[1,128,32,128]{3,1,0,2:T(8,128)(2,1)} %copy.189), calls=%async_computation | async-start | bytes 2097152 | tf_op jit(solution)/shard_map/all_to_all | solution.py:116
  77.7 2.3 collective-permute-start.1
  79.9 4.1 %collective-permute-start = (bf16[1,512,8,128]{3,1,2,0:T(8,128)(2,1)}, bf16[1,512,8,128]{3,1,2,0:T(8,128)(2,1)}, u32[]{:S(2)}, u32[]{:S(2)}) collective-permute-start(bf16[1,512,8,128]{3,1,2,0:T(8,128)(2,1)} %bitcast.6), channel_id=1, source_target_pairs={{0,1},{1,2},{2,3},{4,5},{5,6},{6,7},{8,9},{9,10},{10,11},{12,13},{... | collective-permute-start | bytes 3145736 | tf_op jit(solution)/shard_map/ppermute | solution.py:15
  84.1 2.8 slice_bitcast_fusion.40
  86.9 2.6 slice_bitcast_fusion.41
  89.5 5.0 %all-to-all-done = bf16[1,128,32,128]{3,1,0,2:T(8,128)(2,1)S(1)} async-done(((bf16[1,128,32,128]{3,1,0,2:T(8,128)(2,1)}), bf16[1,128,32,128]{3,1,0,2:T(8,128)(2,1)S(1)}, u32[]{:S(2)}, u32[]{:S(2)}) %all-to-all-start) | async-done | bytes 1048608 | tf_op jit(solution)/shard_map/all_to_all | solution.py:116
  122.3 29.2 %all-reduce.3.cloned.1.call-done = (bf16[8,2,128,128]{3,2,1,0:T(8,128)(2,1)}, bf16[8,2,128,128]{3,2,1,0:T(8,128)(2,1)}) async-done(((bf16[8,2,128,128]{3,2,1,0:T(8,128)(2,1)}, bf16[8,2,128,128]{3,2,1,0:T(8,128)(2,1)}), (bf16[8,2,128,128]{3,2,1,0:T(8,128)(2,1)}, bf16[8,2,128,128]{3,2,1,0:T(8,128)(2,1)})) %all-reduce.3.cloned.1.call-update) | async-done | bytes 1048592 | tf_op jit(solution)/shard_map/psum | solution.py:140
  151.5 2.2 slice_bitcast_fusion.16
  153.8 2.2 slice_bitcast_fusion
  156.8 2.2 slice_bitcast_fusion.1
  160.5 5.3 %while.270 = (s32[]{:T(128)}, f32[4,128]{1,0:T(4,128)S(1)}, f32[4,128]{1,0:T(4,128)S(1)}, f32[4,128,128]{2,1,0:T(8,128)S(1)}, s32[]{:T(128)}, /*index=5*/s32[2]{...) while((s32[]{:T(128)}, f32[4,128]{1,0:T(4,128)S(1)}, ...), condition=%wide.region_82.83_spmd.clone, body=%wide.region_79.82_spmd.clone.sunk | while | flops 34145300 | bytes 2261341 | solution.py:90
  166.3 7.7 %while.271 = (s32[]{:T(128)}, f32[4,128]{1,0:T(4,128)S(1)}, f32[4,128]{1,0:T(4,128)S(1)}, f32[4,128,128]{2,1,0:T(8,128)S(1)}, s32[]{:T(128)}, /*index=5*/s32[2]{...) while((s32[]{:T(128)}, f32[4,128]{1,0:T(4,128)S(1)}, ...), condition=%wide.region_86.87_spmd.clone, body=%wide.region_83.86_spmd.clone.sunk | while | flops 34146360 | bytes 1806711 | solution.py:105
  175.3 10.6 %while.268 = (s32[]{:T(128)}, f32[4,128]{1,0:T(4,128)S(1)}, f32[4,128]{1,0:T(4,128)S(1)}, f32[4,128,128]{2,1,0:T(8,128)S(1)}, s32[]{:T(128)}, /*index=5*/s32[2]{...) while((s32[]{:T(128)}, f32[4,128]{1,0:T(4,128)S(1)}, ...), condition=%wide.region_72.73_spmd.clone, body=%wide.region_69.72_spmd.clone.sunk | while | flops 34145300 | bytes 2261273 | solution.py:90
  185.9 5.1 %while.269 = (s32[]{:T(128)}, f32[4,128]{1,0:T(4,128)S(1)}, f32[4,128]{1,0:T(4,128)S(1)}, f32[4,128,128]{2,1,0:T(8,128)S(1)}, s32[]{:T(128)}, /*index=5*/s32[2]{...) while((s32[]{:T(128)}, f32[4,128]{1,0:T(4,128)S(1)}, ...), condition=%wide.region_76.77_spmd.clone, body=%wide.region_73.76_spmd.clone.sunk | while | flops 34146360 | bytes 1544979 | solution.py:105
  194.3 4.8 %while.266 = (s32[]{:T(128)}, f32[4,128]{1,0:T(4,128)S(1)}, f32[4,128]{1,0:T(4,128)S(1)}, f32[4,128,128]{2,1,0:T(8,128)S(1)}, s32[]{:T(128)}, /*index=5*/s32[2]{...) while((s32[]{:T(128)}, f32[4,128]{1,0:T(4,128)S(1)}, ...), condition=%wide.region_62.63_spmd.clone, body=%wide.region_59.62_spmd.clone.sunk | while | flops 34145300 | bytes 2261273 | solution.py:90
  199.7 11.3 %while.267 = (s32[]{:T(128)}, f32[4,128]{1,0:T(4,128)S(1)}, f32[4,128]{1,0:T(4,128)S(1)}, f32[4,128,128]{2,1,0:T(8,128)S(1)}, s32[]{:T(128)}, /*index=5*/s32[2]{...) while((s32[]{:T(128)}, f32[4,128]{1,0:T(4,128)S(1)}, ...), condition=%wide.region_66.67_spmd.clone, body=%wide.region_63.66_spmd.clone.sunk | while | flops 34146360 | bytes 1806643 | solution.py:105
  211.7 6.9 %while.264 = (s32[]{:T(128)}, f32[4,128]{1,0:T(4,128)S(1)}, f32[4,128]{1,0:T(4,128)S(1)}, f32[4,128,128]{2,1,0:T(8,128)S(1)}, s32[]{:T(128)}, /*index=5*/s32[2]{...) while((s32[]{:T(128)}, f32[4,128]{1,0:T(4,128)S(1)}, ...), condition=%wide.region_52.53_spmd.clone, body=%wide.region_49.52_spmd.clone.sunk | while | flops 34145300 | bytes 2261273 | solution.py:90
  219.3 4.7 %while.265 = (s32[]{:T(128)}, f32[4,128]{1,0:T(4,128)S(1)}, f32[4,128]{1,0:T(4,128)S(1)}, f32[4,128,128]{2,1,0:T(8,128)S(1)}, s32[]{:T(128)}, /*index=5*/s32[2]{...) while((s32[]{:T(128)}, f32[4,128]{1,0:T(4,128)S(1)}, ...), condition=%wide.region_56.57_spmd.clone, body=%wide.region_53.56_spmd.clone.sunk | while | flops 34146360 | bytes 1544979 | solution.py:105
  226.6 8.9 %while.262 = (s32[]{:T(128)}, f32[4,128]{1,0:T(4,128)S(1)}, f32[4,128]{1,0:T(4,128)S(1)}, f32[4,128,128]{2,1,0:T(8,128)S(1)}, s32[]{:T(128)}, /*index=5*/s32[2]{...) while((s32[]{:T(128)}, f32[4,128]{1,0:T(4,128)S(1)}, ...), condition=%wide.region_42.43_spmd.clone, body=%wide.region_39.42_spmd.clone.sunk | while | flops 34145300 | bytes 2261273 | solution.py:90
  236.1 9.7 %while.263 = (s32[]{:T(128)}, f32[4,128]{1,0:T(4,128)S(1)}, f32[4,128]{1,0:T(4,128)S(1)}, f32[4,128,128]{2,1,0:T(8,128)S(1)}, s32[]{:T(128)}, /*index=5*/s32[2]{...) while((s32[]{:T(128)}, f32[4,128]{1,0:T(4,128)S(1)}, ...), condition=%wide.region_46.47_spmd.clone, body=%wide.region_43.46_spmd.clone.sunk | while | flops 34146360 | bytes 2069323 | solution.py:105
  246.5 3.7 %while.260 = (s32[]{:T(128)}, f32[4,128]{1,0:T(4,128)S(1)}, f32[4,128]{1,0:T(4,128)S(1)}, f32[4,128,128]{2,1,0:T(8,128)S(1)}, s32[]{:T(128)}, /*index=5*/s32[2]{...) while((s32[]{:T(128)}, f32[4,128]{1,0:T(4,128)S(1)}, ...), condition=%wide.region_32.33_spmd.clone, body=%wide.region_29.32_spmd.clone.sunk | while | flops 34145300 | bytes 2261273 | solution.py:90
  250.8 8.1 %while.261 = (s32[]{:T(128)}, f32[4,128]{1,0:T(4,128)S(1)}, f32[4,128]{1,0:T(4,128)S(1)}, f32[4,128,128]{2,1,0:T(8,128)S(1)}, s32[]{:T(128)}, /*index=5*/s32[2]{...) while((s32[]{:T(128)}, f32[4,128]{1,0:T(4,128)S(1)}, ...), condition=%wide.region_36.37_spmd.clone, body=%wide.region_33.36_spmd.clone.sunk | while | flops 34146360 | bytes 1544979 | solution.py:105
  260.7 7.2 %while.258 = (s32[]{:T(128)}, f32[4,128]{1,0:T(4,128)S(1)}, f32[4,128]{1,0:T(4,128)S(1)}, f32[4,128,128]{2,1,0:T(8,128)S(1)}, s32[]{:T(128)}, /*index=5*/s32[2]{...) while((s32[]{:T(128)}, f32[4,128]{1,0:T(4,128)S(1)}, ...), condition=%wide.region_22.23_spmd.clone, body=%wide.region_19.22_spmd.clone.sunk | while | flops 34145300 | bytes 2261273 | solution.py:90
  268.5 5.2 %while.259 = (s32[]{:T(128)}, f32[4,128]{1,0:T(4,128)S(1)}, f32[4,128]{1,0:T(4,128)S(1)}, f32[4,128,128]{2,1,0:T(8,128)S(1)}, s32[]{:T(128)}, /*index=5*/s32[2]{...) while((s32[]{:T(128)}, f32[4,128]{1,0:T(4,128)S(1)}, ...), condition=%wide.region_26.27_spmd.clone, body=%wide.region_23.26_spmd.clone.sunk | while | flops 34146360 | bytes 2069323 | solution.py:105
  274.4 7.0 %while.256 = (s32[]{:T(128)}, f32[4,128]{1,0:T(4,128)S(1)}, f32[4,128]{1,0:T(4,128)S(1)}, f32[4,128,128]{2,1,0:T(8,128)S(1)}, s32[]{:T(128)}, /*index=5*/s32[2]{...) while((s32[]{:T(128)}, f32[4,128]{1,0:T(4,128)S(1)}, ...), condition=%wide.region_7.8_spmd.clone, body=%wide.region_4.7_spmd.clone.sunk | while | flops 34145300 | bytes 2261273 | solution.py:90
  282.1 4.4 %while.257 = (s32[]{:T(128)}, f32[4,128]{1,0:T(4,128)S(1)}, f32[4,128]{1,0:T(4,128)S(1)}, f32[4,128,128]{2,1,0:T(8,128)S(1)}, s32[]{:T(128)}, /*index=5*/s32[2]{...) while((s32[]{:T(128)}, f32[4,128]{1,0:T(4,128)S(1)}, ...), condition=%wide.region_16.17_spmd.clone, body=%wide.region_13.16_spmd.clone.sunk | while | flops 34146360 | bytes 1544979 | solution.py:105
  289.3 40.2 %all_to_all.72 = bf16[1,512,8,128]{3,2,0,1:T(8,128)(2,1)S(1)} all-to-all(bf16[1,512,8,128]{3,2,0,1:T(8,128)(2,1)S(1)} %copy.205), channel_id=1, replica_groups=mesh['groups'=2,'seq'=4,'qblk'=2,'sub'=2] {'seq'}, dimensions={1} | all-to-all | bytes 2097152 | tf_op jit(solution)/shard_map/all_to_all | solution.py:171
  (530 shorter events, 132.8 us)
Async XLA Ops:
  9.1 5.5 %copy-start.13 = (bf16[1,128,32,128]{3,2,1,0:T(8,128)(2,1)S(1)}, bf16[1,128,32,128]{3,2,1,0:T(8,128)(2,1)}, u32[]{:S(2)}) copy-start(bf16[1,128,32,128]{3,2,1,0:T(8,128)(2,1)} %param.41) | copy-start | bytes 3145732
  9.1 27.9 %all-to-all-start.1 = ((bf16[1,128,32,128]{3,1,0,2:T(8,128)(2,1)}), bf16[1,128,32,128]{3,1,0,2:T(8,128)(2,1)S(1)}, u32[]{:S(2)}, u32[]{:S(2)}) async-start(bf16[1,128,32,128]{3,1,0,2:T(8,128)(2,1)} %copy.191), calls=%async_computation.1 | async-start | bytes 2097152 | tf_op jit(solution)/shard_map/all_to_all | solution.py:117
  16.0 27.8 %copy-start.14 = (bf16[1,128,32,128]{3,2,1,0:T(8,128)(2,1)S(1)}, bf16[1,128,32,128]{3,2,1,0:T(8,128)(2,1)}, u32[]{:S(2)}) copy-start(bf16[1,128,32,128]{3,2,1,0:T(8,128)(2,1)} %param.39) | copy-start | bytes 3145732
  37.0 28.7 %all-to-all-start.2 = ((bf16[1,128,32,128]{3,1,0,2:T(8,128)(2,1)}), bf16[1,128,32,128]{3,1,0,2:T(8,128)(2,1)S(1)}, u32[]{:S(2)}, u32[]{:S(2)}) async-start(bf16[1,128,32,128]{3,1,0,2:T(8,128)(2,1)} %copy.193), calls=%async_computation.2 | async-start | bytes 2097152 | tf_op jit(solution)/shard_map/all_to_all | solution.py:118
  65.8 28.7 %all-to-all-start = ((bf16[1,128,32,128]{3,1,0,2:T(8,128)(2,1)}), bf16[1,128,32,128]{3,1,0,2:T(8,128)(2,1)S(1)}, u32[]{:S(2)}, u32[]{:S(2)}) async-start(bf16[1,128,32,128]{3,1,0,2:T(8,128)(2,1)} %copy.189), calls=%async_computation | async-start | bytes 2097152 | tf_op jit(solution)/shard_map/all_to_all | solution.py:116
  72.5 79.0 %all-reduce.3.cloned.1.call-start = ((), (), s32[]{:S(2)}) async-start(), calls=%async_computation.4 | async-start | bytes 2097152 | tf_op jit(solution)/shard_map/psum | solution.py:140
  77.7 76.1 %collective-permute-start.1 = (bf16[1,512,8,128]{3,1,2,0:T(8,128)(2,1)}, bf16[1,512,8,128]{3,1,2,0:T(8,128)(2,1)}, u32[]{:S(2)}, u32[]{:S(2)}) collective-permute-start(bf16[1,512,8,128]{3,1,2,0:T(8,128)(2,1)} %bitcast.10), channel_id=1, source_target_pairs={{0,1},{1,2},{2,3},{4,5},{5,6},{6,7},{8,9},{9,10},{10,11},{12,13},{... | collective-permute-start | bytes 3145736 | tf_op jit(solution)/shard_map/ppermute | solution.py:15
  79.9 76.8 %collective-permute-start = (bf16[1,512,8,128]{3,1,2,0:T(8,128)(2,1)}, bf16[1,512,8,128]{3,1,2,0:T(8,128)(2,1)}, u32[]{:S(2)}, u32[]{:S(2)}) collective-permute-start(bf16[1,512,8,128]{3,1,2,0:T(8,128)(2,1)} %bitcast.6), channel_id=1, source_target_pairs={{0,1},{1,2},{2,3},{4,5},{5,6},{6,7},{8,9},{9,10},{10,11},{12,13},{... | collective-permute-start | bytes 3145736 | tf_op jit(solution)/shard_map/ppermute | solution.py:15
  108.3 2.3 copy-start.37
  108.5 2.3 copy-start
  109.1 3.0 copy-start.4
  109.2 3.0 copy-start.5
  110.8 2.5 copy-start.2
  153.7 2.3 copy-start.65
  153.7 2.2 copy-start.66
  156.8 2.2 copy-start.63
  156.8 2.2 copy-start.64
  175.3 10.6 %copy-start.20 = (bf16[2,128,128]{2,1,0:T(8,128)(2,1)S(1)}, bf16[2,128,128]{2,1,0:T(8,128)(2,1)}, u32[]{:S(2)}) copy-start(bf16[2,128,128]{2,1,0:T(8,128)(2,1)} %get-tuple-element.4354) | copy-start | bytes 196612
  175.3 10.6 %copy-start.27 = (bf16[2,128,128]{2,1,0:T(8,128)(2,1)S(1)}, bf16[2,128,128]{2,1,0:T(8,128)(2,1)}, u32[]{:S(2)}) copy-start(bf16[2,128,128]{2,1,0:T(8,128)(2,1)} %get-tuple-element.4352) | copy-start | bytes 196612
  185.9 5.1 %copy-start.57 = (bf16[512,128]{1,0:T(8,128)(2,1)S(1)}, bf16[512,128]{1,0:T(8,128)(2,1)}, u32[]{:S(2)}) copy-start(bf16[512,128]{1,0:T(8,128)(2,1)} %get-tuple-element.2408) | copy-start | bytes 393220
  185.9 5.1 %copy-start.58 = (bf16[512,128]{1,0:T(8,128)(2,1)S(1)}, bf16[512,128]{1,0:T(8,128)(2,1)}, u32[]{:S(2)}) copy-start(bf16[512,128]{1,0:T(8,128)(2,1)} %get-tuple-element.2409) | copy-start | bytes 393220
  211.7 6.9 %copy-start.18 = (bf16[2,128,128]{2,1,0:T(8,128)(2,1)S(1)}, bf16[2,128,128]{2,1,0:T(8,128)(2,1)}, u32[]{:S(2)}) copy-start(bf16[2,128,128]{2,1,0:T(8,128)(2,1)} %get-tuple-element.4174) | copy-start | bytes 196612
  211.7 6.9 %copy-start.26 = (bf16[2,128,128]{2,1,0:T(8,128)(2,1)S(1)}, bf16[2,128,128]{2,1,0:T(8,128)(2,1)}, u32[]{:S(2)}) copy-start(bf16[2,128,128]{2,1,0:T(8,128)(2,1)} %get-tuple-element.4172) | copy-start | bytes 196612
  219.2 4.7 %copy-start.51 = (bf16[512,128]{1,0:T(8,128)(2,1)S(1)}, bf16[512,128]{1,0:T(8,128)(2,1)}, u32[]{:S(2)}) copy-start(bf16[512,128]{1,0:T(8,128)(2,1)} %get-tuple-element.2406) | copy-start | bytes 393220
  219.3 4.7 %copy-start.52 = (bf16[512,128]{1,0:T(8,128)(2,1)S(1)}, bf16[512,128]{1,0:T(8,128)(2,1)}, u32[]{:S(2)}) copy-start(bf16[512,128]{1,0:T(8,128)(2,1)} %get-tuple-element.2407) | copy-start | bytes 393220
  246.5 3.7 %copy-start.16 = (bf16[2,128,128]{2,1,0:T(8,128)(2,1)S(1)}, bf16[2,128,128]{2,1,0:T(8,128)(2,1)}, u32[]{:S(2)}) copy-start(bf16[2,128,128]{2,1,0:T(8,128)(2,1)} %get-tuple-element.3994) | copy-start | bytes 196612
  246.5 3.7 %copy-start.24 = (bf16[2,128,128]{2,1,0:T(8,128)(2,1)S(1)}, bf16[2,128,128]{2,1,0:T(8,128)(2,1)}, u32[]{:S(2)}) copy-start(bf16[2,128,128]{2,1,0:T(8,128)(2,1)} %get-tuple-element.3992) | copy-start | bytes 196612
  250.8 8.1 %copy-start.43 = (bf16[512,128]{1,0:T(8,128)(2,1)S(1)}, bf16[512,128]{1,0:T(8,128)(2,1)}, u32[]{:S(2)}) copy-start(bf16[512,128]{1,0:T(8,128)(2,1)} %get-tuple-element.2404) | copy-start | bytes 393220
  250.8 8.1 %copy-start.44 = (bf16[512,128]{1,0:T(8,128)(2,1)S(1)}, bf16[512,128]{1,0:T(8,128)(2,1)}, u32[]{:S(2)}) copy-start(bf16[512,128]{1,0:T(8,128)(2,1)} %get-tuple-element.2405) | copy-start | bytes 393220
  250.8 8.1 %copy-start.47 = (bf16[512,128]{1,0:T(8,128)(2,1)S(1)}, bf16[512,128]{1,0:T(8,128)(2,1)}, u32[]{:S(2)}) copy-start(bf16[512,128]{1,0:T(8,128)(2,1)} %get-tuple-element.2401) | copy-start | bytes 393220
  250.8 8.1 %copy-start.48 = (bf16[512,128]{1,0:T(8,128)(2,1)S(1)}, bf16[512,128]{1,0:T(8,128)(2,1)}, u32[]{:S(2)}) copy-start(bf16[512,128]{1,0:T(8,128)(2,1)} %get-tuple-element.2402) | copy-start | bytes 393220
  274.4 7.1 %copy-start.22 = (bf16[2,128,128]{2,1,0:T(8,128)(2,1)S(1)}, bf16[2,128,128]{2,1,0:T(8,128)(2,1)}, u32[]{:S(2)}) copy-start(bf16[2,128,128]{2,1,0:T(8,128)(2,1)} %get-tuple-element.3812) | copy-start | bytes 196612
  (72 other events, 66.3 us)
Sparse Core Ops, SparseCore 0:
  113.5 37.9 all-reduce.2
where the time goes:
time: 344 us; the launch traced here: 337 us
  local copies, waits for them, and re-layouts  82.1 us (24%)
  waiting for transfers between devices  75 us (22%)
  other arithmetic  47.4 us (14%)
  blocking collectives  40.2 us (12%)
  loops' own time  35.1 us (10%)
  starting transfers between devices  25.4 us (7%)
  matrix products  17.9 us (5%)
  between operations  14.4 us (4%)
    all_to_all x1, blocking collectives, body(): lax.all_to_all(stacked, 'seq', split_axis=1, concat_axis=2, tiled=True)  40.2 us
    psum x1, waiting for transfers between devices, body(): lax.psum(picked_k, ('qblk', 'sub')).astype(jnp.float32)  29.2 us
    unnamed x184, local copies, waits for them, and re-layouts  24.6 us
    another operation x8, loops' own time, attend_head(): carry_state = lax.fori_loop(0, s_count, slash_step, carry_state)  22.4 us
    all_to_all x1, waiting for transfers between devices, body(): lax.all_to_all(keys, 'seq', split_axis=2, concat_axis=1, tiled=True)  21.1 us
    all_to_all x1, waiting for transfers between devices, body(): lax.all_to_all(values, 'seq', split_axis=2, concat_axis=1, tiled=True)  19.6 us
    another operation x8, loops' own time, attend_head(): carry_state = lax.fori_loop(0, v_count, vertical_step, carry_state)  12.7 us
    dynamic_slice x13, local copies, waits for them, and re-layouts, slash_step(): offset = s_list[turn_index]  9.24 us
  transfers between devices with their start and end apart: 6, of which 4 were waited for; matrix products, arithmetic and copies ran while one was open for 12% of the time, Pallas kernels for 0%

commit v1 on v0

--- a/solution.py
+++ b/solution.py
@@ -1,6 +1,10 @@
+import functools
+
 import jax
 import jax.numpy as jnp
 from jax import lax
+from jax.experimental import pallas as pl
+from jax.experimental.pallas import tpu as pltpu
 from jax.sharding import PartitionSpec as P
 
 BLK = 128
@@ -107,7 +111,7 @@
     return (run_acc / run_sum[..., None]).astype(jnp.bfloat16).reshape(span_rows, head_width)
 
 
-def body(queries, keys, values, vert_idx, vert_cnt, slash_off, slash_cnt):
+def spans_body(queries, keys, values, vert_idx, vert_cnt, slash_off, slash_cnt):
     n_seq = lax.axis_size("seq")
     heads = queries.shape[2]
     per_dev = heads // n_seq
@@ -172,6 +176,90 @@
     return restored
 
 
+PROMPT = ("qblk", "sub", "seq")
+
+
+def pair_scores(q, k_cols, scaling):
+    return lax.dot_general(
+        q, k_cols, (((1,), (1,)), ((), ())), preferred_element_type=jnp.float32
+    ) * scaling
+
+
+def attend_kernel(vert_idx, vert_cnt, slash_off, slash_cnt, qkv, out, *, scaling):
+    blocks, _, heads = qkv.shape[:3]
+    n_vert, n_slash = vert_idx.shape[1], slash_off.shape[1]
+    row = lax.broadcasted_iota(jnp.int32, (BLK, BLK), 0)
+    col = lax.broadcasted_iota(jnp.int32, (BLK, BLK), 1)
+    causal = row >= col
+
+    def unit(head, block):
+        cols, live = [block], []
+        for turn in range(n_slash):
+            offset = slash_off[head, turn]
+            live.append((turn < slash_cnt[head]) & (block >= offset))
+            cols.append(jnp.maximum(block - offset, 0))
+        for turn in range(n_vert):
+            column = vert_idx[head, turn]
+            distance = block - column
+            ok = (turn < vert_cnt[head]) & (distance > 0)
+            for other in range(n_slash):
+                hit = (other < slash_cnt[head]) & (slash_off[head, other] == distance)
+                ok = ok & jnp.logical_not(hit)
+            live.append(ok)
+            cols.append(column)
+        q = qkv[block, 0, head]
+        parts = [jnp.where(causal, pair_scores(q, qkv[block, 1, head], scaling), -jnp.inf)]
+        for column, ok in zip(cols[1:], live):
+            bias = jnp.where(ok, 0.0, -jnp.inf).astype(jnp.float32)
+            parts.append(pair_scores(q, qkv[column, 1, head], scaling) + bias)
+        scores = jnp.concatenate(parts, axis=1)
+        top = jnp.max(scores, axis=1, keepdims=True)
+        weights = jnp.exp(scores - top)
+        total = jnp.sum(weights, axis=1, keepdims=True)
+        vals = jnp.concatenate([qkv[column, 2, head] for column in cols], axis=0)
+        acc = jnp.dot(weights.astype(jnp.bfloat16), vals, preferred_element_type=jnp.float32)
+        out[block, head] = (acc / total).astype(jnp.bfloat16)
+
+    for head in range(heads):
+        @pl.loop(0, blocks // 4)
+        def _(step):
+            for inner in range(4):
+                unit(head, step * 4 + inner)
+
+
+def prompt_body(queries, keys, values, vert_idx, vert_cnt, slash_off, slash_cnt):
+    count = lax.axis_size(PROMPT)
+    heads, width = queries.shape[2:]
+    per_dev = heads // count
+    stacked = jnp.concatenate([queries, keys, values], axis=0)
+    stacked = stacked.reshape(3, BLK, count, per_dev, width).transpose(2, 0, 3, 1, 4)
+    qkv = lax.all_to_all(stacked, PROMPT, split_axis=0, concat_axis=0, tiled=True)
+    first = lax.axis_index(PROMPT) * per_dev
+    tables = [
+        lax.dynamic_slice_in_dim(table, first, per_dev, 0)
+        for table in (vert_idx, vert_cnt, slash_off, slash_cnt)
+    ]
+    smem = pl.BlockSpec(memory_space=pltpu.SMEM)
+    vmem = pl.BlockSpec(memory_space=pltpu.VMEM)
+    attended = pl.pallas_call(
+        functools.partial(attend_kernel, scaling=width ** (-0.5)),
+        out_shape=jax.ShapeDtypeStruct((count, per_dev, BLK, width), jnp.bfloat16),
+        in_specs=[smem] * 4 + [vmem],
+        out_specs=vmem,
+        compiler_params=pltpu.CompilerParams(vmem_limit_bytes=24 * 2**20),
+        name="attend",
+    )(*tables, qkv)
+    back = lax.all_to_all(attended, PROMPT, split_axis=0, concat_axis=0, tiled=True)
+    return back.reshape(heads, BLK, width).transpose(1, 0, 2)[None]
+
+
+def body(queries, keys, values, *tables):
+    devices = lax.axis_size(PROMPT)
+    if queries.shape[2] % devices == 0 and queries.shape[:2] == (1, BLK):
+        return prompt_body(queries, keys, values, *tables)
+    return spans_body(queries, keys, values, *tables)
+
+
 def solution(mesh):
     placed = (
         P(("groups", "qblk", "sub"), "seq", None, None),

time: 344 us -> 131 us (0.38)
  the two profiles are of different devices: /device:TPU:12 before, /device:TPU:0 now
where the time goes in v1:
time: 131 us
  waiting for transfers between devices  71.5 us (55%)
  blocking collectives  30.1 us (23%)
  Pallas kernels  13.2 us (10%)
  local copies, waits for them, and re-layouts  7.9 us (6%)
  starting transfers between devices  7.5 us (6%)
    all_to_all x1, waiting for transfers between devices, prompt_body(): lax.all_to_all(stacked, PROMPT, split_axis=0, concat_axis=0, tiled=True)  71.5 us
    all_to_all x1, blocking collectives, prompt_body(): lax.all_to_all(attended, PROMPT, split_axis=0, concat_axis=0, tiled=True)  30.1 us
    pallas_call x1, Pallas kernels, prompt_body(): pl.pallas_call(functools.partial(attend_kernel, scaling=width ** (-0.5)),...  13.2 us
    all_to_all x1, starting transfers between devices, prompt_body(): lax.all_to_all(stacked, PROMPT, split_axis=0, concat_axis=0, tiled=True)  7.5 us
    unnamed x15, local copies, waits for them, and re-layouts  3.97 us
  transfers between devices with their start and end apart: 1, of which 1 were waited for; matrix products, arithmetic and copies ran while one was open for 0% of the time, Pallas kernels for 0%

profile of v1, /device:TPU:0, one launch (start us, length us, event | category | flops | bytes accessed | tf_op | source)
XLA Modules:
  0.0 130.5 jit_solution(3070497892536004187)
XLA Ops:
  0.0 0.0 copy-start
  0.0 1.7 %copy.13 = bf16[1,128,32,128]{3,1,2,0:T(8,128)(2,1)S(1)} copy(bf16[1,128,32,128]{3,2,1,0:T(8,128)(2,1)} %param.7) | data formatting | bytes 2097152 | tf_op args[0]
  1.7 1.6 %copy.14 = bf16[1,128,32,128]{3,1,2,0:T(8,128)(2,1)S(1)} copy(bf16[1,128,32,128]{3,2,1,0:T(8,128)(2,1)} %param.8) | data formatting | bytes 2097152 | tf_op args[1]
  3.4 0.0 copy-done
  3.4 0.4 copy.15
  3.8 0.3 pad_maximum_fusion
  4.1 2.1 %copy.22 = bf16[3,128,16,2,128]{4,1,3,0,2:T(8,128)(2,1)} copy(bf16[3,128,16,2,128]{4,1,3,2,0:T(8,128)(2,1)S(1)} %bitcast.11) | data formatting | bytes 6291456 | tf_op jit(solution)/shard_map/reshape | solution.py:235
  6.2 0.0 copy-start.3
  6.2 0.0 copy-start.4
  6.2 0.0 copy-start.1
  6.2 0.0 copy-start.2
  6.2 7.5 %all-to-all-start = ((bf16[16,3,2,128,128]{4,3,2,1,0:T(8,128)(2,1)}), bf16[16,3,2,128,128]{4,3,2,1,0:T(8,128)(2,1)S(1)}, u32[]{:S(2)}, u32[]{:S(2)}) async-start(bf16[16,3,2,128,128]{4,3,2,1,0:T(8,128)(2,1)} %bitcast.10), calls=%async_computation | async-start | bytes 6291456 | tf_op jit(solution)/shard_map/all_to_all | solution.py:236
  13.7 0.0 copy-done.3
  13.7 0.1 dynamic_slice.13.vert_cnt
  13.8 0.0 copy-done.4
  13.8 0.1 dynamic_slice.15.slash_cnt
  13.9 0.0 copy-done.1
  13.9 0.0 copy-done.2
  13.9 0.1 constant_dynamic-slice_fusion
  14.0 0.1 copy.19.slash_off
  14.1 0.1 copy.18.vert_idx
  14.2 71.5 %all-to-all-done.qkv = bf16[16,3,2,128,128]{4,3,2,1,0:T(8,128)(2,1)S(1)} async-done(((bf16[16,3,2,128,128]{4,3,2,1,0:T(8,128)(2,1)}), bf16[16,3,2,128,128]{4,3,2,1,0:T(8,128)(2,1)S(1)}, u32[]{:S(2)}, u32[]{:S(2)}) %all-to-all-start) | async-done | bytes 3145760 | tf_op jit(solution)/shard_map/all_to_all | solution.py:236
  85.6 13.2 %attend.1 = bf16[16,2,128,128]{3,2,1,0:T(8,128)(2,1)S(1)} custom-call(s32[2,2]{1,0:T(2,128)S(1)} %copy.18.vert_idx, s32[2]{0:T(128)S(1)} %dynamic_slice.13.vert_cnt, s32[2,2]{1,0:T(2,128)S(1)} %copy.19.slash_off, s32[2]{0:T(128)S(1)} %dynamic_slice.15.slash_cnt, bf16[16,3,2,128,128]{4,3,2,1,0:T(8,128)(2,1)S(1)} %all-to-all-done.qkv), custom_call_target="tpu_custom_call" | custom-call | tf_op jit(solution)/shard_map/attend/pallas_call | solution.py:244
  98.8 30.1 %all_to_all.10 = bf16[16,2,128,128]{3,2,1,0:T(8,128)(2,1)S(1)} all-to-all(bf16[16,2,128,128]{3,2,1,0:T(8,128)(2,1)S(1)} %attend.1), channel_id=1, replica_groups=mesh['groups'=2,'seq'=4,'qblk'=2,'sub'=2] {'qblk','sub','seq'}, dimensions={0} | all-to-all | bytes 2097152 | tf_op jit(solution)/shard_map/all_to_all | solution.py:252
  128.9 1.6 %copy.23 = bf16[32,128,128]{2,0,1:T(8,128)(2,1)} copy(bf16[32,128,128]{2,1,0:T(8,128)(2,1)S(1)} %bitcast.12) | data formatting | bytes 2097152 | tf_op jit(solution)/shard_map/reshape | solution.py:253
Async XLA Ops:
  0.0 3.4 %copy-start = (bf16[1,128,32,128]{3,2,1,0:T(8,128)(2,1)S(1)}, bf16[1,128,32,128]{3,2,1,0:T(8,128)(2,1)}, u32[]{:S(2)}) copy-start(bf16[1,128,32,128]{3,2,1,0:T(8,128)(2,1)} %param.9) | copy-start | bytes 3145732
  6.2 7.5 %copy-start.3 = (s32[32]{0:T(128)S(1)}, s32[32]{0:T(128)}, u32[]{:S(2)}) copy-start(s32[32]{0:T(128)} %param.11) | copy-start | bytes 388
  6.2 7.6 %copy-start.4 = (s32[32]{0:T(128)S(1)}, s32[32]{0:T(128)}, u32[]{:S(2)}) copy-start(s32[32]{0:T(128)} %param.13) | copy-start | bytes 388
  6.2 7.7 %copy-start.1 = (s32[32,2]{0,1:T(2,128)S(1)}, s32[32,2]{0,1:T(2,128)}, u32[]{:S(2)}) copy-start(s32[32,2]{0,1:T(2,128)} %param.12) | copy-start | bytes 772
  6.2 7.7 %copy-start.2 = (s32[32,2]{0,1:T(2,128)S(1)}, s32[32,2]{0,1:T(2,128)}, u32[]{:S(2)}) copy-start(s32[32,2]{0,1:T(2,128)} %param.10) | copy-start | bytes 772
  6.2 79.4 %all-to-all-start = ((bf16[16,3,2,128,128]{4,3,2,1,0:T(8,128)(2,1)}), bf16[16,3,2,128,128]{4,3,2,1,0:T(8,128)(2,1)S(1)}, u32[]{:S(2)}, u32[]{:S(2)}) async-start(bf16[16,3,2,128,128]{4,3,2,1,0:T(8,128)(2,1)} %bitcast.10), calls=%async_computation | async-start | bytes 6291456 | tf_op jit(solution)/shard_map/all_to_all | solution.py:236

commit v2 on v0

--- a/solution.py
+++ b/solution.py
@@ -1,6 +1,10 @@
+import functools
+
 import jax
 import jax.numpy as jnp
 from jax import lax
+from jax.experimental import pallas as pl
+from jax.experimental.pallas import tpu as pltpu
 from jax.sharding import PartitionSpec as P
 
 BLK = 128
@@ -107,7 +111,7 @@
     return (run_acc / run_sum[..., None]).astype(jnp.bfloat16).reshape(span_rows, head_width)
 
 
-def body(queries, keys, values, vert_idx, vert_cnt, slash_off, slash_cnt):
+def spans_body(queries, keys, values, vert_idx, vert_cnt, slash_off, slash_cnt):
     n_seq = lax.axis_size("seq")
     heads = queries.shape[2]
     per_dev = heads // n_seq
@@ -172,6 +176,312 @@
     return restored
 
 
+GROUP = ("seq", "qblk")
+MIB = 2**20
+REGROUP_VMEM = 60 * MIB
+ANY = pl.BlockSpec(memory_space=pl.ANY)
+HBM = pl.BlockSpec(memory_space=pltpu.HBM)
+SMEM = pl.BlockSpec(memory_space=pltpu.SMEM)
+VMEM = pl.BlockSpec(memory_space=pltpu.VMEM)
+
+
+def swap_with(value, axes, mask):
+    count = lax.axis_size(axes)
+    return lax.ppermute(value, axes, [(source, source ^ mask) for source in range(count)])
+
+
+def first_head(place, masks, heads, groups):
+    half = groups // 2
+    return pl.multiple_of(((place[0] ^ masks[0]) // half) * (heads // 2), heads // 2)
+
+
+def regroup_kernel(place, *refs, tensors, takes, pieces, groups):
+    sources, parts = refs[:tensors], refs[tensors : tensors + len(pieces)]
+    staged, turned, load_sem, store_sem = refs[tensors + len(pieces) :]
+    count, per_group = turned.shape[0], turned.shape[2]
+    heads = sources[0].shape[1]
+    loads = [
+        pltpu.make_async_copy(
+            sources[tensor].at[:, pl.ds(first_head(place, masks, heads, groups), heads // 2)],
+            staged.at[at],
+            load_sem.at[at],
+        )
+        for at, (masks, tensor) in enumerate(takes)
+    ]
+    for load in loads:
+        load.start()
+    stores = []
+    for at, load in enumerate(loads):
+        load.wait()
+        heads_first = jnp.swapaxes(staged[at], 0, 1)
+        for group in range(count):
+            turned[group, at] = heads_first[group * per_group : (group + 1) * per_group]
+        for into, ((mask, begin, length), part) in enumerate(zip(pieces, parts)):
+            if begin + length == at + 1:
+                part_at = turned.at[(place[0] ^ mask) % count, pl.ds(begin, length)]
+                stores.append(pltpu.make_async_copy(part_at, part, store_sem.at[into]))
+                stores[-1].start()
+    for store in stores:
+        store.wait()
+
+
+def regroup(place, tensors, takes, pieces, groups):
+    tokens, heads, width = tensors[0].shape
+    part = (heads // groups, tokens, width)
+    parts = pl.pallas_call(
+        functools.partial(
+            regroup_kernel, tensors=len(tensors), takes=takes, pieces=pieces, groups=groups
+        ),
+        out_shape=[
+            jax.ShapeDtypeStruct((length,) + part, jnp.bfloat16) for _, _, length in pieces
+        ],
+        in_specs=[SMEM] + [HBM] * len(tensors),
+        out_specs=[ANY] * len(pieces),
+        scratch_shapes=[
+            pltpu.VMEM((len(takes), tokens, heads // 2, width), jnp.bfloat16),
+            pltpu.VMEM((groups // 2, len(takes)) + part, jnp.bfloat16),
+            pltpu.SemaphoreType.DMA((len(takes),)),
+            pltpu.SemaphoreType.DMA((len(pieces),)),
+        ],
+        compiler_params=pltpu.CompilerParams(vmem_limit_bytes=REGROUP_VMEM),
+        cost_estimate=pl.CostEstimate(flops=1, bytes_accessed=1, transcendentals=0),
+        name="regroup",
+    )(place, *tensors)
+    return dict(zip(pieces, parts))
+
+
+def ungroup_half(place, *refs, masks, groups):
+    parts = refs[: len(masks)]
+    out, staged, turned, load_sem, store_sem = refs[-5:]
+    count, per_group, tokens, width = staged.shape
+    heads = out.shape[1]
+    loads = [
+        pltpu.make_async_copy(part, staged.at[(place[0] ^ mask) % count], load_sem.at[at])
+        for at, (mask, part) in enumerate(zip(masks, parts))
+    ]
+    for load in loads:
+        load.start()
+    for load in loads:
+        load.wait()
+    heads_first = staged[...].reshape(count * per_group, tokens, width)
+    turned[...] = jnp.swapaxes(heads_first, 0, 1)
+    first = first_head(place, masks, heads, groups)
+    store = pltpu.make_async_copy(turned, out.at[:, pl.ds(first, heads // 2)], store_sem)
+    store.start()
+    store.wait()
+
+
+def ungroup(place, parts, masks, groups, begun=None):
+    per_group, tokens, width = parts[masks[0]].shape
+    shape = (tokens, groups * per_group, width)
+    return pl.pallas_call(
+        functools.partial(ungroup_half, masks=masks, groups=groups),
+        out_shape=jax.ShapeDtypeStruct(shape, jnp.bfloat16),
+        in_specs=[SMEM] + [ANY] * len(masks) + ([] if begun is None else [HBM]),
+        out_specs=HBM,
+        scratch_shapes=[
+            pltpu.VMEM((len(masks), per_group, tokens, width), jnp.bfloat16),
+            pltpu.VMEM((tokens, len(masks) * per_group, width), jnp.bfloat16),
+            pltpu.SemaphoreType.DMA((len(masks),)),
+            pltpu.SemaphoreType.DMA,
+        ],
+        input_output_aliases={} if begun is None else {1 + len(masks): 0},
+        compiler_params=pltpu.CompilerParams(vmem_limit_bytes=6 * MIB),
+        cost_estimate=pl.CostEstimate(flops=1, bytes_accessed=1, transcendentals=0),
+        name="ungroup",
+    )(place, *[parts[mask] for mask in masks], *([] if begun is None else [begun]))
+
+
+def block_of(place, mask, n_seq, n_qblk):
+    partner = place[0] ^ mask
+    return (2 * (partner % n_qblk) + place[1]) * n_seq + partner // n_qblk
+
+
+def gather_kernel(place, *refs, groups, n_seq, n_qblk):
+    own, out, sem = refs[:groups], refs[groups], refs[groups + 1]
+    copies = [
+        pltpu.make_async_copy(
+            part.at[pl.ds(0, 2)],
+            out.at[((place[0] ^ mask) % n_qblk) * n_seq + (place[0] ^ mask) // n_qblk],
+            sem.at[mask],
+        )
+        for mask, part in enumerate(own)
+    ]
+    for copy in copies:
+        copy.start()
+    for copy in copies:
+        copy.wait()
+
+
+def gather(place, parts):
+    groups = len(parts)
+    shape = (groups, 2) + parts[0].shape[1:]
+    return pl.pallas_call(
+        functools.partial(
+            gather_kernel,
+            groups=groups,
+            n_seq=lax.axis_size("seq"),
+            n_qblk=lax.axis_size("qblk"),
+        ),
+        out_shape=jax.ShapeDtypeStruct(shape, jnp.bfloat16),
+        in_specs=[SMEM] + [ANY] * groups,
+        out_specs=ANY,
+        scratch_shapes=[pltpu.SemaphoreType.DMA((groups,))],
+        compiler_params=pltpu.CompilerParams(vmem_limit_bytes=2 * MIB),
+        cost_estimate=pl.CostEstimate(flops=1, bytes_accessed=1, transcendentals=0),
+        name="gather",
+    )(place, *parts)
+
+
+def join_kernel(place, own, other, out, sem):
+    copies = [
+        pltpu.make_async_copy(own, out.at[place[1]], sem.at[0]),
+        pltpu.make_async_copy(other, out.at[1 - place[1]], sem.at[1]),
+    ]
+    for copy in copies:
+        copy.start()
+    for copy in copies:
+        copy.wait()
+
+
+def join(place, own, other):
+    return pl.pallas_call(
+        join_kernel,
+        out_shape=jax.ShapeDtypeStruct((2,) + own.shape, jnp.bfloat16),
+        in_specs=[SMEM, ANY, ANY],
+        out_specs=ANY,
+        scratch_shapes=[pltpu.SemaphoreType.DMA((2,))],
+        compiler_params=pltpu.CompilerParams(vmem_limit_bytes=2 * MIB),
+        cost_estimate=pl.CostEstimate(flops=1, bytes_accessed=1, transcendentals=0),
+        name="join",
+    )(place, own, other)
+
+
+def attend_kernel(place, tables, kv, *refs, masks, sizes, n_seq, n_qblk):
+    queries, outs = refs[: len(masks)], refs[len(masks) :]
+    heads, width = kv.shape[3], kv.shape[-1]
+    scaling = width ** (-0.5)
+    all_heads, n_vert, n_slash = sizes
+    vert_cnt = all_heads * n_vert
+    slash_off = vert_cnt + all_heads
+    slash_cnt = slash_off + all_heads * n_slash
+    key_row = lax.broadcasted_iota(jnp.int32, (BLK, BLK), 0)
+    query_col = lax.broadcasted_iota(jnp.int32, (BLK, BLK), 1)
+    causal = key_row <= query_col
+
+    def place_of(block):
+        span = block // n_seq
+        return span % 2, (span // 2) * n_seq + block % n_seq
+
+    def unit(query, out, slot, block):
+        head = place[0] * heads + slot
+        vert_live, slash_live = tables[vert_cnt + head], tables[slash_cnt + head]
+        offsets = [tables[slash_off + turn * all_heads + head] for turn in range(n_slash)]
+        cols, live = [block], []
+        for turn, offset in enumerate(offsets):
+            live.append((turn < slash_live) & (block >= offset))
+            cols.append(jnp.maximum(block - offset, 0))
+        for turn in range(n_vert):
+            column = tables[turn * all_heads + head]
+            distance = block - column
+            ok = (turn < vert_live) & (distance > 0)
+            for other, offset in enumerate(offsets):
+                ok = ok & jnp.logical_not((other < slash_live) & (offset == distance))
+            live.append(ok)
+            cols.append(column)
+        spots = [place_of(column) for column in cols]
+        keys = jnp.concatenate([kv[side, at, 0, slot] for side, at in spots], axis=0)
+        vals = jnp.concatenate([kv[side, at, 1, slot] for side, at in spots], axis=0)
+        scores = lax.dot_general(
+            keys, query[query.shape[0] - 1, slot], (((1,), (1,)), ((), ())), preferred_element_type=jnp.float32
+        )
+        parts = [jnp.where(causal, scores[:BLK], -jnp.inf)]
+        for at, ok in enumerate(live):
+            bias = jnp.where(ok, 0.0, -jnp.inf).astype(jnp.float32)
+            parts.append(scores[(at + 1) * BLK : (at + 2) * BLK] + bias)
+        top = functools.reduce(jnp.maximum, parts)
+        top = jnp.max(top, axis=0, keepdims=True)
+        weights = [jnp.exp((part - top) * scaling) for part in parts]
+        total = jnp.sum(functools.reduce(jnp.add, weights), axis=0, keepdims=True)
+        rounded = jnp.concatenate([weight.astype(jnp.bfloat16) for weight in weights], axis=0)
+        acc = lax.dot_general(
+            vals, rounded, (((0,), (0,)), ((), ())), preferred_element_type=jnp.float32
+        )
+        out[slot] = (acc / total).T.astype(jnp.bfloat16)
+
+    @pl.loop(0, heads)
+    def _(slot):
+        for mask, query, out in zip(masks, queries, outs):
+            unit(query, out, slot, block_of(place, mask, n_seq, n_qblk))
+
+
+def attend(place, tables, sizes, kv, queries, masks):
+    count = len(masks)
+    _, _, _, heads, tokens, width = kv.shape
+    outs = pl.pallas_call(
+        functools.partial(
+            attend_kernel,
+            masks=masks,
+            sizes=sizes,
+            n_seq=lax.axis_size("seq"),
+            n_qblk=lax.axis_size("qblk"),
+        ),
+        out_shape=[jax.ShapeDtypeStruct((heads, tokens, width), jnp.bfloat16)] * count,
+        in_specs=[SMEM] * 2 + [VMEM] * (1 + count),
+        out_specs=[VMEM] * count,
+        compiler_params=pltpu.CompilerParams(vmem_limit_bytes=12 * MIB),
+        cost_estimate=pl.CostEstimate(flops=1, bytes_accessed=1, transcendentals=0),
+        name="attend",
+    )(place, tables, kv, *[queries[mask] for mask in masks])
+    return dict(zip(masks, outs))
+
+
+def after(value, *others):
+    return lax.optimization_barrier((value, *others))[0]
+
+
+def group_body(queries, keys, values, *tables):
+    n_seq, n_qblk = lax.axis_size("seq"), lax.axis_size("qblk")
+    groups = n_seq * n_qblk
+    place = jnp.stack([lax.axis_index(GROUP), lax.axis_index("sub")]).astype(jnp.int32)
+    sizes = (queries.shape[2], tables[0].shape[1], tables[2].shape[1])
+    flat = jnp.concatenate([table.T.reshape(-1) for table in tables])
+    near, far = list(range(groups // 2)), list(range(groups // 2, groups))
+    def send(part, mask, *behind):
+        return swap_with(after(part, *behind) if behind else part, GROUP, mask)
+
+    keys, values, queries = keys[0], values[0], queries[0]
+    pieces = [(mask, 0, 2) for mask in far]
+    kv_far = regroup(place, (keys, values), [(far, 0), (far, 1)], pieces, groups)
+    takes = [(near, 0), (near, 1), (near, 2), (far, 2)]
+    pieces = [(mask, 0, 3) for mask in near] + [(mask, 3, 1) for mask in far]
+    rest = regroup(place, (keys, values, after(queries, flat)), takes, pieces, groups)
+    got = {mask: send(kv_far[mask, 0, 2], mask) for mask in far}
+    for mask in near:
+        got[mask] = send(rest[mask, 0, 3], mask) if mask else rest[mask, 0, 3]
+    own = gather(place, [got[mask] for mask in range(groups)])
+    whole = join(place, own, swap_with(own, "sub", 1))
+    arrived = {mask: got[mask] for mask in near}
+    for mask in far:
+        arrived[mask] = send(rest[mask, 3, 1], mask, got[mask])
+    outs = attend(place, flat, sizes, whole, arrived, near)
+    arrived[far[0]] = after(arrived[far[0]], outs[near[0]])
+    outs.update(attend(place, flat, sizes, whole, arrived, far))
+    back = {mask: send(outs[mask], mask) for mask in far}
+    for mask in near:
+        back[mask] = send(outs[mask], mask) if mask else outs[mask]
+    begun = ungroup(place, back, near, groups)
+    return ungroup(place, back, far, groups, begun)[None]
+
+
+def body(queries, keys, values, *tables):
+    groups, heads = lax.axis_size(GROUP), queries.shape[2]
+    fits = heads % groups == 0 and heads % 32 == 0 and queries.shape[:2] == (1, BLK)
+    if fits and groups & (groups - 1) == 0 and lax.axis_size("sub") == 2:
+        return group_body(queries, keys, values, *tables)
+    return spans_body(queries, keys, values, *tables)
+
+
 def solution(mesh):
     placed = (
         P(("groups", "qblk", "sub"), "seq", None, None),

time: 344 us -> 115 us (0.33); the launches traced: 337 us -> 115 us
  local copies, waits for them, and re-layouts: 82.1 us -> 1.2 us
  other arithmetic: 47.4 us -> 0.73 us
  blocking collectives: 40.2 us -> 0 us
  loops' own time: 35.1 us -> 0 us
  Pallas kernels: 0 us -> 23.1 us
  matrix products: 17.9 us -> 0 us
  waiting for transfers between devices: 75 us -> 60.1 us
  between operations: 14.4 us -> 0.18 us
  starting transfers between devices: 25.4 us -> 29.6 us
    ppermute x2 -> x19, waiting for transfers between devices: 0.01 us -> 60.1 us  [swap_with(): lax.ppermute(value, axes, [(source, source ^ mask) for source in range(co...]
    all_to_all x3 -> x0, waiting for transfers between devices: 45.7 us -> none  [the longest x1 21.1 us: body(): lax.all_to_all(keys, 'seq', split_axis=2, concat_axis=1, tiled=True)]
    all_to_all x1 -> x0, blocking collectives: 40.2 us -> none  [body(): lax.all_to_all(stacked, 'seq', split_axis=1, concat_axis=2, tiled=True)]
    another operation x16 -> x0, loops' own time: 35.1 us -> none  [the longest x8 22.4 us: attend_head(): carry_state = lax.fori_loop(0, s_count, slash_step, carry_state)]
    psum x1 -> x0, waiting for transfers between devices: 29.2 us -> none  [body(): lax.psum(picked_k, ('qblk', 'sub')).astype(jnp.float32)]
    unnamed x184 -> x26, local copies, waits for them, and re-layouts: 24.6 us -> 1.04 us
    ppermute x2 -> x19, starting transfers between devices: 6.41 us -> 29.6 us  [swap_with(): lax.ppermute(value, axes, [(source, source ^ mask) for source in range(co...]
    pallas_call x0 -> x8, Pallas kernels: none -> 23.1 us  [the longest x2 10.3 us: attend(): pl.pallas_call(functools.partial(attend_kernel, masks=masks, sizes=sizes,...]
  transfers between devices with their start and end apart: 6 -> 19, of which waited for: 4 -> 12; matrix products, arithmetic and copies ran while one was open for 12% -> 0% of each run, Pallas kernels for 0% -> 15%
where the time goes in v2:
time: 115 us
  waiting for transfers between devices  60.1 us (52%)
  starting transfers between devices  29.6 us (26%)
  Pallas kernels  23.1 us (20%)
  local copies, waits for them, and re-layouts  1.2 us (1%)
    ppermute x19, waiting for transfers between devices, swap_with(): lax.ppermute(value, axes, [(source, source ^ mask) for source in range(co...  60.1 us
    ppermute x19, starting transfers between devices, swap_with(): lax.ppermute(value, axes, [(source, source ^ mask) for source in range(co...  29.6 us
    pallas_call x2, Pallas kernels, attend(): pl.pallas_call(functools.partial(attend_kernel, masks=masks, sizes=sizes,...  10.3 us
    pallas_call x2, Pallas kernels, regroup(): pl.pallas_call(functools.partial(regroup_kernel, tensors=len(tensors), ta...  6.68 us
    pallas_call x2, Pallas kernels, ungroup(): pl.pallas_call(functools.partial(ungroup_half, masks=masks, groups=groups...  4.41 us
  transfers between devices with their start and end apart: 19, of which 12 were waited for; matrix products, arithmetic and copies ran while one was open for 0% of the time, Pallas kernels for 15%

profile of v2, /device:TPU:12, one launch (start us, length us, event | category | flops | bytes accessed | tf_op | source)
XLA Modules:
  0.0 114.9 jit_solution(8447841789001227673)
XLA Ops:
  0.7 3.1 %regroup.3 = (bf16[2,4,128,128]{3,2,1,0:T(8,128)(2,1)}, bf16[2,4,128,128]{3,2,1,0:T(8,128)(2,1)}, bf16[2,4,128,128]{3,2,1,0:T(8,128)(2,1)}, bf16[2,4,128,128]{3,2,1,0:T(8,128)(2,1)}) custom-call(s32[2]{0:T(128)} %pad_add_fusion.1.place, bf16[128,32,128]{2,1,0:T(8,128)(2,1)} %bitcast.8, bf16[128,32,128]{2,1,0:T(8,128)(2,1)} %bitcast.10), custom_call_target="tpu_custom_call" | custom-call | flops 1 | bytes 1 | tf_op jit(solution)/shard_map/regroup/pallas_call | solution.py:231
  3.8 2.7 %collective-permute-start.3 = (bf16[2,4,128,128]{3,2,1,0:T(8,128)(2,1)}, bf16[2,4,128,128]{3,2,1,0:T(8,128)(2,1)S(1)}, u32[]{:S(2)}, u32[]{:S(2)}) collective-permute-start(bf16[2,4,128,128]{3,2,1,0:T(8,128)(2,1)} %get-tuple-element.36), channel_id=1, source_target_pairs={{0,8},{2,10},{4,12},{6,14},{8,0},{10,2},{12,4},{14,6},{1,9},{3,11}... | collective-permute-start | bytes 786440 | tf_op jit(solution)/shard_map/ppermute | solution.py:190
  6.4 1.3 %collective-permute-start.4 = (bf16[2,4,128,128]{3,2,1,0:T(8,128)(2,1)}, bf16[2,4,128,128]{3,2,1,0:T(8,128)(2,1)S(1)}, u32[]{:S(2)}, u32[]{:S(2)}) collective-permute-start(bf16[2,4,128,128]{3,2,1,0:T(8,128)(2,1)} %get-tuple-element.37), channel_id=1, source_target_pairs={{0,10},{2,8},{4,14},{6,12},{8,2},{10,0},{12,6},{14,4},{1,11},{3,9}... | collective-permute-start | bytes 786440 | tf_op jit(solution)/shard_map/ppermute | solution.py:190
  8.0 3.6 %regroup.2 = (bf16[3,4,128,128]{3,2,1,0:T(8,128)(2,1)}, bf16[3,4,128,128]{3,2,1,0:T(8,128)(2,1)}, bf16[3,4,128,128]{3,2,1,0:T(8,128)(2,1)}, bf16[3,4,128,128]{3,...) custom-call(s32[2]{0:T(128)} %pad_add_fusion.1.place, ...), custom_call_target="tpu_custom_call" | custom-call | flops 1 | bytes 1 | tf_op jit(solution)/shard_map/regroup/pallas_call | solution.py:231
  12.6 2.5 %collective-permute-start.2 = (bf16[3,4,128,128]{3,2,1,0:T(8,128)(2,1)}, bf16[3,4,128,128]{3,2,1,0:T(8,128)(2,1)S(1)}, u32[]{:S(2)}, u32[]{:S(2)}) collective-permute-start(bf16[3,4,128,128]{3,2,1,0:T(8,128)(2,1)} %get-tuple-element.35), channel_id=1, source_target_pairs={{0,6},{2,4},{4,2},{6,0},{8,14},{10,12},{12,10},{14,8},{1,7},{3,5},... | collective-permute-start | bytes 1179656 | tf_op jit(solution)/shard_map/ppermute | solution.py:190
  15.1 8.5 %collective-permute-done.3.refs_4_ = bf16[2,4,128,128]{3,2,1,0:T(8,128)(2,1)S(1)} collective-permute-done((bf16[2,4,128,128]{3,2,1,0:T(8,128)(2,1)}, bf16[2,4,128,128]{3,2,1,0:T(8,128)(2,1)S(1)}, u32[]{:S(2)}, u32[]{:S(2)}) %collective-permute-start.3) | collective-permute-done | bytes 262176 | tf_op jit(solution)/shard_map/ppermute | solution.py:190
  24.1 5.1 %collective-permute-done.4.refs_5_ = bf16[2,4,128,128]{3,2,1,0:T(8,128)(2,1)S(1)} collective-permute-done((bf16[2,4,128,128]{3,2,1,0:T(8,128)(2,1)}, bf16[2,4,128,128]{3,2,1,0:T(8,128)(2,1)S(1)}, u32[]{:S(2)}, u32[]{:S(2)}) %collective-permute-start.4) | collective-permute-done | bytes 262176 | tf_op jit(solution)/shard_map/ppermute | solution.py:190
  29.2 1.4 %collective-permute-start.6 = (bf16[2,4,128,128]{3,2,1,0:T(8,128)(2,1)S(1)}, bf16[2,4,128,128]{3,2,1,0:T(8,128)(2,1)S(1)}, u32[]{:S(2)}, u32[]{:S(2)}) collective-permute-start(bf16[2,4,128,128]{3,2,1,0:T(8,128)(2,1)S(1)} %copy-done.5), channel_id=1, source_target_pairs={{0,14},{2,12},{4,10},{6,8},{8,6},{10,4},{12,2},{14,0},{1,15},{3,13... | collective-permute-start | bytes 786440 | tf_op jit(solution)/shard_map/ppermute | solution.py:190
  30.6 6.2 %collective-permute-done.5.refs_6_ = bf16[2,4,128,128]{3,2,1,0:T(8,128)(2,1)S(1)} collective-permute-done((bf16[2,4,128,128]{3,2,1,0:T(8,128)(2,1)S(1)}, bf16[2,4,128,128]{3,2,1,0:T(8,128)(2,1)S(1)}, u32[]{:S(2)}, u32[]{:S(2)}) %collective-permute-start.5) | collective-permute-done | bytes 262176 | tf_op jit(solution)/shard_map/ppermute | solution.py:190
  36.7 15.5 %collective-permute-done.6.refs_7_ = bf16[2,4,128,128]{3,2,1,0:T(8,128)(2,1)S(1)} collective-permute-done((bf16[2,4,128,128]{3,2,1,0:T(8,128)(2,1)S(1)}, bf16[2,4,128,128]{3,2,1,0:T(8,128)(2,1)S(1)}, u32[]{:S(2)}, u32[]{:S(2)}) %collective-permute-start.6) | collective-permute-done | bytes 262176 | tf_op jit(solution)/shard_map/ppermute | solution.py:190
  52.3 1.0 copy-done
  54.2 4.5 %collective-permute-start.8 = (bf16[1,4,128,128]{3,2,1,0:T(8,128)(2,1)S(1)}, bf16[1,4,128,128]{3,2,1,0:T(8,128)(2,1)S(1)}, u32[]{:S(2)}, u32[]{:S(2)}) collective-permute-start(bf16[1,4,128,128]{3,2,1,0:T(8,128)(2,1)S(1)} %copy-done.10), channel_id=1, source_target_pairs={{0,8},{2,10},{4,12},{6,14},{8,0},{10,2},{12,4},{14,6},{1,9},{3,11}... | collective-permute-start | bytes 393224 | tf_op jit(solution)/shard_map/ppermute | solution.py:190
  58.7 2.0 %collective-permute-start.10 = (bf16[1,4,128,128]{3,2,1,0:T(8,128)(2,1)S(1)}, bf16[1,4,128,128]{3,2,1,0:T(8,128)(2,1)S(1)}, u32[]{:S(2)}, u32[]{:S(2)}) collective-permute-start(bf16[1,4,128,128]{3,2,1,0:T(8,128)(2,1)S(1)} %copy-done.8), channel_id=1, source_target_pairs={{0,12},{2,14},{4,8},{6,10},{8,4},{10,6},{12,0},{14,2},{1,13},{3,15... | collective-permute-start | bytes 393224 | tf_op jit(solution)/shard_map/ppermute | solution.py:190
  60.7 2.8 %collective-permute-start.9 = (bf16[1,4,128,128]{3,2,1,0:T(8,128)(2,1)S(1)}, bf16[1,4,128,128]{3,2,1,0:T(8,128)(2,1)S(1)}, u32[]{:S(2)}, u32[]{:S(2)}) collective-permute-start(bf16[1,4,128,128]{3,2,1,0:T(8,128)(2,1)S(1)} %copy-done.7), channel_id=1, source_target_pairs={{0,10},{2,8},{4,14},{6,12},{8,2},{10,0},{12,6},{14,4},{1,11},{3,9}... | collective-permute-start | bytes 393224 | tf_op jit(solution)/shard_map/ppermute | solution.py:190
  63.5 0.8 join.1.kv
  64.4 5.1 %attend.2 = (bf16[4,128,128]{2,1,0:T(8,128)(2,1)S(1)}, bf16[4,128,128]{2,1,0:T(8,128)(2,1)S(1)}, bf16[4,128,128]{2,1,0:T(8,128)(2,1)S(1)}, bf16[4,128,128]{2,1,0:T(8,128)(2,1)S(1)}) custom-call(s32[2]{0:T(128)S(1)} %copy-done.2, s32[192]{0:T(256)S(1)} %pad_add_fusion.tables, bf16[2,8,2,4,128,128]{5,4,3,2,1,0:T(8,128)(2,1)S(1)} %join.1.kv, ...), custom_call_target="tpu_custom_call" | custom-call | flops 1 | bytes 1 | tf_op jit(solution)/shard_map/attend/pallas_call | solution.py:421
  70.1 2.4 %collective-permute-done.8.refs_0_ = bf16[1,4,128,128]{3,2,1,0:T(8,128)(2,1)S(1)} collective-permute-done((bf16[1,4,128,128]{3,2,1,0:T(8,128)(2,1)S(1)}, bf16[1,4,128,128]{3,2,1,0:T(8,128)(2,1)S(1)}, u32[]{:S(2)}, u32[]{:S(2)}) %collective-permute-start.8) | collective-permute-done | bytes 131104 | tf_op jit(solution)/shard_map/ppermute | solution.py:190
  72.4 1.6 %collective-permute-start.17 = (bf16[4,128,128]{2,1,0:T(8,128)(2,1)S(1)}, bf16[4,128,128]{2,1,0:T(8,128)(2,1)S(1)}, u32[]{:S(2)}, u32[]{:S(2)}) collective-permute-start(bf16[4,128,128]{2,1,0:T(8,128)(2,1)S(1)} %get-tuple-element.55), channel_id=1, source_target_pairs={{0,4},{2,6},{4,0},{6,2},{8,12},{10,14},{12,8},{14,10},{1,5},{3,7},... | collective-permute-start | bytes 393224 | tf_op jit(solution)/shard_map/ppermute | solution.py:190
  74.0 1.4 %collective-permute-done.11.refs_3_ = bf16[1,4,128,128]{3,2,1,0:T(8,128)(2,1)S(1)} collective-permute-done((bf16[1,4,128,128]{3,2,1,0:T(8,128)(2,1)S(1)}, bf16[1,4,128,128]{3,2,1,0:T(8,128)(2,1)S(1)}, u32[]{:S(2)}, u32[]{:S(2)}) %collective-permute-start.11) | collective-permute-done | bytes 131104 | tf_op jit(solution)/shard_map/ppermute | solution.py:190
  75.4 2.8 %collective-permute-done.10.refs_2_ = bf16[1,4,128,128]{3,2,1,0:T(8,128)(2,1)S(1)} collective-permute-done((bf16[1,4,128,128]{3,2,1,0:T(8,128)(2,1)S(1)}, bf16[1,4,128,128]{3,2,1,0:T(8,128)(2,1)S(1)}, u32[]{:S(2)}, u32[]{:S(2)}) %collective-permute-start.10) | collective-permute-done | bytes 131104 | tf_op jit(solution)/shard_map/ppermute | solution.py:190
  78.2 2.7 %collective-permute-done.9.refs_1_ = bf16[1,4,128,128]{3,2,1,0:T(8,128)(2,1)S(1)} collective-permute-done((bf16[1,4,128,128]{3,2,1,0:T(8,128)(2,1)S(1)}, bf16[1,4,128,128]{3,2,1,0:T(8,128)(2,1)S(1)}, u32[]{:S(2)}, u32[]{:S(2)}) %collective-permute-start.9) | collective-permute-done | bytes 131104 | tf_op jit(solution)/shard_map/ppermute | solution.py:190
  80.9 5.3 %attend.3 = (bf16[4,128,128]{2,1,0:T(8,128)(2,1)S(1)}, bf16[4,128,128]{2,1,0:T(8,128)(2,1)S(1)}, bf16[4,128,128]{2,1,0:T(8,128)(2,1)S(1)}, bf16[4,128,128]{2,1,0:T(8,128)(2,1)S(1)}) custom-call(s32[2]{0:T(128)S(1)} %copy-done.2, s32[192]{0:T(256)S(1)} %pad_add_fusion.tables, bf16[2,8,2,4,128,128]{5,4,3,2,1,0:T(8,128)(2,1)S(1)} %join.1.kv, ...), custom_call_target="tpu_custom_call" | custom-call | flops 1 | bytes 1 | tf_op jit(solution)/shard_map/attend/pallas_call | solution.py:421
  86.2 3.4 %collective-permute-start.12 = (bf16[4,128,128]{2,1,0:T(8,128)(2,1)S(1)}, bf16[4,128,128]{2,1,0:T(8,128)(2,1)S(1)}, u32[]{:S(2)}, u32[]{:S(2)}) collective-permute-start(bf16[4,128,128]{2,1,0:T(8,128)(2,1)S(1)} %get-tuple-element.50), channel_id=1, source_target_pairs={{0,8},{2,10},{4,12},{6,14},{8,0},{10,2},{12,4},{14,6},{1,9},{3,11}... | collective-permute-start | bytes 393224 | tf_op jit(solution)/shard_map/ppermute | solution.py:190
  89.6 1.0 collective-permute-start.13
  91.3 2.7 %collective-permute-start.14 = (bf16[4,128,128]{2,1,0:T(8,128)(2,1)S(1)}, bf16[4,128,128]{2,1,0:T(8,128)(2,1)S(1)}, u32[]{:S(2)}, u32[]{:S(2)}) collective-permute-start(bf16[4,128,128]{2,1,0:T(8,128)(2,1)S(1)} %get-tuple-element.52), channel_id=1, source_target_pairs={{0,12},{2,14},{4,8},{6,10},{8,4},{10,6},{12,0},{14,2},{1,13},{3,15... | collective-permute-start | bytes 393224 | tf_op jit(solution)/shard_map/ppermute | solution.py:190
  94.0 1.0 collective-permute-start.15
  95.0 4.5 %collective-permute-done.18.refs_3_ = bf16[4,128,128]{2,1,0:T(8,128)(2,1)S(1)} collective-permute-done((bf16[4,128,128]{2,1,0:T(8,128)(2,1)S(1)}, bf16[4,128,128]{2,1,0:T(8,128)(2,1)S(1)}, u32[]{:S(2)}, u32[]{:S(2)}) %collective-permute-start.18) | collective-permute-done | bytes 131104 | tf_op jit(solution)/shard_map/ppermute | solution.py:190
  99.5 2.2 %ungroup.2.refs_4_ = bf16[128,32,128]{2,1,0:T(8,128)(2,1)} custom-call(s32[2]{0:T(128)S(1)} %copy-done.2, bf16[4,128,128]{2,1,0:T(8,128)(2,1)S(1)} %get-tuple-element.42.refs_0_, bf16[4,128,128]{2,1,0:T(8,128)(2,1)S(1)} %collective-permute-done.16.refs_1_, bf16[4,128,128]{2,1,0:T(8,128)(2,1)S(1)} %collective-permute-done.17.refs_2_, ...), custom_call_target="tpu_custom_call" | custom-call | flops 1 | bytes 1 | tf_op jit(solution)/shard_map/ungroup/pallas_call | solution.py:277
  101.7 2.7 %collective-permute-done.13.refs_1_ = bf16[4,128,128]{2,1,0:T(8,128)(2,1)S(1)} collective-permute-done((bf16[4,128,128]{2,1,0:T(8,128)(2,1)S(1)}, bf16[4,128,128]{2,1,0:T(8,128)(2,1)S(1)}, u32[]{:S(2)}, u32[]{:S(2)}) %collective-permute-start.13) | collective-permute-done | bytes 131104 | tf_op jit(solution)/shard_map/ppermute | solution.py:190
  104.5 5.7 %collective-permute-done.14.refs_2_ = bf16[4,128,128]{2,1,0:T(8,128)(2,1)S(1)} collective-permute-done((bf16[4,128,128]{2,1,0:T(8,128)(2,1)S(1)}, bf16[4,128,128]{2,1,0:T(8,128)(2,1)S(1)}, u32[]{:S(2)}, u32[]{:S(2)}) %collective-permute-start.14) | collective-permute-done | bytes 131104 | tf_op jit(solution)/shard_map/ppermute | solution.py:190
  110.2 2.5 %collective-permute-done.15.refs_3_ = bf16[4,128,128]{2,1,0:T(8,128)(2,1)S(1)} collective-permute-done((bf16[4,128,128]{2,1,0:T(8,128)(2,1)S(1)}, bf16[4,128,128]{2,1,0:T(8,128)(2,1)S(1)}, u32[]{:S(2)}, u32[]{:S(2)}) %collective-permute-start.15) | collective-permute-done | bytes 131104 | tf_op jit(solution)/shard_map/ppermute | solution.py:190
  112.7 2.2 %ungroup.3 = bf16[128,32,128]{2,1,0:T(8,128)(2,1)} custom-call(s32[2]{0:T(128)S(1)} %copy-done.2, bf16[4,128,128]{2,1,0:T(8,128)(2,1)S(1)} %collective-permute-done.12.refs_0_, bf16[4,128,128]{2,1,0:T(8,128)(2,1)S(1)} %collective-permute-done.13.refs_1_, bf16[4,128,128]{2,1,0:T(8,128)(2,1)S(1)} %collective-permute-done.14.refs_2_, ...), custom_call_target="tpu_custom_call", output_to_operand_aliasing={{}: (5, {})} | custom-call | flops 1 | bytes 1 | tf_op jit(solution)/shard_map/ungroup/pallas_call | solution.py:277
  (44 shorter events, 4.7 us)
Async XLA Ops:
  0.0 7.7 %copy-start.11 = (s32[32,2]{0,1:T(2,128)S(1)}, s32[32,2]{0,1:T(2,128)}, u32[]{:S(2)}) copy-start(s32[32,2]{0,1:T(2,128)} %param.10) | copy-start | bytes 772
  0.0 7.8 %copy-start.12 = (s32[32,2]{0,1:T(2,128)S(1)}, s32[32,2]{0,1:T(2,128)}, u32[]{:S(2)}) copy-start(s32[32,2]{0,1:T(2,128)} %param.12) | copy-start | bytes 772
  0.0 7.9 %copy-start.3 = (s32[32]{0:T(128)S(1)}, s32[32]{0:T(128)}, u32[]{:S(2)}) copy-start(s32[32]{0:T(128)} %param.13) | copy-start | bytes 388
  0.0 7.9 %copy-start.4 = (s32[32]{0:T(128)S(1)}, s32[32]{0:T(128)}, u32[]{:S(2)}) copy-start(s32[32]{0:T(128)} %param.11) | copy-start | bytes 388
  3.8 19.8 %copy-start.6 = (bf16[2,4,128,128]{3,2,1,0:T(8,128)(2,1)S(1)}, bf16[2,4,128,128]{3,2,1,0:T(8,128)(2,1)}, u32[]{:S(2)}) copy-start(bf16[2,4,128,128]{3,2,1,0:T(8,128)(2,1)} %get-tuple-element.38) | copy-start | bytes 786436
  3.8 25.4 %copy-start.5 = (bf16[2,4,128,128]{3,2,1,0:T(8,128)(2,1)S(1)}, bf16[2,4,128,128]{3,2,1,0:T(8,128)(2,1)}, u32[]{:S(2)}) copy-start(bf16[2,4,128,128]{3,2,1,0:T(8,128)(2,1)} %get-tuple-element.39) | copy-start | bytes 786436
  3.8 48.5 %copy-start.2 = (s32[2]{0:T(128)S(1)}, s32[2]{0:T(128)}, u32[]{:S(2)}) copy-start(s32[2]{0:T(128)} %pad_add_fusion.1.place) | copy-start | bytes 28
  3.8 19.8 %collective-permute-start.3 = (bf16[2,4,128,128]{3,2,1,0:T(8,128)(2,1)}, bf16[2,4,128,128]{3,2,1,0:T(8,128)(2,1)S(1)}, u32[]{:S(2)}, u32[]{:S(2)}) collective-permute-start(bf16[2,4,128,128]{3,2,1,0:T(8,128)(2,1)} %get-tuple-element.36), channel_id=1, source_target_pairs={{0,8},{2,10},{4,12},{6,14},{8,0},{10,2},{12,4},{14,6},{1,9},{3,11}... | collective-permute-start | bytes 786440 | tf_op jit(solution)/shard_map/ppermute | solution.py:190
  6.4 22.8 %collective-permute-start.4 = (bf16[2,4,128,128]{3,2,1,0:T(8,128)(2,1)}, bf16[2,4,128,128]{3,2,1,0:T(8,128)(2,1)S(1)}, u32[]{:S(2)}, u32[]{:S(2)}) collective-permute-start(bf16[2,4,128,128]{3,2,1,0:T(8,128)(2,1)} %get-tuple-element.37), channel_id=1, source_target_pairs={{0,10},{2,8},{4,14},{6,12},{8,2},{10,0},{12,6},{14,4},{1,11},{3,9}... | collective-permute-start | bytes 786440 | tf_op jit(solution)/shard_map/ppermute | solution.py:190
  11.6 40.7 %collective-permute-start = (bf16[3,4,128,128]{3,2,1,0:T(8,128)(2,1)}, bf16[3,4,128,128]{3,2,1,0:T(8,128)(2,1)S(1)}, u32[]{:S(2)}, u32[]{:S(2)}) collective-permute-start(bf16[3,4,128,128]{3,2,1,0:T(8,128)(2,1)} %get-tuple-element.33), channel_id=1, source_target_pairs={{0,2},{2,0},{4,6},{6,4},{8,10},{10,8},{12,14},{14,12},{1,3},{3,1},... | collective-permute-start | bytes 1179656 | tf_op jit(solution)/shard_map/ppermute | solution.py:190
  12.2 40.1 %collective-permute-start.1 = (bf16[3,4,128,128]{3,2,1,0:T(8,128)(2,1)}, bf16[3,4,128,128]{3,2,1,0:T(8,128)(2,1)S(1)}, u32[]{:S(2)}, u32[]{:S(2)}) collective-permute-start(bf16[3,4,128,128]{3,2,1,0:T(8,128)(2,1)} %get-tuple-element.34), channel_id=1, source_target_pairs={{0,4},{2,6},{4,0},{6,2},{8,12},{10,14},{12,8},{14,10},{1,5},{3,7},... | collective-permute-start | bytes 1179656 | tf_op jit(solution)/shard_map/ppermute | solution.py:190
  12.6 39.7 %collective-permute-start.2 = (bf16[3,4,128,128]{3,2,1,0:T(8,128)(2,1)}, bf16[3,4,128,128]{3,2,1,0:T(8,128)(2,1)S(1)}, u32[]{:S(2)}, u32[]{:S(2)}) collective-permute-start(bf16[3,4,128,128]{3,2,1,0:T(8,128)(2,1)} %get-tuple-element.35), channel_id=1, source_target_pairs={{0,6},{2,4},{4,2},{6,0},{8,14},{10,12},{12,10},{14,8},{1,7},{3,5},... | collective-permute-start | bytes 1179656 | tf_op jit(solution)/shard_map/ppermute | solution.py:190
  23.6 13.2 %collective-permute-start.5 = (bf16[2,4,128,128]{3,2,1,0:T(8,128)(2,1)S(1)}, bf16[2,4,128,128]{3,2,1,0:T(8,128)(2,1)S(1)}, u32[]{:S(2)}, u32[]{:S(2)}) collective-permute-start(bf16[2,4,128,128]{3,2,1,0:T(8,128)(2,1)S(1)} %copy-done.6), channel_id=1, source_target_pairs={{0,12},{2,14},{4,8},{6,10},{8,4},{10,6},{12,0},{14,2},{1,13},{3,15... | collective-permute-start | bytes 786440 | tf_op jit(solution)/shard_map/ppermute | solution.py:190
  29.2 23.1 %collective-permute-start.6 = (bf16[2,4,128,128]{3,2,1,0:T(8,128)(2,1)S(1)}, bf16[2,4,128,128]{3,2,1,0:T(8,128)(2,1)S(1)}, u32[]{:S(2)}, u32[]{:S(2)}) collective-permute-start(bf16[2,4,128,128]{3,2,1,0:T(8,128)(2,1)S(1)} %copy-done.5), channel_id=1, source_target_pairs={{0,14},{2,12},{4,10},{6,8},{8,6},{10,4},{12,2},{14,0},{1,15},{3,13... | collective-permute-start | bytes 786440 | tf_op jit(solution)/shard_map/ppermute | solution.py:190
  52.3 1.0 copy-start
  53.3 0.9 copy-start.10
  53.3 5.4 %copy-start.9 = (bf16[1,4,128,128]{3,2,1,0:T(8,128)(2,1)S(1)}, bf16[1,4,128,128]{3,2,1,0:T(8,128)(2,1)}, u32[]{:S(2)}) copy-start(bf16[1,4,128,128]{3,2,1,0:T(8,128)(2,1)} %get-tuple-element.49) | copy-start | bytes 393220
  53.3 5.4 %copy-start.8 = (bf16[1,4,128,128]{3,2,1,0:T(8,128)(2,1)S(1)}, bf16[1,4,128,128]{3,2,1,0:T(8,128)(2,1)}, u32[]{:S(2)}) copy-start(bf16[1,4,128,128]{3,2,1,0:T(8,128)(2,1)} %get-tuple-element.47) | copy-start | bytes 393220
  53.3 7.4 %copy-start.7 = (bf16[1,4,128,128]{3,2,1,0:T(8,128)(2,1)S(1)}, bf16[1,4,128,128]{3,2,1,0:T(8,128)(2,1)}, u32[]{:S(2)}) copy-start(bf16[1,4,128,128]{3,2,1,0:T(8,128)(2,1)} %get-tuple-element.45) | copy-start | bytes 393220
  54.2 9.4 %collective-permute-start.7 = (bf16[8,2,4,128,128]{4,3,2,1,0:T(8,128)(2,1)S(1)}, bf16[8,2,4,128,128]{4,3,2,1,0:T(8,128)(2,1)S(1)}, u32[]{:S(2)}, u32[]{:S(2)}) collective-permute-start(bf16[8,2,4,128,128]{4,3,2,1,0:T(8,128)(2,1)S(1)} %gather.1.own), channel_id=1, source_target_pairs={{0,1},{1,0},{2,3},{3,2},{4,5},{5,4},{6,7},{7,6},{8,9},{9,8},{10,11... | collective-permute-start | bytes 6291464 | tf_op jit(solution)/shard_map/ppermute | solution.py:190
  54.2 18.2 %collective-permute-start.8 = (bf16[1,4,128,128]{3,2,1,0:T(8,128)(2,1)S(1)}, bf16[1,4,128,128]{3,2,1,0:T(8,128)(2,1)S(1)}, u32[]{:S(2)}, u32[]{:S(2)}) collective-permute-start(bf16[1,4,128,128]{3,2,1,0:T(8,128)(2,1)S(1)} %copy-done.10), channel_id=1, source_target_pairs={{0,8},{2,10},{4,12},{6,14},{8,0},{10,2},{12,4},{14,6},{1,9},{3,11}... | collective-permute-start | bytes 393224 | tf_op jit(solution)/shard_map/ppermute | solution.py:190
  58.7 5.7 %copy-start.1 = (bf16[3,4,128,128]{3,2,1,0:T(8,128)(2,1)S(1)}, bf16[3,4,128,128]{3,2,1,0:T(8,128)(2,1)}, u32[]{:S(2)}) copy-start(bf16[3,4,128,128]{3,2,1,0:T(8,128)(2,1)} %get-tuple-element.32.refs_0_) | copy-start | bytes 1179652
  58.7 16.6 %collective-permute-start.11 = (bf16[1,4,128,128]{3,2,1,0:T(8,128)(2,1)S(1)}, bf16[1,4,128,128]{3,2,1,0:T(8,128)(2,1)S(1)}, u32[]{:S(2)}, u32[]{:S(2)}) collective-permute-start(bf16[1,4,128,128]{3,2,1,0:T(8,128)(2,1)S(1)} %copy-done.9), channel_id=1, source_target_pairs={{0,14},{2,12},{4,10},{6,8},{8,6},{10,4},{12,2},{14,0},{1,15},{3,13... | collective-permute-start | bytes 393224 | tf_op jit(solution)/shard_map/ppermute | solution.py:190
  58.7 19.5 %collective-permute-start.10 = (bf16[1,4,128,128]{3,2,1,0:T(8,128)(2,1)S(1)}, bf16[1,4,128,128]{3,2,1,0:T(8,128)(2,1)S(1)}, u32[]{:S(2)}, u32[]{:S(2)}) collective-permute-start(bf16[1,4,128,128]{3,2,1,0:T(8,128)(2,1)S(1)} %copy-done.8), channel_id=1, source_target_pairs={{0,12},{2,14},{4,8},{6,10},{8,4},{10,6},{12,0},{14,2},{1,13},{3,15... | collective-permute-start | bytes 393224 | tf_op jit(solution)/shard_map/ppermute | solution.py:190
  60.7 20.2 %collective-permute-start.9 = (bf16[1,4,128,128]{3,2,1,0:T(8,128)(2,1)S(1)}, bf16[1,4,128,128]{3,2,1,0:T(8,128)(2,1)S(1)}, u32[]{:S(2)}, u32[]{:S(2)}) collective-permute-start(bf16[1,4,128,128]{3,2,1,0:T(8,128)(2,1)S(1)} %copy-done.7), channel_id=1, source_target_pairs={{0,10},{2,8},{4,14},{6,12},{8,2},{10,0},{12,6},{14,4},{1,11},{3,9}... | collective-permute-start | bytes 393224 | tf_op jit(solution)/shard_map/ppermute | solution.py:190
  69.5 21.9 %collective-permute-start.16 = (bf16[4,128,128]{2,1,0:T(8,128)(2,1)S(1)}, bf16[4,128,128]{2,1,0:T(8,128)(2,1)S(1)}, u32[]{:S(2)}, u32[]{:S(2)}) collective-permute-start(bf16[4,128,128]{2,1,0:T(8,128)(2,1)S(1)} %get-tuple-element.54), channel_id=1, source_target_pairs={{0,2},{2,0},{4,6},{6,4},{8,10},{10,8},{12,14},{14,12},{1,3},{3,1},... | collective-permute-start | bytes 393224 | tf_op jit(solution)/shard_map/ppermute | solution.py:190
  72.4 21.6 %collective-permute-start.17 = (bf16[4,128,128]{2,1,0:T(8,128)(2,1)S(1)}, bf16[4,128,128]{2,1,0:T(8,128)(2,1)S(1)}, u32[]{:S(2)}, u32[]{:S(2)}) collective-permute-start(bf16[4,128,128]{2,1,0:T(8,128)(2,1)S(1)} %get-tuple-element.55), channel_id=1, source_target_pairs={{0,4},{2,6},{4,0},{6,2},{8,12},{10,14},{12,8},{14,10},{1,5},{3,7},... | collective-permute-start | bytes 393224 | tf_op jit(solution)/shard_map/ppermute | solution.py:190
  86.2 15.5 %collective-permute-start.12 = (bf16[4,128,128]{2,1,0:T(8,128)(2,1)S(1)}, bf16[4,128,128]{2,1,0:T(8,128)(2,1)S(1)}, u32[]{:S(2)}, u32[]{:S(2)}) collective-permute-start(bf16[4,128,128]{2,1,0:T(8,128)(2,1)S(1)} %get-tuple-element.50), channel_id=1, source_target_pairs={{0,8},{2,10},{4,12},{6,14},{8,0},{10,2},{12,4},{14,6},{1,9},{3,11}... | collective-permute-start | bytes 393224 | tf_op jit(solution)/shard_map/ppermute | solution.py:190
  89.6 14.9 %collective-permute-start.13 = (bf16[4,128,128]{2,1,0:T(8,128)(2,1)S(1)}, bf16[4,128,128]{2,1,0:T(8,128)(2,1)S(1)}, u32[]{:S(2)}, u32[]{:S(2)}) collective-permute-start(bf16[4,128,128]{2,1,0:T(8,128)(2,1)S(1)} %get-tuple-element.51), channel_id=1, source_target_pairs={{0,10},{2,8},{4,14},{6,12},{8,2},{10,0},{12,6},{14,4},{1,11},{3,9}... | collective-permute-start | bytes 393224 | tf_op jit(solution)/shard_map/ppermute | solution.py:190
  90.6 8.9 %collective-permute-start.18 = (bf16[4,128,128]{2,1,0:T(8,128)(2,1)S(1)}, bf16[4,128,128]{2,1,0:T(8,128)(2,1)S(1)}, u32[]{:S(2)}, u32[]{:S(2)}) collective-permute-start(bf16[4,128,128]{2,1,0:T(8,128)(2,1)S(1)} %get-tuple-element.56), channel_id=1, source_target_pairs={{0,6},{2,4},{4,2},{6,0},{8,14},{10,12},{12,10},{14,8},{1,7},{3,5},... | collective-permute-start | bytes 393224 | tf_op jit(solution)/shard_map/ppermute | solution.py:190
  91.3 18.8 %collective-permute-start.14 = (bf16[4,128,128]{2,1,0:T(8,128)(2,1)S(1)}, bf16[4,128,128]{2,1,0:T(8,128)(2,1)S(1)}, u32[]{:S(2)}, u32[]{:S(2)}) collective-permute-start(bf16[4,128,128]{2,1,0:T(8,128)(2,1)S(1)} %get-tuple-element.52), channel_id=1, source_target_pairs={{0,12},{2,14},{4,8},{6,10},{8,4},{10,6},{12,0},{14,2},{1,13},{3,15... | collective-permute-start | bytes 393224 | tf_op jit(solution)/shard_map/ppermute | solution.py:190
  94.0 18.7 %collective-permute-start.15 = (bf16[4,128,128]{2,1,0:T(8,128)(2,1)S(1)}, bf16[4,128,128]{2,1,0:T(8,128)(2,1)S(1)}, u32[]{:S(2)}, u32[]{:S(2)}) collective-permute-start(bf16[4,128,128]{2,1,0:T(8,128)(2,1)S(1)} %get-tuple-element.53), channel_id=1, source_target_pairs={{0,14},{2,12},{4,10},{6,8},{8,6},{10,4},{12,2},{14,0},{1,15},{3,13... | collective-permute-start | bytes 393224 | tf_op jit(solution)/shard_map/ppermute | solution.py:190

commit v3 on v2

--- a/solution.py
+++ b/solution.py
@@ -179,6 +179,9 @@
 GROUP = ("seq", "qblk")
 MIB = 2**20
 REGROUP_VMEM = 60 * MIB
+RUNS = 2
+CHUNKS = 4
+LOG2_E = 1.4426950408889634
 ANY = pl.BlockSpec(memory_space=pl.ANY)
 HBM = pl.BlockSpec(memory_space=pltpu.HBM)
 SMEM = pl.BlockSpec(memory_space=pltpu.SMEM)
@@ -199,27 +202,28 @@
     sources, parts = refs[:tensors], refs[tensors : tensors + len(pieces)]
     staged, turned, load_sem, store_sem = refs[tensors + len(pieces) :]
     count, per_group = turned.shape[0], turned.shape[2]
-    heads = sources[0].shape[1]
-    loads = [
-        pltpu.make_async_copy(
-            sources[tensor].at[:, pl.ds(first_head(place, masks, heads, groups), heads // 2)],
-            staged.at[at],
-            load_sem.at[at],
-        )
-        for at, (masks, tensor) in enumerate(takes)
-    ]
-    for load in loads:
-        load.start()
+    tokens, heads = sources[0].shape[:2]
+    runs = [pl.ds(run * tokens // RUNS, tokens // RUNS) for run in range(RUNS)]
+    loads = []
+    for at, (masks, tensor) in enumerate(takes):
+        first = first_head(place, masks, heads, groups)
+        for into, run in enumerate(runs):
+            source = sources[tensor].at[run, pl.ds(first, heads // 2)]
+            loads.append(pltpu.make_async_copy(source, staged.at[at, run], load_sem.at[at, into]))
+            loads[-1].start()
     stores = []
-    for at, load in enumerate(loads):
-        load.wait()
-        heads_first = jnp.swapaxes(staged[at], 0, 1)
-        for group in range(count):
-            turned[group, at] = heads_first[group * per_group : (group + 1) * per_group]
+    for at in range(len(takes)):
+        for into, run in enumerate(runs):
+            loads[at * RUNS + into].wait()
+            heads_first = jnp.swapaxes(staged[at, run], 0, 1)
+            for group in range(count):
+                turned[group, at, :, run] = heads_first[group * per_group : (group + 1) * per_group]
         for into, ((mask, begin, length), part) in enumerate(zip(pieces, parts)):
-            if begin + length == at + 1:
-                part_at = turned.at[(place[0] ^ mask) % count, pl.ds(begin, length)]
-                stores.append(pltpu.make_async_copy(part_at, part, store_sem.at[into]))
+            if begin <= at < begin + length:
+                source = turned.at[(place[0] ^ mask) % count, at]
+                stores.append(
+                    pltpu.make_async_copy(source, part.at[at - begin], store_sem.at[into, at - begin])
+                )
                 stores[-1].start()
     for store in stores:
         store.wait()
@@ -240,8 +244,8 @@
         scratch_shapes=[
             pltpu.VMEM((len(takes), tokens, heads // 2, width), jnp.bfloat16),
             pltpu.VMEM((groups // 2, len(takes)) + part, jnp.bfloat16),
-            pltpu.SemaphoreType.DMA((len(takes),)),
-            pltpu.SemaphoreType.DMA((len(pieces),)),
+            pltpu.SemaphoreType.DMA((len(takes), RUNS)),
+            pltpu.SemaphoreType.DMA((len(pieces), len(takes))),
         ],
         compiler_params=pltpu.CompilerParams(vmem_limit_bytes=REGROUP_VMEM),
         cost_estimate=pl.CostEstimate(flops=1, bytes_accessed=1, transcendentals=0),
@@ -250,40 +254,38 @@
     return dict(zip(pieces, parts))
 
 
-def ungroup_half(place, *refs, masks, groups):
+def ungroup_kernel(place, *refs, masks, groups):
     parts = refs[: len(masks)]
-    out, staged, turned, load_sem, store_sem = refs[-5:]
-    count, per_group, tokens, width = staged.shape
-    heads = out.shape[1]
-    loads = [
-        pltpu.make_async_copy(part, staged.at[(place[0] ^ mask) % count], load_sem.at[at])
-        for at, (mask, part) in enumerate(zip(masks, parts))
-    ]
-    for load in loads:
-        load.start()
-    for load in loads:
-        load.wait()
-    heads_first = staged[...].reshape(count * per_group, tokens, width)
-    turned[...] = jnp.swapaxes(heads_first, 0, 1)
+    out, staged, turned, store_sem = refs[-4:]
+    count, per_group, _, width = staged.shape
+    tokens, heads = out.shape[:2]
     first = first_head(place, masks, heads, groups)
-    store = pltpu.make_async_copy(turned, out.at[:, pl.ds(first, heads // 2)], store_sem)
-    store.start()
-    store.wait()
+    for part, mask in zip(parts, masks):
+        staged[(place[0] ^ mask) % count] = part[...]
+    stores = []
+    for chunk in range(CHUNKS):
+        run = pl.ds(chunk * tokens // CHUNKS, tokens // CHUNKS)
+        heads_first = staged[:, :, run].reshape(count * per_group, tokens // CHUNKS, width)
+        turned[run] = jnp.swapaxes(heads_first, 0, 1)
+        target = out.at[run, pl.ds(first, heads // 2)]
+        stores.append(pltpu.make_async_copy(turned.at[run], target, store_sem.at[chunk]))
+        stores[-1].start()
+    for store in stores:
+        store.wait()
 
 
 def ungroup(place, parts, masks, groups, begun=None):
     per_group, tokens, width = parts[masks[0]].shape
     shape = (tokens, groups * per_group, width)
     return pl.pallas_call(
-        functools.partial(ungroup_half, masks=masks, groups=groups),
+        functools.partial(ungroup_kernel, masks=masks, groups=groups),
         out_shape=jax.ShapeDtypeStruct(shape, jnp.bfloat16),
-        in_specs=[SMEM] + [ANY] * len(masks) + ([] if begun is None else [HBM]),
+        in_specs=[SMEM] + [VMEM] * len(masks) + ([] if begun is None else [HBM]),
         out_specs=HBM,
         scratch_shapes=[
             pltpu.VMEM((len(masks), per_group, tokens, width), jnp.bfloat16),
             pltpu.VMEM((tokens, len(masks) * per_group, width), jnp.bfloat16),
-            pltpu.SemaphoreType.DMA((len(masks),)),
-            pltpu.SemaphoreType.DMA,
+            pltpu.SemaphoreType.DMA((CHUNKS,)),
         ],
         input_output_aliases={} if begun is None else {1 + len(masks): 0},
         compiler_params=pltpu.CompilerParams(vmem_limit_bytes=6 * MIB),
@@ -333,34 +335,21 @@
     )(place, *parts)
 
 
-def join_kernel(place, own, other, out, sem):
-    copies = [
-        pltpu.make_async_copy(own, out.at[place[1]], sem.at[0]),
-        pltpu.make_async_copy(other, out.at[1 - place[1]], sem.at[1]),
-    ]
-    for copy in copies:
-        copy.start()
-    for copy in copies:
-        copy.wait()
-
-
-def join(place, own, other):
-    return pl.pallas_call(
-        join_kernel,
-        out_shape=jax.ShapeDtypeStruct((2,) + own.shape, jnp.bfloat16),
-        in_specs=[SMEM, ANY, ANY],
-        out_specs=ANY,
-        scratch_shapes=[pltpu.SemaphoreType.DMA((2,))],
-        compiler_params=pltpu.CompilerParams(vmem_limit_bytes=2 * MIB),
-        cost_estimate=pl.CostEstimate(flops=1, bytes_accessed=1, transcendentals=0),
-        name="join",
-    )(place, own, other)
-
-
-def attend_kernel(place, tables, kv, *refs, masks, sizes, n_seq, n_qblk):
-    queries, outs = refs[: len(masks)], refs[len(masks) :]
-    heads, width = kv.shape[3], kv.shape[-1]
-    scaling = width ** (-0.5)
+def attend_kernel(place, tables, *refs, masks, sizes, n_seq, n_qblk, sides):
+    count = len(masks)
+    loads = []
+    if sides:
+        sides, queries, outs = refs[:2], refs[2 : 2 + count], refs[2 + count : 2 + 2 * count]
+        kv, sem = refs[-2:]
+        for slot in range(kv.shape[0]):
+            for at, side in enumerate(sides):
+                target = kv.at[slot, place[1] ^ at]
+                loads.append(pltpu.make_async_copy(side.at[:, :, slot], target, sem.at[slot, at]))
+                loads[-1].start()
+    else:
+        kv, queries, outs = refs[0], refs[1 : 1 + count], refs[1 + count :]
+    heads, width = kv.shape[0], kv.shape[-1]
+    scaling = width ** (-0.5) * LOG2_E
     all_heads, n_vert, n_slash = sizes
     vert_cnt = all_heads * n_vert
     slash_off = vert_cnt + all_heads
@@ -369,9 +358,9 @@
     query_col = lax.broadcasted_iota(jnp.int32, (BLK, BLK), 1)
     causal = key_row <= query_col
 
-    def place_of(block):
+    def tile(block, tensor, slot):
         span = block // n_seq
-        return span % 2, (span // 2) * n_seq + block % n_seq
+        return kv[slot, span % 2, (span // 2) * n_seq + block % n_seq, tensor]
 
     def unit(query, out, slot, block):
         head = place[0] * heads + slot
@@ -389,9 +378,8 @@
                 ok = ok & jnp.logical_not((other < slash_live) & (offset == distance))
             live.append(ok)
             cols.append(column)
-        spots = [place_of(column) for column in cols]
-        keys = jnp.concatenate([kv[side, at, 0, slot] for side, at in spots], axis=0)
-        vals = jnp.concatenate([kv[side, at, 1, slot] for side, at in spots], axis=0)
+        keys = jnp.concatenate([tile(column, 0, slot) for column in cols], axis=0)
+        vals = jnp.concatenate([tile(column, 1, slot) for column in cols], axis=0)
         scores = lax.dot_general(
             keys, query[query.shape[0] - 1, slot], (((1,), (1,)), ((), ())), preferred_element_type=jnp.float32
         )
@@ -401,23 +389,28 @@
             parts.append(scores[(at + 1) * BLK : (at + 2) * BLK] + bias)
         top = functools.reduce(jnp.maximum, parts)
         top = jnp.max(top, axis=0, keepdims=True)
-        weights = [jnp.exp((part - top) * scaling) for part in parts]
+        weights = [jnp.exp2((part - top) * scaling) for part in parts]
         total = jnp.sum(functools.reduce(jnp.add, weights), axis=0, keepdims=True)
         rounded = jnp.concatenate([weight.astype(jnp.bfloat16) for weight in weights], axis=0)
         acc = lax.dot_general(
             vals, rounded, (((0,), (0,)), ((), ())), preferred_element_type=jnp.float32
         )
-        out[slot] = (acc / total).T.astype(jnp.bfloat16)
-
-    @pl.loop(0, heads)
-    def _(slot):
+        out[slot] = (acc * (1.0 / total)).T.astype(jnp.bfloat16)
+
+    for slot in range(heads):
+        for load in loads[2 * slot : 2 * slot + 2]:
+            load.wait()
         for mask, query, out in zip(masks, queries, outs):
             unit(query, out, slot, block_of(place, mask, n_seq, n_qblk))
 
 
 def attend(place, tables, sizes, kv, queries, masks):
-    count = len(masks)
-    _, _, _, heads, tokens, width = kv.shape
+    sides, count = isinstance(kv, (tuple, list)), len(masks)
+    if sides:
+        spots, _, heads, tokens, width = kv[0].shape
+        whole = jax.ShapeDtypeStruct((heads, 2, spots, 2, tokens, width), jnp.bfloat16)
+    else:
+        heads, _, _, _, tokens, width = kv.shape
     outs = pl.pallas_call(
         functools.partial(
             attend_kernel,
@@ -425,15 +418,18 @@
             sizes=sizes,
             n_seq=lax.axis_size("seq"),
             n_qblk=lax.axis_size("qblk"),
+            sides=sides,
         ),
-        out_shape=[jax.ShapeDtypeStruct((heads, tokens, width), jnp.bfloat16)] * count,
-        in_specs=[SMEM] * 2 + [VMEM] * (1 + count),
-        out_specs=[VMEM] * count,
+        out_shape=[jax.ShapeDtypeStruct((heads, tokens, width), jnp.bfloat16)] * count
+        + ([whole] if sides else []),
+        in_specs=[SMEM] * 2 + ([ANY] * 2 if sides else [VMEM]) + [VMEM] * count,
+        out_specs=[VMEM] * (count + sides),
+        scratch_shapes=[pltpu.SemaphoreType.DMA((heads, 2))] if sides else [],
         compiler_params=pltpu.CompilerParams(vmem_limit_bytes=12 * MIB),
         cost_estimate=pl.CostEstimate(flops=1, bytes_accessed=1, transcendentals=0),
         name="attend",
-    )(place, tables, kv, *[queries[mask] for mask in masks])
-    return dict(zip(masks, outs))
+    )(place, tables, *(kv if sides else [kv]), *[queries[mask] for mask in masks])
+    return dict(zip(masks, outs)), (outs[-1] if sides else kv)
 
 
 def after(value, *others):
@@ -459,14 +455,21 @@
     got = {mask: send(kv_far[mask, 0, 2], mask) for mask in far}
     for mask in near:
         got[mask] = send(rest[mask, 0, 3], mask) if mask else rest[mask, 0, 3]
-    own = gather(place, [got[mask] for mask in range(groups)])
-    whole = join(place, own, swap_with(own, "sub", 1))
+    def share(*parts):
+        own = gather(place, parts)
+        return own, swap_with(own, "sub", 1)
+
+    def share_again(*parts):
+        own = gather(place, parts)
+        return own, swap_with(after(own, place), "sub", 1)
+
+    some = tables[1][0] >= 1
+    sides = lax.cond(some, share, share_again, *[got[mask] for mask in range(groups)])
     arrived = {mask: got[mask] for mask in near}
     for mask in far:
-        arrived[mask] = send(rest[mask, 3, 1], mask, got[mask])
-    outs = attend(place, flat, sizes, whole, arrived, near)
-    arrived[far[0]] = after(arrived[far[0]], outs[near[0]])
-    outs.update(attend(place, flat, sizes, whole, arrived, far))
+        arrived[mask] = send(rest[mask, 3, 1], mask)
+    outs, kv = attend(place, flat, sizes, sides, arrived, near)
+    outs.update(attend(place, flat, sizes, kv, arrived, far)[0])
     back = {mask: send(outs[mask], mask) for mask in far}
     for mask in near:
         back[mask] = send(outs[mask], mask) if mask else outs[mask]

time: 115 us -> 106 us (0.922)
  waiting for transfers between devices: 60.1 us -> 52.3 us
  starting transfers between devices: 29.6 us -> 32.8 us
  Pallas kernels: 23.1 us -> 20.5 us
    ppermute x19, waiting for transfers between devices: 60.1 us -> 52.3 us  [swap_with(): lax.ppermute(value, axes, [(source, source ^ mask) for source in range(co...]
    ppermute x19, starting transfers between devices: 29.6 us -> 32.8 us  [swap_with(): lax.ppermute(value, axes, [(source, source ^ mask) for source in range(co...]
    pallas_call x3 -> x2, Pallas kernels: 5.26 us -> 2.9 us  [ungroup(): pl.pallas_call(functools.partial(ungroup_kernel, masks=masks, groups=grou...]
    pallas_call x2, Pallas kernels: 10.3 us -> 9.03 us  [attend(): pl.pallas_call(functools.partial(attend_kernel, masks=masks, sizes=sizes,...]
  transfers between devices with their start and end apart: 19 -> 19, of which waited for: 12 -> 9; matrix products, arithmetic and copies ran while one was open for 0% -> 0% of each run, Pallas kernels for 15% -> 15%
where the time goes in v3:
time: 106 us
  waiting for transfers between devices  52.3 us (49%)
  starting transfers between devices  32.8 us (31%)
  Pallas kernels  20.5 us (19%)
    ppermute x19, waiting for transfers between devices, swap_with(): lax.ppermute(value, axes, [(source, source ^ mask) for source in range(co...  52.3 us
    ppermute x19, starting transfers between devices, swap_with(): lax.ppermute(value, axes, [(source, source ^ mask) for source in range(co...  32.8 us
    pallas_call x2, Pallas kernels, attend(): pl.pallas_call(functools.partial(attend_kernel, masks=masks, sizes=sizes,...  9.03 us
    pallas_call x2, Pallas kernels, regroup(): pl.pallas_call(functools.partial(regroup_kernel, tensors=len(tensors), ta...  6.62 us
    pallas_call x2, Pallas kernels, ungroup(): pl.pallas_call(functools.partial(ungroup_kernel, masks=masks, groups=grou...  2.9 us
  transfers between devices with their start and end apart: 19, of which 9 were waited for; matrix products, arithmetic and copies ran while one was open for 0% of the time, Pallas kernels for 15%

profile of v3, /device:TPU:12, one launch (start us, length us, event | category | flops | bytes accessed | tf_op | source)
XLA Modules:
  0.0 106.1 jit_solution(13374756710641670937)
XLA Ops:
  0.1 2.8 %regroup.3 = (bf16[2,4,128,128]{3,2,1,0:T(8,128)(2,1)}, bf16[2,4,128,128]{3,2,1,0:T(8,128)(2,1)}, bf16[2,4,128,128]{3,2,1,0:T(8,128)(2,1)}, bf16[2,4,128,128]{3,2,1,0:T(8,128)(2,1)}) custom-call(s32[2]{0:T(128)S(1)} %pad_add_fusion.1.place, bf16[128,32,128]{2,1,0:T(8,128)(2,1)} %bitcast.10, bf16[128,32,128]{2,1,0:T(8,128)(2,1)} %bitcast.12), custom_call_target="tpu_custom_call" | custom-call | flops 1 | bytes 1 | tf_op jit(solution)/shard_map/regroup/pallas_call | solution.py:235
  2.9 2.7 %collective-permute-start.5 = (bf16[2,4,128,128]{3,2,1,0:T(8,128)(2,1)}, bf16[2,4,128,128]{3,2,1,0:T(8,128)(2,1)S(1)}, u32[]{:S(2)}, u32[]{:S(2)}) collective-permute-start(bf16[2,4,128,128]{3,2,1,0:T(8,128)(2,1)} %get-tuple-element.89), channel_id=1, source_target_pairs={{0,8},{2,10},{4,12},{6,14},{8,0},{10,2},{12,4},{14,6},{1,9},{3,11}... | collective-permute-start | bytes 786440 | tf_op jit(solution)/shard_map/ppermute | solution.py:193
  5.6 1.3 %collective-permute-start.6 = (bf16[2,4,128,128]{3,2,1,0:T(8,128)(2,1)}, bf16[2,4,128,128]{3,2,1,0:T(8,128)(2,1)S(1)}, u32[]{:S(2)}, u32[]{:S(2)}) collective-permute-start(bf16[2,4,128,128]{3,2,1,0:T(8,128)(2,1)} %get-tuple-element.90), channel_id=1, source_target_pairs={{0,10},{2,8},{4,14},{6,12},{8,2},{10,0},{12,6},{14,4},{1,11},{3,9}... | collective-permute-start | bytes 786440 | tf_op jit(solution)/shard_map/ppermute | solution.py:193
  7.1 3.8 %regroup.2 = (bf16[3,4,128,128]{3,2,1,0:T(8,128)(2,1)S(1)}, bf16[3,4,128,128]{3,2,1,0:T(8,128)(2,1)}, bf16[3,4,128,128]{3,2,1,0:T(8,128)(2,1)}, bf16[3,4,128,128...) custom-call(s32[2]{0:T(128)S(1)} %pad_add_fusion.1.place, ...), custom_call_target="tpu_custom_call" | custom-call | flops 1 | bytes 1 | tf_op jit(solution)/shard_map/regroup/pallas_call | solution.py:235
  10.9 0.6 collective-permute-start.2
  11.5 0.4 collective-permute-start.3
  12.0 2.5 %collective-permute-start.4 = (bf16[3,4,128,128]{3,2,1,0:T(8,128)(2,1)}, bf16[3,4,128,128]{3,2,1,0:T(8,128)(2,1)S(1)}, u32[]{:S(2)}, u32[]{:S(2)}) collective-permute-start(bf16[3,4,128,128]{3,2,1,0:T(8,128)(2,1)} %get-tuple-element.88), channel_id=1, source_target_pairs={{0,6},{2,4},{4,2},{6,0},{8,14},{10,12},{12,10},{14,8},{1,7},{3,5},... | collective-permute-start | bytes 1179656 | tf_op jit(solution)/shard_map/ppermute | solution.py:193
  14.5 8.2 %collective-permute-done.5 = bf16[2,4,128,128]{3,2,1,0:T(8,128)(2,1)S(1)} collective-permute-done((bf16[2,4,128,128]{3,2,1,0:T(8,128)(2,1)}, bf16[2,4,128,128]{3,2,1,0:T(8,128)(2,1)S(1)}, u32[]{:S(2)}, u32[]{:S(2)}) %collective-permute-start.5) | collective-permute-done | bytes 262176 | tf_op jit(solution)/shard_map/ppermute | solution.py:193
  22.7 0.5 collective-permute-start.7
  23.2 5.1 %collective-permute-done.6 = bf16[2,4,128,128]{3,2,1,0:T(8,128)(2,1)S(1)} collective-permute-done((bf16[2,4,128,128]{3,2,1,0:T(8,128)(2,1)}, bf16[2,4,128,128]{3,2,1,0:T(8,128)(2,1)S(1)}, u32[]{:S(2)}, u32[]{:S(2)}) %collective-permute-start.6) | collective-permute-done | bytes 262176 | tf_op jit(solution)/shard_map/ppermute | solution.py:193
  28.3 1.4 %collective-permute-start.8 = (bf16[2,4,128,128]{3,2,1,0:T(8,128)(2,1)S(1)}, bf16[2,4,128,128]{3,2,1,0:T(8,128)(2,1)S(1)}, u32[]{:S(2)}, u32[]{:S(2)}) collective-permute-start(bf16[2,4,128,128]{3,2,1,0:T(8,128)(2,1)S(1)} %copy-done.2), channel_id=1, source_target_pairs={{0,14},{2,12},{4,10},{6,8},{8,6},{10,4},{12,2},{14,0},{1,15},{3,13... | collective-permute-start | bytes 786440 | tf_op jit(solution)/shard_map/ppermute | solution.py:193
  29.7 6.1 %collective-permute-done.7 = bf16[2,4,128,128]{3,2,1,0:T(8,128)(2,1)S(1)} collective-permute-done((bf16[2,4,128,128]{3,2,1,0:T(8,128)(2,1)S(1)}, bf16[2,4,128,128]{3,2,1,0:T(8,128)(2,1)S(1)}, u32[]{:S(2)}, u32[]{:S(2)}) %collective-permute-start.7) | collective-permute-done | bytes 262176 | tf_op jit(solution)/shard_map/ppermute | solution.py:193
  35.9 8.2 %collective-permute-start.9 = (bf16[1,4,128,128]{3,2,1,0:T(8,128)(2,1)}, bf16[1,4,128,128]{3,2,1,0:T(8,128)(2,1)S(1)}, u32[]{:S(2)}, u32[]{:S(2)}) collective-permute-start(bf16[1,4,128,128]{3,2,1,0:T(8,128)(2,1)} %get-tuple-element.96), channel_id=1, source_target_pairs={{0,8},{2,10},{4,12},{6,14},{8,0},{10,2},{12,4},{14,6},{1,9},{3,11}... | collective-permute-start | bytes 393224 | tf_op jit(solution)/shard_map/ppermute | solution.py:193
  44.1 11.2 %collective-permute-done.8 = bf16[2,4,128,128]{3,2,1,0:T(8,128)(2,1)S(1)} collective-permute-done((bf16[2,4,128,128]{3,2,1,0:T(8,128)(2,1)S(1)}, bf16[2,4,128,128]{3,2,1,0:T(8,128)(2,1)S(1)}, u32[]{:S(2)}, u32[]{:S(2)}) %collective-permute-start.8) | collective-permute-done | bytes 262176 | tf_op jit(solution)/shard_map/ppermute | solution.py:193
  55.4 1.6 %collective-permute-start.11 = (bf16[1,4,128,128]{3,2,1,0:T(8,128)(2,1)}, bf16[1,4,128,128]{3,2,1,0:T(8,128)(2,1)S(1)}, u32[]{:S(2)}, u32[]{:S(2)}) collective-permute-start(bf16[1,4,128,128]{3,2,1,0:T(8,128)(2,1)} %get-tuple-element.98), channel_id=1, source_target_pairs={{0,12},{2,14},{4,8},{6,10},{8,4},{10,6},{12,0},{14,2},{1,13},{3,15... | collective-permute-start | bytes 393224 | tf_op jit(solution)/shard_map/ppermute | solution.py:193
  56.9 0.4 collective-permute-start.12
  57.4 6.5 %conditional.1 = (bf16[8,2,4,128,128]{4,3,2,1,0:T(8,128)(2,1)}, bf16[8,2,4,128,128]{4,3,2,1,0:T(8,128)(2,1)}) conditional(s32[]{:T(128)} %bitcast.4, (s32[2]{0:T(128)S(1)}, bf16[3,4,128,128]{3,2,1,0:T(8,128)(2,1)S(1)}, bf16[3,4,128,128]{3,2,1,0:T(8,128)(2,1)S(1)}, bf16[3,4,128,128]{3,2,1,0:T(8,128)(2,1)S(1)}, bf16[3,4,128,128]{3,2,1,0:T(8,128)(2,1)S(1)}, ...), branch_computations={%region_0.0_spmd, %region_1.0_spmd} | conditional | flops 1 | bytes 8388665 | solution.py:467
  57.4 1.9 %gather.3 = bf16[8,2,4,128,128]{4,3,2,1,0:T(8,128)(2,1)} custom-call(s32[2]{0:T(128)S(1)} %get-tuple-element.51.place, bf16[3,4,128,128]{3,2,1,0:T(8,128)(2,1)S(1)} %get-tuple-element.52.refs_0_, bf16[3,4,128,128]{3,2,1,0:T(8,128)(2,1)S(1)} %get-tuple-element.53.refs_1_, bf16[3,4,128,128]{3,2,1,0:T(8,128)(2,1)S(1)} %get-tuple-element.54.refs_2_, ...), custom_call_target="tpu_custom_call" | custom-call | flops 1 | bytes 1 | tf_op jit(solution)/shard_map/cond/branch_1_fun/gather/pallas_call | solution.py:321
  59.4 4.5 %collective-permute-done.1 = bf16[8,2,4,128,128]{4,3,2,1,0:T(8,128)(2,1)} collective-permute-done((bf16[8,2,4,128,128]{4,3,2,1,0:T(8,128)(2,1)}, bf16[8,2,4,128,128]{4,3,2,1,0:T(8,128)(2,1)}, u32[]{:S(2)}, u32[]{:S(2)}) %collective-permute-start.1) | collective-permute-done | bytes 2097184 | tf_op jit(solution)/shard_map/cond/branch_1_fun/ppermute | solution.py:193
  63.9 5.7 %attend.2 = (bf16[4,128,128]{2,1,0:T(8,128)(2,1)S(1)}, bf16[4,128,128]{2,1,0:T(8,128)(2,1)S(1)}, bf16[4,128,128]{2,1,0:T(8,128)(2,1)S(1)}, bf16[4,128,128]{2,1,0...) custom-call(s32[2]{0:T(128)S(1)} %pad_add_fusion.1.place, s32[192]{0:T(256)S(1)} %pad_add_fusion.tables, ...), custom_call_target="tpu_custom_call" | custom-call | flops 1 | bytes 1 | tf_op jit(solution)/shard_map/attend/pallas_call | solution.py:414
  69.5 1.6 %collective-permute-start.17 = (bf16[4,128,128]{2,1,0:T(8,128)(2,1)S(1)}, bf16[4,128,128]{2,1,0:T(8,128)(2,1)S(1)}, u32[]{:S(2)}, u32[]{:S(2)}) collective-permute-start(bf16[4,128,128]{2,1,0:T(8,128)(2,1)S(1)} %get-tuple-element.105), channel_id=1, source_target_pairs={{0,2},{2,0},{4,6},{6,4},{8,10},{10,8},{12,14},{14,12},{1,3},{3,1},... | collective-permute-start | bytes 393224 | tf_op jit(solution)/shard_map/ppermute | solution.py:193
  71.1 4.8 %collective-permute-start.18 = (bf16[4,128,128]{2,1,0:T(8,128)(2,1)S(1)}, bf16[4,128,128]{2,1,0:T(8,128)(2,1)S(1)}, u32[]{:S(2)}, u32[]{:S(2)}) collective-permute-start(bf16[4,128,128]{2,1,0:T(8,128)(2,1)S(1)} %get-tuple-element.106), channel_id=1, source_target_pairs={{0,4},{2,6},{4,0},{6,2},{8,12},{10,14},{12,8},{14,10},{1,5},{3,7},... | collective-permute-start | bytes 393224 | tf_op jit(solution)/shard_map/ppermute | solution.py:193
  75.9 3.4 %attend.3 = (bf16[4,128,128]{2,1,0:T(8,128)(2,1)S(1)}, bf16[4,128,128]{2,1,0:T(8,128)(2,1)S(1)}, bf16[4,128,128]{2,1,0:T(8,128)(2,1)S(1)}, bf16[4,128,128]{2,1,0:T(8,128)(2,1)S(1)}) custom-call(s32[2]{0:T(128)S(1)} %pad_add_fusion.1.place, s32[192]{0:T(256)S(1)} %pad_add_fusion.tables, bf16[4,2,8,2,128,128]{5,4,3,2,1,0:T(8,128)(2,1)S(1)} %get-tuple-element.95.refs_0_, ...), custom_call_target="tpu_custom_call" | custom-call | flops 1 | bytes 1 | tf_op jit(solution)/shard_map/attend/pallas_call | solution.py:414
  79.4 3.8 %collective-permute-start.14 = (bf16[4,128,128]{2,1,0:T(8,128)(2,1)S(1)}, bf16[4,128,128]{2,1,0:T(8,128)(2,1)S(1)}, u32[]{:S(2)}, u32[]{:S(2)}) collective-permute-start(bf16[4,128,128]{2,1,0:T(8,128)(2,1)S(1)} %get-tuple-element.101), channel_id=1, source_target_pairs={{0,10},{2,8},{4,14},{6,12},{8,2},{10,0},{12,6},{14,4},{1,11},{3,9}... | collective-permute-start | bytes 393224 | tf_op jit(solution)/shard_map/ppermute | solution.py:193
  83.2 0.6 collective-permute-start.15
  83.8 2.3 %collective-permute-start.16 = (bf16[4,128,128]{2,1,0:T(8,128)(2,1)S(1)}, bf16[4,128,128]{2,1,0:T(8,128)(2,1)S(1)}, u32[]{:S(2)}, u32[]{:S(2)}) collective-permute-start(bf16[4,128,128]{2,1,0:T(8,128)(2,1)S(1)} %get-tuple-element.103), channel_id=1, source_target_pairs={{0,14},{2,12},{4,10},{6,8},{8,6},{10,4},{12,2},{14,0},{1,15},{3,13... | collective-permute-start | bytes 393224 | tf_op jit(solution)/shard_map/ppermute | solution.py:193
  86.1 6.1 %collective-permute-done.19.refs_3_ = bf16[4,128,128]{2,1,0:T(8,128)(2,1)S(1)} collective-permute-done((bf16[4,128,128]{2,1,0:T(8,128)(2,1)S(1)}, bf16[4,128,128]{2,1,0:T(8,128)(2,1)S(1)}, u32[]{:S(2)}, u32[]{:S(2)}) %collective-permute-start.19) | collective-permute-done | bytes 131104 | tf_op jit(solution)/shard_map/ppermute | solution.py:193
  92.2 1.5 %ungroup.2.refs_4_ = bf16[128,32,128]{2,1,0:T(8,128)(2,1)} custom-call(s32[2]{0:T(128)S(1)} %pad_add_fusion.1.place, bf16[4,128,128]{2,1,0:T(8,128)(2,1)S(1)} %get-tuple-element.104.refs_0_, bf16[4,128,128]{2,1,0:T(8,128)(2,1)S(1)} %collective-permute-done.17.refs_1_, bf16[4,128,128]{2,1,0:T(8,128)(2,1)S(1)} %collective-permute-done.18.refs_2_, ...), custom_call_target="tpu_custom_call" | custom-call | flops 1 | bytes 1 | tf_op jit(solution)/shard_map/ungroup/pallas_call | solution.py:280
  93.7 3.5 %collective-permute-done.14.refs_1_ = bf16[4,128,128]{2,1,0:T(8,128)(2,1)S(1)} collective-permute-done((bf16[4,128,128]{2,1,0:T(8,128)(2,1)S(1)}, bf16[4,128,128]{2,1,0:T(8,128)(2,1)S(1)}, u32[]{:S(2)}, u32[]{:S(2)}) %collective-permute-start.14) | collective-permute-done | bytes 131104 | tf_op jit(solution)/shard_map/ppermute | solution.py:193
  97.2 4.9 %collective-permute-done.15.refs_2_ = bf16[4,128,128]{2,1,0:T(8,128)(2,1)S(1)} collective-permute-done((bf16[4,128,128]{2,1,0:T(8,128)(2,1)S(1)}, bf16[4,128,128]{2,1,0:T(8,128)(2,1)S(1)}, u32[]{:S(2)}, u32[]{:S(2)}) %collective-permute-start.15) | collective-permute-done | bytes 131104 | tf_op jit(solution)/shard_map/ppermute | solution.py:193
  102.0 2.6 %collective-permute-done.16.refs_3_ = bf16[4,128,128]{2,1,0:T(8,128)(2,1)S(1)} collective-permute-done((bf16[4,128,128]{2,1,0:T(8,128)(2,1)S(1)}, bf16[4,128,128]{2,1,0:T(8,128)(2,1)S(1)}, u32[]{:S(2)}, u32[]{:S(2)}) %collective-permute-start.16) | collective-permute-done | bytes 131104 | tf_op jit(solution)/shard_map/ppermute | solution.py:193
  104.7 1.4 %ungroup.3 = bf16[128,32,128]{2,1,0:T(8,128)(2,1)} custom-call(s32[2]{0:T(128)S(1)} %pad_add_fusion.1.place, bf16[4,128,128]{2,1,0:T(8,128)(2,1)S(1)} %collective-permute-done.13.refs_0_, bf16[4,128,128]{2,1,0:T(8,128)(2,1)S(1)} %collective-permute-done.14.refs_1_, ...), custom_call_target="tpu_custom_call", output_to_operand_aliasing={{}: (5, {})} | custom-call | flops 1 | bytes 1 | tf_op jit(solution)/shard_map/ungroup/pallas_call | solution.py:280
  (30 shorter events, 0.5 us)
Async XLA Ops:
  0.0 6.8 %copy-start.4 = (s32[32,2]{0,1:T(2,128)S(1)}, s32[32,2]{0,1:T(2,128)}, u32[]{:S(2)}) copy-start(s32[32,2]{0,1:T(2,128)} %param.12) | copy-start | bytes 772
  0.0 6.9 %copy-start.5 = (s32[32,2]{0,1:T(2,128)S(1)}, s32[32,2]{0,1:T(2,128)}, u32[]{:S(2)}) copy-start(s32[32,2]{0,1:T(2,128)} %param.14) | copy-start | bytes 772
  0.0 7.0 %copy-start.1 = (s32[32]{0:T(128)S(1)}, s32[32]{0:T(128)}, u32[]{:S(2)}) copy-start(s32[32]{0:T(128)} %param.13) | copy-start | bytes 388
  0.0 7.0 %copy-start = (s32[32]{0:T(128)S(1)}, s32[32]{0:T(128)}, u32[]{:S(2)}) copy-start(s32[32]{0:T(128)} %param.15) | copy-start | bytes 388
  2.9 19.8 %copy-start.3 = (bf16[2,4,128,128]{3,2,1,0:T(8,128)(2,1)S(1)}, bf16[2,4,128,128]{3,2,1,0:T(8,128)(2,1)}, u32[]{:S(2)}) copy-start(bf16[2,4,128,128]{3,2,1,0:T(8,128)(2,1)} %get-tuple-element.91) | copy-start | bytes 786436
  2.9 25.4 %copy-start.2 = (bf16[2,4,128,128]{3,2,1,0:T(8,128)(2,1)S(1)}, bf16[2,4,128,128]{3,2,1,0:T(8,128)(2,1)}, u32[]{:S(2)}) copy-start(bf16[2,4,128,128]{3,2,1,0:T(8,128)(2,1)} %get-tuple-element.92) | copy-start | bytes 786436
  2.9 19.8 %collective-permute-start.5 = (bf16[2,4,128,128]{3,2,1,0:T(8,128)(2,1)}, bf16[2,4,128,128]{3,2,1,0:T(8,128)(2,1)S(1)}, u32[]{:S(2)}, u32[]{:S(2)}) collective-permute-start(bf16[2,4,128,128]{3,2,1,0:T(8,128)(2,1)} %get-tuple-element.89), channel_id=1, source_target_pairs={{0,8},{2,10},{4,12},{6,14},{8,0},{10,2},{12,4},{14,6},{1,9},{3,11}... | collective-permute-start | bytes 786440 | tf_op jit(solution)/shard_map/ppermute | solution.py:193
  5.6 22.8 %collective-permute-start.6 = (bf16[2,4,128,128]{3,2,1,0:T(8,128)(2,1)}, bf16[2,4,128,128]{3,2,1,0:T(8,128)(2,1)S(1)}, u32[]{:S(2)}, u32[]{:S(2)}) collective-permute-start(bf16[2,4,128,128]{3,2,1,0:T(8,128)(2,1)} %get-tuple-element.90), channel_id=1, source_target_pairs={{0,10},{2,8},{4,14},{6,12},{8,2},{10,0},{12,6},{14,4},{1,11},{3,9}... | collective-permute-start | bytes 786440 | tf_op jit(solution)/shard_map/ppermute | solution.py:193
  10.9 44.4 %collective-permute-start.2 = (bf16[3,4,128,128]{3,2,1,0:T(8,128)(2,1)}, bf16[3,4,128,128]{3,2,1,0:T(8,128)(2,1)S(1)}, u32[]{:S(2)}, u32[]{:S(2)}) collective-permute-start(bf16[3,4,128,128]{3,2,1,0:T(8,128)(2,1)} %get-tuple-element.86), channel_id=1, source_target_pairs={{0,2},{2,0},{4,6},{6,4},{8,10},{10,8},{12,14},{14,12},{1,3},{3,1},... | collective-permute-start | bytes 1179656 | tf_op jit(solution)/shard_map/ppermute | solution.py:193
  11.5 45.4 %collective-permute-start.3 = (bf16[3,4,128,128]{3,2,1,0:T(8,128)(2,1)}, bf16[3,4,128,128]{3,2,1,0:T(8,128)(2,1)S(1)}, u32[]{:S(2)}, u32[]{:S(2)}) collective-permute-start(bf16[3,4,128,128]{3,2,1,0:T(8,128)(2,1)} %get-tuple-element.87), channel_id=1, source_target_pairs={{0,4},{2,6},{4,0},{6,2},{8,12},{10,14},{12,8},{14,10},{1,5},{3,7},... | collective-permute-start | bytes 1179656 | tf_op jit(solution)/shard_map/ppermute | solution.py:193
  12.0 45.4 %collective-permute-start.4 = (bf16[3,4,128,128]{3,2,1,0:T(8,128)(2,1)}, bf16[3,4,128,128]{3,2,1,0:T(8,128)(2,1)S(1)}, u32[]{:S(2)}, u32[]{:S(2)}) collective-permute-start(bf16[3,4,128,128]{3,2,1,0:T(8,128)(2,1)} %get-tuple-element.88), channel_id=1, source_target_pairs={{0,6},{2,4},{4,2},{6,0},{8,14},{10,12},{12,10},{14,8},{1,7},{3,5},... | collective-permute-start | bytes 1179656 | tf_op jit(solution)/shard_map/ppermute | solution.py:193
  22.7 13.2 %collective-permute-start.7 = (bf16[2,4,128,128]{3,2,1,0:T(8,128)(2,1)S(1)}, bf16[2,4,128,128]{3,2,1,0:T(8,128)(2,1)S(1)}, u32[]{:S(2)}, u32[]{:S(2)}) collective-permute-start(bf16[2,4,128,128]{3,2,1,0:T(8,128)(2,1)S(1)} %copy-done.3), channel_id=1, source_target_pairs={{0,12},{2,14},{4,8},{6,10},{8,4},{10,6},{12,0},{14,2},{1,13},{3,15... | collective-permute-start | bytes 786440 | tf_op jit(solution)/shard_map/ppermute | solution.py:193
  28.3 27.0 %collective-permute-start.8 = (bf16[2,4,128,128]{3,2,1,0:T(8,128)(2,1)S(1)}, bf16[2,4,128,128]{3,2,1,0:T(8,128)(2,1)S(1)}, u32[]{:S(2)}, u32[]{:S(2)}) collective-permute-start(bf16[2,4,128,128]{3,2,1,0:T(8,128)(2,1)S(1)} %copy-done.2), channel_id=1, source_target_pairs={{0,14},{2,12},{4,10},{6,8},{8,6},{10,4},{12,2},{14,0},{1,15},{3,13... | collective-permute-start | bytes 786440 | tf_op jit(solution)/shard_map/ppermute | solution.py:193
  35.9 35.2 %collective-permute-start.9 = (bf16[1,4,128,128]{3,2,1,0:T(8,128)(2,1)}, bf16[1,4,128,128]{3,2,1,0:T(8,128)(2,1)S(1)}, u32[]{:S(2)}, u32[]{:S(2)}) collective-permute-start(bf16[1,4,128,128]{3,2,1,0:T(8,128)(2,1)} %get-tuple-element.96), channel_id=1, source_target_pairs={{0,8},{2,10},{4,12},{6,14},{8,0},{10,2},{12,4},{14,6},{1,9},{3,11}... | collective-permute-start | bytes 393224 | tf_op jit(solution)/shard_map/ppermute | solution.py:193
  55.3 20.6 %collective-permute-start.10 = (bf16[1,4,128,128]{3,2,1,0:T(8,128)(2,1)}, bf16[1,4,128,128]{3,2,1,0:T(8,128)(2,1)S(1)}, u32[]{:S(2)}, u32[]{:S(2)}) collective-permute-start(bf16[1,4,128,128]{3,2,1,0:T(8,128)(2,1)} %get-tuple-element.97), channel_id=1, source_target_pairs={{0,10},{2,8},{4,14},{6,12},{8,2},{10,0},{12,6},{14,4},{1,11},{3,9}... | collective-permute-start | bytes 393224 | tf_op jit(solution)/shard_map/ppermute | solution.py:193
  55.4 20.5 %collective-permute-start.11 = (bf16[1,4,128,128]{3,2,1,0:T(8,128)(2,1)}, bf16[1,4,128,128]{3,2,1,0:T(8,128)(2,1)S(1)}, u32[]{:S(2)}, u32[]{:S(2)}) collective-permute-start(bf16[1,4,128,128]{3,2,1,0:T(8,128)(2,1)} %get-tuple-element.98), channel_id=1, source_target_pairs={{0,12},{2,14},{4,8},{6,10},{8,4},{10,6},{12,0},{14,2},{1,13},{3,15... | collective-permute-start | bytes 393224 | tf_op jit(solution)/shard_map/ppermute | solution.py:193
  56.9 19.0 %collective-permute-start.12 = (bf16[1,4,128,128]{3,2,1,0:T(8,128)(2,1)}, bf16[1,4,128,128]{3,2,1,0:T(8,128)(2,1)S(1)}, u32[]{:S(2)}, u32[]{:S(2)}) collective-permute-start(bf16[1,4,128,128]{3,2,1,0:T(8,128)(2,1)} %get-tuple-element.99), channel_id=1, source_target_pairs={{0,14},{2,12},{4,10},{6,8},{8,6},{10,4},{12,2},{14,0},{1,15},{3,13... | collective-permute-start | bytes 393224 | tf_op jit(solution)/shard_map/ppermute | solution.py:193
  59.3 4.6 %collective-permute-start.1 = (bf16[8,2,4,128,128]{4,3,2,1,0:T(8,128)(2,1)}, bf16[8,2,4,128,128]{4,3,2,1,0:T(8,128)(2,1)}, u32[]{:S(2)}, u32[]{:S(2)}) collective-permute-start(bf16[8,2,4,128,128]{4,3,2,1,0:T(8,128)(2,1)} %gather.3), channel_id=1, source_target_pairs={{0,1},{1,0},{2,3},{3,2},{4,5},{5,4},{6,7},{7,6},{8,9},{9,8},{10,11... | collective-permute-start | bytes 6291464 | tf_op jit(solution)/shard_map/cond/branch_1_fun/ppermute | solution.py:193
  69.5 13.7 %collective-permute-start.17 = (bf16[4,128,128]{2,1,0:T(8,128)(2,1)S(1)}, bf16[4,128,128]{2,1,0:T(8,128)(2,1)S(1)}, u32[]{:S(2)}, u32[]{:S(2)}) collective-permute-start(bf16[4,128,128]{2,1,0:T(8,128)(2,1)S(1)} %get-tuple-element.105), channel_id=1, source_target_pairs={{0,2},{2,0},{4,6},{6,4},{8,10},{10,8},{12,14},{14,12},{1,3},{3,1},... | collective-permute-start | bytes 393224 | tf_op jit(solution)/shard_map/ppermute | solution.py:193
  71.1 12.7 %collective-permute-start.18 = (bf16[4,128,128]{2,1,0:T(8,128)(2,1)S(1)}, bf16[4,128,128]{2,1,0:T(8,128)(2,1)S(1)}, u32[]{:S(2)}, u32[]{:S(2)}) collective-permute-start(bf16[4,128,128]{2,1,0:T(8,128)(2,1)S(1)} %get-tuple-element.106), channel_id=1, source_target_pairs={{0,4},{2,6},{4,0},{6,2},{8,12},{10,14},{12,8},{14,10},{1,5},{3,7},... | collective-permute-start | bytes 393224 | tf_op jit(solution)/shard_map/ppermute | solution.py:193
  79.3 14.4 %collective-permute-start.13 = (bf16[4,128,128]{2,1,0:T(8,128)(2,1)S(1)}, bf16[4,128,128]{2,1,0:T(8,128)(2,1)S(1)}, u32[]{:S(2)}, u32[]{:S(2)}) collective-permute-start(bf16[4,128,128]{2,1,0:T(8,128)(2,1)S(1)} %get-tuple-element.100), channel_id=1, source_target_pairs={{0,8},{2,10},{4,12},{6,14},{8,0},{10,2},{12,4},{14,6},{1,9},{3,11}... | collective-permute-start | bytes 393224 | tf_op jit(solution)/shard_map/ppermute | solution.py:193
  79.4 17.8 %collective-permute-start.14 = (bf16[4,128,128]{2,1,0:T(8,128)(2,1)S(1)}, bf16[4,128,128]{2,1,0:T(8,128)(2,1)S(1)}, u32[]{:S(2)}, u32[]{:S(2)}) collective-permute-start(bf16[4,128,128]{2,1,0:T(8,128)(2,1)S(1)} %get-tuple-element.101), channel_id=1, source_target_pairs={{0,10},{2,8},{4,14},{6,12},{8,2},{10,0},{12,6},{14,4},{1,11},{3,9}... | collective-permute-start | bytes 393224 | tf_op jit(solution)/shard_map/ppermute | solution.py:193
  83.2 9.0 %collective-permute-start.19 = (bf16[4,128,128]{2,1,0:T(8,128)(2,1)S(1)}, bf16[4,128,128]{2,1,0:T(8,128)(2,1)S(1)}, u32[]{:S(2)}, u32[]{:S(2)}) collective-permute-start(bf16[4,128,128]{2,1,0:T(8,128)(2,1)S(1)} %get-tuple-element.107), channel_id=1, source_target_pairs={{0,6},{2,4},{4,2},{6,0},{8,14},{10,12},{12,10},{14,8},{1,7},{3,5},... | collective-permute-start | bytes 393224 | tf_op jit(solution)/shard_map/ppermute | solution.py:193
  83.2 18.8 %collective-permute-start.15 = (bf16[4,128,128]{2,1,0:T(8,128)(2,1)S(1)}, bf16[4,128,128]{2,1,0:T(8,128)(2,1)S(1)}, u32[]{:S(2)}, u32[]{:S(2)}) collective-permute-start(bf16[4,128,128]{2,1,0:T(8,128)(2,1)S(1)} %get-tuple-element.102), channel_id=1, source_target_pairs={{0,12},{2,14},{4,8},{6,10},{8,4},{10,6},{12,0},{14,2},{1,13},{3,15... | collective-permute-start | bytes 393224 | tf_op jit(solution)/shard_map/ppermute | solution.py:193
  83.8 20.8 %collective-permute-start.16 = (bf16[4,128,128]{2,1,0:T(8,128)(2,1)S(1)}, bf16[4,128,128]{2,1,0:T(8,128)(2,1)S(1)}, u32[]{:S(2)}, u32[]{:S(2)}) collective-permute-start(bf16[4,128,128]{2,1,0:T(8,128)(2,1)S(1)} %get-tuple-element.103), channel_id=1, source_target_pairs={{0,14},{2,12},{4,10},{6,8},{8,6},{10,4},{12,2},{14,0},{1,15},{3,13... | collective-permute-start | bytes 393224 | tf_op jit(solution)/shard_map/ppermute | solution.py:193

commit v4 on v3

--- a/solution.py
+++ b/solution.py
@@ -443,8 +443,8 @@
     sizes = (queries.shape[2], tables[0].shape[1], tables[2].shape[1])
     flat = jnp.concatenate([table.T.reshape(-1) for table in tables])
     near, far = list(range(groups // 2)), list(range(groups // 2, groups))
-    def send(part, mask, *behind):
-        return swap_with(after(part, *behind) if behind else part, GROUP, mask)
+    def send(part, mask):
+        return swap_with(part, GROUP, mask) if mask else part
 
     keys, values, queries = keys[0], values[0], queries[0]
     pieces = [(mask, 0, 2) for mask in far]
@@ -452,9 +452,9 @@
     takes = [(near, 0), (near, 1), (near, 2), (far, 2)]
     pieces = [(mask, 0, 3) for mask in near] + [(mask, 3, 1) for mask in far]
     rest = regroup(place, (keys, values, after(queries, flat)), takes, pieces, groups)
-    got = {mask: send(kv_far[mask, 0, 2], mask) for mask in far}
-    for mask in near:
-        got[mask] = send(rest[mask, 0, 3], mask) if mask else rest[mask, 0, 3]
+    got = {mask: send(rest[mask, 0, 3], mask) for mask in near}
+    got.update({mask: send(kv_far[mask, 0, 2], mask) for mask in far})
+
     def share(*parts):
         own = gather(place, parts)
         return own, swap_with(own, "sub", 1)
@@ -466,13 +466,12 @@
     some = tables[1][0] >= 1
     sides = lax.cond(some, share, share_again, *[got[mask] for mask in range(groups)])
     arrived = {mask: got[mask] for mask in near}
-    for mask in far:
-        arrived[mask] = send(rest[mask, 3, 1], mask)
-    outs, kv = attend(place, flat, sizes, sides, arrived, near)
-    outs.update(attend(place, flat, sizes, kv, arrived, far)[0])
-    back = {mask: send(outs[mask], mask) for mask in far}
-    for mask in near:
-        back[mask] = send(outs[mask], mask) if mask else outs[mask]
+    arrived.update({mask: send(rest[mask, 3, 1], mask) for mask in far})
+    cut = len(far) // 2
+    outs, kv = attend(place, flat, sizes, sides, arrived, near + far[:cut])
+    outs.update(attend(place, flat, sizes, kv, arrived, far[cut:])[0])
+    back = {mask: send(outs[mask], mask) for mask in near}
+    back.update({mask: send(outs[mask], mask) for mask in far})
     begun = ungroup(place, back, near, groups)
     return ungroup(place, back, far, groups, begun)[None]
 

time: 106 us -> 105 us (level)
  starting transfers between devices: 32.8 us -> 30 us
  waiting for transfers between devices: 52.3 us -> 54 us
    ppermute x19, starting transfers between devices: 32.8 us -> 30 us  [swap_with(): lax.ppermute(value, axes, [(source, source ^ mask) for source in range(co...]
    ppermute x19, waiting for transfers between devices: 52.3 us -> 54 us  [swap_with(): lax.ppermute(value, axes, [(source, source ^ mask) for source in range(co...]
  transfers between devices with their start and end apart: 19 -> 19, of which waited for: 9 -> 10; matrix products, arithmetic and copies ran while one was open for 0% -> 0% of each run, Pallas kernels for 15% -> 15%
where the time goes in v4:
time: 105 us
  waiting for transfers between devices  54 us (51%)
  starting transfers between devices  30 us (29%)
  Pallas kernels  20.3 us (19%)
    ppermute x19, waiting for transfers between devices, swap_with(): lax.ppermute(value, axes, [(source, source ^ mask) for source in range(co...  54 us
    ppermute x19, starting transfers between devices, swap_with(): lax.ppermute(value, axes, [(source, source ^ mask) for source in range(co...  30 us
    pallas_call x2, Pallas kernels, attend(): pl.pallas_call(functools.partial(attend_kernel, masks=masks, sizes=sizes,...  8.84 us
    pallas_call x2, Pallas kernels, regroup(): pl.pallas_call(functools.partial(regroup_kernel, tensors=len(tensors), ta...  6.62 us
    pallas_call x2, Pallas kernels, ungroup(): pl.pallas_call(functools.partial(ungroup_kernel, masks=masks, groups=grou...  2.9 us
  transfers between devices with their start and end apart: 19, of which 10 were waited for; matrix products, arithmetic and copies ran while one was open for 0% of the time, Pallas kernels for 15%

profile of v4, /device:TPU:12, one launch (start us, length us, event | category | flops | bytes accessed | tf_op | source)
XLA Modules:
  0.0 104.8 jit_solution(4642161777739170800)
XLA Ops:
  0.1 2.8 %regroup.3 = (bf16[2,4,128,128]{3,2,1,0:T(8,128)(2,1)}, bf16[2,4,128,128]{3,2,1,0:T(8,128)(2,1)}, bf16[2,4,128,128]{3,2,1,0:T(8,128)(2,1)}, bf16[2,4,128,128]{3,2,1,0:T(8,128)(2,1)}) custom-call(s32[2]{0:T(128)S(1)} %pad_add_fusion.1.place, bf16[128,32,128]{2,1,0:T(8,128)(2,1)} %bitcast.10, bf16[128,32,128]{2,1,0:T(8,128)(2,1)} %bitcast.12), custom_call_target="tpu_custom_call" | custom-call | flops 1 | bytes 1 | tf_op jit(solution)/shard_map/regroup/pallas_call | solution.py:235
  2.9 2.7 %collective-permute-start.5 = (bf16[2,4,128,128]{3,2,1,0:T(8,128)(2,1)}, bf16[2,4,128,128]{3,2,1,0:T(8,128)(2,1)S(1)}, u32[]{:S(2)}, u32[]{:S(2)}) collective-permute-start(bf16[2,4,128,128]{3,2,1,0:T(8,128)(2,1)} %get-tuple-element.89), channel_id=1, source_target_pairs={{0,8},{2,10},{4,12},{6,14},{8,0},{10,2},{12,4},{14,6},{1,9},{3,11}... | collective-permute-start | bytes 786440 | tf_op jit(solution)/shard_map/ppermute | solution.py:193
  5.6 1.3 %collective-permute-start.6 = (bf16[2,4,128,128]{3,2,1,0:T(8,128)(2,1)}, bf16[2,4,128,128]{3,2,1,0:T(8,128)(2,1)S(1)}, u32[]{:S(2)}, u32[]{:S(2)}) collective-permute-start(bf16[2,4,128,128]{3,2,1,0:T(8,128)(2,1)} %get-tuple-element.90), channel_id=1, source_target_pairs={{0,10},{2,8},{4,14},{6,12},{8,2},{10,0},{12,6},{14,4},{1,11},{3,9}... | collective-permute-start | bytes 786440 | tf_op jit(solution)/shard_map/ppermute | solution.py:193
  7.1 3.8 %regroup.2 = (bf16[3,4,128,128]{3,2,1,0:T(8,128)(2,1)S(1)}, bf16[3,4,128,128]{3,2,1,0:T(8,128)(2,1)}, bf16[3,4,128,128]{3,2,1,0:T(8,128)(2,1)}, bf16[3,4,128,128...) custom-call(s32[2]{0:T(128)S(1)} %pad_add_fusion.1.place, ...), custom_call_target="tpu_custom_call" | custom-call | flops 1 | bytes 1 | tf_op jit(solution)/shard_map/regroup/pallas_call | solution.py:235
  10.9 0.6 collective-permute-start.2
  12.0 2.5 %collective-permute-start.4 = (bf16[3,4,128,128]{3,2,1,0:T(8,128)(2,1)}, bf16[3,4,128,128]{3,2,1,0:T(8,128)(2,1)S(1)}, u32[]{:S(2)}, u32[]{:S(2)}) collective-permute-start(bf16[3,4,128,128]{3,2,1,0:T(8,128)(2,1)} %get-tuple-element.88), channel_id=1, source_target_pairs={{0,6},{2,4},{4,2},{6,0},{8,14},{10,12},{12,10},{14,8},{1,7},{3,5},... | collective-permute-start | bytes 1179656 | tf_op jit(solution)/shard_map/ppermute | solution.py:193
  14.5 8.2 %collective-permute-done.5 = bf16[2,4,128,128]{3,2,1,0:T(8,128)(2,1)S(1)} collective-permute-done((bf16[2,4,128,128]{3,2,1,0:T(8,128)(2,1)}, bf16[2,4,128,128]{3,2,1,0:T(8,128)(2,1)S(1)}, u32[]{:S(2)}, u32[]{:S(2)}) %collective-permute-start.5) | collective-permute-done | bytes 262176 | tf_op jit(solution)/shard_map/ppermute | solution.py:193
  23.2 5.1 %collective-permute-done.6 = bf16[2,4,128,128]{3,2,1,0:T(8,128)(2,1)S(1)} collective-permute-done((bf16[2,4,128,128]{3,2,1,0:T(8,128)(2,1)}, bf16[2,4,128,128]{3,2,1,0:T(8,128)(2,1)S(1)}, u32[]{:S(2)}, u32[]{:S(2)}) %collective-permute-start.6) | collective-permute-done | bytes 262176 | tf_op jit(solution)/shard_map/ppermute | solution.py:193
  28.3 1.4 %collective-permute-start.8 = (bf16[2,4,128,128]{3,2,1,0:T(8,128)(2,1)S(1)}, bf16[2,4,128,128]{3,2,1,0:T(8,128)(2,1)S(1)}, u32[]{:S(2)}, u32[]{:S(2)}) collective-permute-start(bf16[2,4,128,128]{3,2,1,0:T(8,128)(2,1)S(1)} %copy-done.2), channel_id=1, source_target_pairs={{0,14},{2,12},{4,10},{6,8},{8,6},{10,4},{12,2},{14,0},{1,15},{3,13... | collective-permute-start | bytes 786440 | tf_op jit(solution)/shard_map/ppermute | solution.py:193
  29.7 6.2 %collective-permute-done.7 = bf16[2,4,128,128]{3,2,1,0:T(8,128)(2,1)S(1)} collective-permute-done((bf16[2,4,128,128]{3,2,1,0:T(8,128)(2,1)S(1)}, bf16[2,4,128,128]{3,2,1,0:T(8,128)(2,1)S(1)}, u32[]{:S(2)}, u32[]{:S(2)}) %collective-permute-start.7) | collective-permute-done | bytes 262176 | tf_op jit(solution)/shard_map/ppermute | solution.py:193
  35.9 8.2 %collective-permute-start.9 = (bf16[1,4,128,128]{3,2,1,0:T(8,128)(2,1)}, bf16[1,4,128,128]{3,2,1,0:T(8,128)(2,1)S(1)}, u32[]{:S(2)}, u32[]{:S(2)}) collective-permute-start(bf16[1,4,128,128]{3,2,1,0:T(8,128)(2,1)} %get-tuple-element.95), channel_id=1, source_target_pairs={{0,8},{2,10},{4,12},{6,14},{8,0},{10,2},{12,4},{14,6},{1,9},{3,11}... | collective-permute-start | bytes 393224 | tf_op jit(solution)/shard_map/ppermute | solution.py:193
  44.1 11.3 %collective-permute-done.8 = bf16[2,4,128,128]{3,2,1,0:T(8,128)(2,1)S(1)} collective-permute-done((bf16[2,4,128,128]{3,2,1,0:T(8,128)(2,1)S(1)}, bf16[2,4,128,128]{3,2,1,0:T(8,128)(2,1)S(1)}, u32[]{:S(2)}, u32[]{:S(2)}) %collective-permute-start.8) | collective-permute-done | bytes 262176 | tf_op jit(solution)/shard_map/ppermute | solution.py:193
  55.4 1.6 %collective-permute-start.13 = (bf16[1,4,128,128]{3,2,1,0:T(8,128)(2,1)}, bf16[1,4,128,128]{3,2,1,0:T(8,128)(2,1)S(1)}, u32[]{:S(2)}, u32[]{:S(2)}) collective-permute-start(bf16[1,4,128,128]{3,2,1,0:T(8,128)(2,1)} %get-tuple-element.100), channel_id=1, source_target_pairs={{0,12},{2,14},{4,8},{6,10},{8,4},{10,6},{12,0},{14,2},{1,13},{3,15... | collective-permute-start | bytes 393224 | tf_op jit(solution)/shard_map/ppermute | solution.py:193
  57.5 6.5 %conditional.1 = (bf16[8,2,4,128,128]{4,3,2,1,0:T(8,128)(2,1)}, bf16[8,2,4,128,128]{4,3,2,1,0:T(8,128)(2,1)}) conditional(s32[]{:T(128)} %bitcast.4, (s32[2]{0:T(128)S(1)}, bf16[3,4,128,128]{3,2,1,0:T(8,128)(2,1)S(1)}, bf16[3,4,128,128]{3,2,1,0:T(8,128)(2,1)S(1)}, bf16[3,4,128,128]{3,2,1,0:T(8,128)(2,1)S(1)}, bf16[3,4,128,128]{3,2,1,0:T(8,128)(2,1)S(1)}, ...), branch_computations={%region_0.0_spmd, %region_1.0_spmd} | conditional | flops 1 | bytes 8388665 | solution.py:467
  57.5 1.9 %gather.3 = bf16[8,2,4,128,128]{4,3,2,1,0:T(8,128)(2,1)} custom-call(s32[2]{0:T(128)S(1)} %get-tuple-element.51.place, bf16[3,4,128,128]{3,2,1,0:T(8,128)(2,1)S(1)} %get-tuple-element.52.refs_0_, bf16[3,4,128,128]{3,2,1,0:T(8,128)(2,1)S(1)} %get-tuple-element.53.refs_1_, bf16[3,4,128,128]{3,2,1,0:T(8,128)(2,1)S(1)} %get-tuple-element.54.refs_2_, ...), custom_call_target="tpu_custom_call" | custom-call | flops 1 | bytes 1 | tf_op jit(solution)/shard_map/cond/branch_1_fun/gather/pallas_call | solution.py:321
  59.5 4.5 %collective-permute-done.1 = bf16[8,2,4,128,128]{4,3,2,1,0:T(8,128)(2,1)} collective-permute-done((bf16[8,2,4,128,128]{4,3,2,1,0:T(8,128)(2,1)}, bf16[8,2,4,128,128]{4,3,2,1,0:T(8,128)(2,1)}, u32[]{:S(2)}, u32[]{:S(2)}) %collective-permute-start.1) | collective-permute-done | bytes 2097184 | tf_op jit(solution)/shard_map/cond/branch_1_fun/ppermute | solution.py:193
  64.0 4.1 %collective-permute-done.10.refs_7_ = bf16[1,4,128,128]{3,2,1,0:T(8,128)(2,1)S(1)} collective-permute-done((bf16[1,4,128,128]{3,2,1,0:T(8,128)(2,1)}, bf16[1,4,128,128]{3,2,1,0:T(8,128)(2,1)S(1)}, u32[]{:S(2)}, u32[]{:S(2)}) %collective-permute-start.10) | collective-permute-done | bytes 131104 | tf_op jit(solution)/shard_map/ppermute | solution.py:193
  68.0 6.7 %attend.2 = (bf16[4,128,128]{2,1,0:T(8,128)(2,1)S(1)}, bf16[4,128,128]{2,1,0:T(8,128)(2,1)S(1)}, bf16[4,128,128]{2,1,0:T(8,128)(2,1)S(1)}, bf16[4,128,128]{2,1,0...) custom-call(s32[2]{0:T(128)S(1)} %pad_add_fusion.1.place, ...), custom_call_target="tpu_custom_call" | custom-call | flops 1 | bytes 1 | tf_op jit(solution)/shard_map/attend/pallas_call | solution.py:414
  74.8 1.1 %collective-permute-start.17 = (bf16[4,128,128]{2,1,0:T(8,128)(2,1)S(1)}, bf16[4,128,128]{2,1,0:T(8,128)(2,1)S(1)}, u32[]{:S(2)}, u32[]{:S(2)}) collective-permute-start(bf16[4,128,128]{2,1,0:T(8,128)(2,1)S(1)} %get-tuple-element.105), channel_id=1, source_target_pairs={{0,2},{2,0},{4,6},{6,4},{8,10},{10,8},{12,14},{14,12},{1,3},{3,1},... | collective-permute-start | bytes 393224 | tf_op jit(solution)/shard_map/ppermute | solution.py:193
  75.9 3.2 %collective-permute-start.18 = (bf16[4,128,128]{2,1,0:T(8,128)(2,1)S(1)}, bf16[4,128,128]{2,1,0:T(8,128)(2,1)S(1)}, u32[]{:S(2)}, u32[]{:S(2)}) collective-permute-start(bf16[4,128,128]{2,1,0:T(8,128)(2,1)S(1)} %get-tuple-element.106), channel_id=1, source_target_pairs={{0,4},{2,6},{4,0},{6,2},{8,12},{10,14},{12,8},{14,10},{1,5},{3,7},... | collective-permute-start | bytes 393224 | tf_op jit(solution)/shard_map/ppermute | solution.py:193
  79.1 0.5 collective-permute-start.11
  79.6 2.4 %collective-permute-start.12 = (bf16[4,128,128]{2,1,0:T(8,128)(2,1)S(1)}, bf16[4,128,128]{2,1,0:T(8,128)(2,1)S(1)}, u32[]{:S(2)}, u32[]{:S(2)}) collective-permute-start(bf16[4,128,128]{2,1,0:T(8,128)(2,1)S(1)} %get-tuple-element.98), channel_id=1, source_target_pairs={{0,10},{2,8},{4,14},{6,12},{8,2},{10,0},{12,6},{14,4},{1,11},{3,9}... | collective-permute-start | bytes 393224 | tf_op jit(solution)/shard_map/ppermute | solution.py:193
  82.0 0.9 collective-permute-start.19
  83.0 2.1 %attend.3 = (bf16[4,128,128]{2,1,0:T(8,128)(2,1)S(1)}, bf16[4,128,128]{2,1,0:T(8,128)(2,1)S(1)}) custom-call(s32[2]{0:T(128)S(1)} %pad_add_fusion.1.place, s32[192]{0:T(256)S(1)} %pad_add_fusion.tables, bf16[4,2,8,2,128,128]{5,4,3,2,1,0:T(8,128)(2,1)S(1)} %get-tuple-element.99.refs_0_, bf16[1,4,128,128]{3,2,1,0:T(8,128)(2,1)S(1)} %collective-permute-done.13.refs_1_, ...), custom_call_target="tpu_custom_call" | custom-call | flops 1 | bytes 1 | tf_op jit(solution)/shard_map/attend/pallas_call | solution.py:414
  85.1 1.1 %collective-permute-start.15 = (bf16[4,128,128]{2,1,0:T(8,128)(2,1)S(1)}, bf16[4,128,128]{2,1,0:T(8,128)(2,1)S(1)}, u32[]{:S(2)}, u32[]{:S(2)}) collective-permute-start(bf16[4,128,128]{2,1,0:T(8,128)(2,1)S(1)} %get-tuple-element.102), channel_id=1, source_target_pairs={{0,12},{2,14},{4,8},{6,10},{8,4},{10,6},{12,0},{14,2},{1,13},{3,15... | collective-permute-start | bytes 393224 | tf_op jit(solution)/shard_map/ppermute | solution.py:193
  86.2 1.1 %collective-permute-start.16 = (bf16[4,128,128]{2,1,0:T(8,128)(2,1)S(1)}, bf16[4,128,128]{2,1,0:T(8,128)(2,1)S(1)}, u32[]{:S(2)}, u32[]{:S(2)}) collective-permute-start(bf16[4,128,128]{2,1,0:T(8,128)(2,1)S(1)} %get-tuple-element.103), channel_id=1, source_target_pairs={{0,14},{2,12},{4,10},{6,8},{8,6},{10,4},{12,2},{14,0},{1,15},{3,13... | collective-permute-start | bytes 393224 | tf_op jit(solution)/shard_map/ppermute | solution.py:193
  87.3 4.9 %collective-permute-done.19.refs_3_ = bf16[4,128,128]{2,1,0:T(8,128)(2,1)S(1)} collective-permute-done((bf16[4,128,128]{2,1,0:T(8,128)(2,1)S(1)}, bf16[4,128,128]{2,1,0:T(8,128)(2,1)S(1)}, u32[]{:S(2)}, u32[]{:S(2)}) %collective-permute-start.19) | collective-permute-done | bytes 131104 | tf_op jit(solution)/shard_map/ppermute | solution.py:193
  92.2 1.4 %ungroup.2.refs_4_ = bf16[128,32,128]{2,1,0:T(8,128)(2,1)} custom-call(s32[2]{0:T(128)S(1)} %pad_add_fusion.1.place, bf16[4,128,128]{2,1,0:T(8,128)(2,1)S(1)} %get-tuple-element.104.refs_0_, bf16[4,128,128]{2,1,0:T(8,128)(2,1)S(1)} %collective-permute-done.17.refs_1_, bf16[4,128,128]{2,1,0:T(8,128)(2,1)S(1)} %collective-permute-done.18.refs_2_, ...), custom_call_target="tpu_custom_call" | custom-call | flops 1 | bytes 1 | tf_op jit(solution)/shard_map/ungroup/pallas_call | solution.py:280
  93.6 3.4 %collective-permute-done.12.refs_1_ = bf16[4,128,128]{2,1,0:T(8,128)(2,1)S(1)} collective-permute-done((bf16[4,128,128]{2,1,0:T(8,128)(2,1)S(1)}, bf16[4,128,128]{2,1,0:T(8,128)(2,1)S(1)}, u32[]{:S(2)}, u32[]{:S(2)}) %collective-permute-start.12) | collective-permute-done | bytes 131104 | tf_op jit(solution)/shard_map/ppermute | solution.py:193
  97.1 4.0 %collective-permute-done.15.refs_2_ = bf16[4,128,128]{2,1,0:T(8,128)(2,1)S(1)} collective-permute-done((bf16[4,128,128]{2,1,0:T(8,128)(2,1)S(1)}, bf16[4,128,128]{2,1,0:T(8,128)(2,1)S(1)}, u32[]{:S(2)}, u32[]{:S(2)}) %collective-permute-start.15) | collective-permute-done | bytes 131104 | tf_op jit(solution)/shard_map/ppermute | solution.py:193
  101.0 2.3 %collective-permute-done.16.refs_3_ = bf16[4,128,128]{2,1,0:T(8,128)(2,1)S(1)} collective-permute-done((bf16[4,128,128]{2,1,0:T(8,128)(2,1)S(1)}, bf16[4,128,128]{2,1,0:T(8,128)(2,1)S(1)}, u32[]{:S(2)}, u32[]{:S(2)}) %collective-permute-start.16) | collective-permute-done | bytes 131104 | tf_op jit(solution)/shard_map/ppermute | solution.py:193
  103.4 1.4 %ungroup.3 = bf16[128,32,128]{2,1,0:T(8,128)(2,1)} custom-call(s32[2]{0:T(128)S(1)} %pad_add_fusion.1.place, bf16[4,128,128]{2,1,0:T(8,128)(2,1)S(1)} %collective-permute-done.11.refs_0_, bf16[4,128,128]{2,1,0:T(8,128)(2,1)S(1)} %collective-permute-done.12.refs_1_, ...), custom_call_target="tpu_custom_call", output_to_operand_aliasing={{}: (5, {})} | custom-call | flops 1 | bytes 1 | tf_op jit(solution)/shard_map/ungroup/pallas_call | solution.py:280
  (30 shorter events, 1.8 us)
Async XLA Ops:
  0.0 6.8 %copy-start.4 = (s32[32,2]{0,1:T(2,128)S(1)}, s32[32,2]{0,1:T(2,128)}, u32[]{:S(2)}) copy-start(s32[32,2]{0,1:T(2,128)} %param.12) | copy-start | bytes 772
  0.0 6.9 %copy-start.5 = (s32[32,2]{0,1:T(2,128)S(1)}, s32[32,2]{0,1:T(2,128)}, u32[]{:S(2)}) copy-start(s32[32,2]{0,1:T(2,128)} %param.14) | copy-start | bytes 772
  0.0 7.0 %copy-start.1 = (s32[32]{0:T(128)S(1)}, s32[32]{0:T(128)}, u32[]{:S(2)}) copy-start(s32[32]{0:T(128)} %param.13) | copy-start | bytes 388
  0.0 7.0 %copy-start = (s32[32]{0:T(128)S(1)}, s32[32]{0:T(128)}, u32[]{:S(2)}) copy-start(s32[32]{0:T(128)} %param.15) | copy-start | bytes 388
  2.9 19.8 %copy-start.3 = (bf16[2,4,128,128]{3,2,1,0:T(8,128)(2,1)S(1)}, bf16[2,4,128,128]{3,2,1,0:T(8,128)(2,1)}, u32[]{:S(2)}) copy-start(bf16[2,4,128,128]{3,2,1,0:T(8,128)(2,1)} %get-tuple-element.91) | copy-start | bytes 786436
  2.9 25.4 %copy-start.2 = (bf16[2,4,128,128]{3,2,1,0:T(8,128)(2,1)S(1)}, bf16[2,4,128,128]{3,2,1,0:T(8,128)(2,1)}, u32[]{:S(2)}) copy-start(bf16[2,4,128,128]{3,2,1,0:T(8,128)(2,1)} %get-tuple-element.92) | copy-start | bytes 786436
  2.9 19.8 %collective-permute-start.5 = (bf16[2,4,128,128]{3,2,1,0:T(8,128)(2,1)}, bf16[2,4,128,128]{3,2,1,0:T(8,128)(2,1)S(1)}, u32[]{:S(2)}, u32[]{:S(2)}) collective-permute-start(bf16[2,4,128,128]{3,2,1,0:T(8,128)(2,1)} %get-tuple-element.89), channel_id=1, source_target_pairs={{0,8},{2,10},{4,12},{6,14},{8,0},{10,2},{12,4},{14,6},{1,9},{3,11}... | collective-permute-start | bytes 786440 | tf_op jit(solution)/shard_map/ppermute | solution.py:193
  5.6 22.8 %collective-permute-start.6 = (bf16[2,4,128,128]{3,2,1,0:T(8,128)(2,1)}, bf16[2,4,128,128]{3,2,1,0:T(8,128)(2,1)S(1)}, u32[]{:S(2)}, u32[]{:S(2)}) collective-permute-start(bf16[2,4,128,128]{3,2,1,0:T(8,128)(2,1)} %get-tuple-element.90), channel_id=1, source_target_pairs={{0,10},{2,8},{4,14},{6,12},{8,2},{10,0},{12,6},{14,4},{1,11},{3,9}... | collective-permute-start | bytes 786440 | tf_op jit(solution)/shard_map/ppermute | solution.py:193
  10.9 44.5 %collective-permute-start.2 = (bf16[3,4,128,128]{3,2,1,0:T(8,128)(2,1)}, bf16[3,4,128,128]{3,2,1,0:T(8,128)(2,1)S(1)}, u32[]{:S(2)}, u32[]{:S(2)}) collective-permute-start(bf16[3,4,128,128]{3,2,1,0:T(8,128)(2,1)} %get-tuple-element.86), channel_id=1, source_target_pairs={{0,2},{2,0},{4,6},{6,4},{8,10},{10,8},{12,14},{14,12},{1,3},{3,1},... | collective-permute-start | bytes 1179656 | tf_op jit(solution)/shard_map/ppermute | solution.py:193
  11.5 45.5 %collective-permute-start.3 = (bf16[3,4,128,128]{3,2,1,0:T(8,128)(2,1)}, bf16[3,4,128,128]{3,2,1,0:T(8,128)(2,1)S(1)}, u32[]{:S(2)}, u32[]{:S(2)}) collective-permute-start(bf16[3,4,128,128]{3,2,1,0:T(8,128)(2,1)} %get-tuple-element.87), channel_id=1, source_target_pairs={{0,4},{2,6},{4,0},{6,2},{8,12},{10,14},{12,8},{14,10},{1,5},{3,7},... | collective-permute-start | bytes 1179656 | tf_op jit(solution)/shard_map/ppermute | solution.py:193
  12.0 45.5 %collective-permute-start.4 = (bf16[3,4,128,128]{3,2,1,0:T(8,128)(2,1)}, bf16[3,4,128,128]{3,2,1,0:T(8,128)(2,1)S(1)}, u32[]{:S(2)}, u32[]{:S(2)}) collective-permute-start(bf16[3,4,128,128]{3,2,1,0:T(8,128)(2,1)} %get-tuple-element.88), channel_id=1, source_target_pairs={{0,6},{2,4},{4,2},{6,0},{8,14},{10,12},{12,10},{14,8},{1,7},{3,5},... | collective-permute-start | bytes 1179656 | tf_op jit(solution)/shard_map/ppermute | solution.py:193
  22.7 13.2 %collective-permute-start.7 = (bf16[2,4,128,128]{3,2,1,0:T(8,128)(2,1)S(1)}, bf16[2,4,128,128]{3,2,1,0:T(8,128)(2,1)S(1)}, u32[]{:S(2)}, u32[]{:S(2)}) collective-permute-start(bf16[2,4,128,128]{3,2,1,0:T(8,128)(2,1)S(1)} %copy-done.3), channel_id=1, source_target_pairs={{0,12},{2,14},{4,8},{6,10},{8,4},{10,6},{12,0},{14,2},{1,13},{3,15... | collective-permute-start | bytes 786440 | tf_op jit(solution)/shard_map/ppermute | solution.py:193
  28.3 27.0 %collective-permute-start.8 = (bf16[2,4,128,128]{3,2,1,0:T(8,128)(2,1)S(1)}, bf16[2,4,128,128]{3,2,1,0:T(8,128)(2,1)S(1)}, u32[]{:S(2)}, u32[]{:S(2)}) collective-permute-start(bf16[2,4,128,128]{3,2,1,0:T(8,128)(2,1)S(1)} %copy-done.2), channel_id=1, source_target_pairs={{0,14},{2,12},{4,10},{6,8},{8,6},{10,4},{12,2},{14,0},{1,15},{3,13... | collective-permute-start | bytes 786440 | tf_op jit(solution)/shard_map/ppermute | solution.py:193
  35.9 28.1 %collective-permute-start.9 = (bf16[1,4,128,128]{3,2,1,0:T(8,128)(2,1)}, bf16[1,4,128,128]{3,2,1,0:T(8,128)(2,1)S(1)}, u32[]{:S(2)}, u32[]{:S(2)}) collective-permute-start(bf16[1,4,128,128]{3,2,1,0:T(8,128)(2,1)} %get-tuple-element.95), channel_id=1, source_target_pairs={{0,8},{2,10},{4,12},{6,14},{8,0},{10,2},{12,4},{14,6},{1,9},{3,11}... | collective-permute-start | bytes 393224 | tf_op jit(solution)/shard_map/ppermute | solution.py:193
  55.3 12.7 %collective-permute-start.10 = (bf16[1,4,128,128]{3,2,1,0:T(8,128)(2,1)}, bf16[1,4,128,128]{3,2,1,0:T(8,128)(2,1)S(1)}, u32[]{:S(2)}, u32[]{:S(2)}) collective-permute-start(bf16[1,4,128,128]{3,2,1,0:T(8,128)(2,1)} %get-tuple-element.96), channel_id=1, source_target_pairs={{0,10},{2,8},{4,14},{6,12},{8,2},{10,0},{12,6},{14,4},{1,11},{3,9}... | collective-permute-start | bytes 393224 | tf_op jit(solution)/shard_map/ppermute | solution.py:193
  55.4 24.2 %collective-permute-start.13 = (bf16[1,4,128,128]{3,2,1,0:T(8,128)(2,1)}, bf16[1,4,128,128]{3,2,1,0:T(8,128)(2,1)S(1)}, u32[]{:S(2)}, u32[]{:S(2)}) collective-permute-start(bf16[1,4,128,128]{3,2,1,0:T(8,128)(2,1)} %get-tuple-element.100), channel_id=1, source_target_pairs={{0,12},{2,14},{4,8},{6,10},{8,4},{10,6},{12,0},{14,2},{1,13},{3,15... | collective-permute-start | bytes 393224 | tf_op jit(solution)/shard_map/ppermute | solution.py:193
  57.0 25.0 %collective-permute-start.14 = (bf16[1,4,128,128]{3,2,1,0:T(8,128)(2,1)}, bf16[1,4,128,128]{3,2,1,0:T(8,128)(2,1)S(1)}, u32[]{:S(2)}, u32[]{:S(2)}) collective-permute-start(bf16[1,4,128,128]{3,2,1,0:T(8,128)(2,1)} %get-tuple-element.101), channel_id=1, source_target_pairs={{0,14},{2,12},{4,10},{6,8},{8,6},{10,4},{12,2},{14,0},{1,15},{3,13... | collective-permute-start | bytes 393224 | tf_op jit(solution)/shard_map/ppermute | solution.py:193
  59.4 4.6 %collective-permute-start.1 = (bf16[8,2,4,128,128]{4,3,2,1,0:T(8,128)(2,1)}, bf16[8,2,4,128,128]{4,3,2,1,0:T(8,128)(2,1)}, u32[]{:S(2)}, u32[]{:S(2)}) collective-permute-start(bf16[8,2,4,128,128]{4,3,2,1,0:T(8,128)(2,1)} %gather.3), channel_id=1, source_target_pairs={{0,1},{1,0},{2,3},{3,2},{4,5},{5,4},{6,7},{7,6},{8,9},{9,8},{10,11... | collective-permute-start | bytes 6291464 | tf_op jit(solution)/shard_map/cond/branch_1_fun/ppermute | solution.py:193
  74.8 10.3 %collective-permute-start.17 = (bf16[4,128,128]{2,1,0:T(8,128)(2,1)S(1)}, bf16[4,128,128]{2,1,0:T(8,128)(2,1)S(1)}, u32[]{:S(2)}, u32[]{:S(2)}) collective-permute-start(bf16[4,128,128]{2,1,0:T(8,128)(2,1)S(1)} %get-tuple-element.105), channel_id=1, source_target_pairs={{0,2},{2,0},{4,6},{6,4},{8,10},{10,8},{12,14},{14,12},{1,3},{3,1},... | collective-permute-start | bytes 393224 | tf_op jit(solution)/shard_map/ppermute | solution.py:193
  75.9 10.2 %collective-permute-start.18 = (bf16[4,128,128]{2,1,0:T(8,128)(2,1)S(1)}, bf16[4,128,128]{2,1,0:T(8,128)(2,1)S(1)}, u32[]{:S(2)}, u32[]{:S(2)}) collective-permute-start(bf16[4,128,128]{2,1,0:T(8,128)(2,1)S(1)} %get-tuple-element.106), channel_id=1, source_target_pairs={{0,4},{2,6},{4,0},{6,2},{8,12},{10,14},{12,8},{14,10},{1,5},{3,7},... | collective-permute-start | bytes 393224 | tf_op jit(solution)/shard_map/ppermute | solution.py:193
  79.1 14.5 %collective-permute-start.11 = (bf16[4,128,128]{2,1,0:T(8,128)(2,1)S(1)}, bf16[4,128,128]{2,1,0:T(8,128)(2,1)S(1)}, u32[]{:S(2)}, u32[]{:S(2)}) collective-permute-start(bf16[4,128,128]{2,1,0:T(8,128)(2,1)S(1)} %get-tuple-element.97), channel_id=1, source_target_pairs={{0,8},{2,10},{4,12},{6,14},{8,0},{10,2},{12,4},{14,6},{1,9},{3,11}... | collective-permute-start | bytes 393224 | tf_op jit(solution)/shard_map/ppermute | solution.py:193
  79.6 17.5 %collective-permute-start.12 = (bf16[4,128,128]{2,1,0:T(8,128)(2,1)S(1)}, bf16[4,128,128]{2,1,0:T(8,128)(2,1)S(1)}, u32[]{:S(2)}, u32[]{:S(2)}) collective-permute-start(bf16[4,128,128]{2,1,0:T(8,128)(2,1)S(1)} %get-tuple-element.98), channel_id=1, source_target_pairs={{0,10},{2,8},{4,14},{6,12},{8,2},{10,0},{12,6},{14,4},{1,11},{3,9}... | collective-permute-start | bytes 393224 | tf_op jit(solution)/shard_map/ppermute | solution.py:193
  82.0 10.2 %collective-permute-start.19 = (bf16[4,128,128]{2,1,0:T(8,128)(2,1)S(1)}, bf16[4,128,128]{2,1,0:T(8,128)(2,1)S(1)}, u32[]{:S(2)}, u32[]{:S(2)}) collective-permute-start(bf16[4,128,128]{2,1,0:T(8,128)(2,1)S(1)} %get-tuple-element.107), channel_id=1, source_target_pairs={{0,6},{2,4},{4,2},{6,0},{8,14},{10,12},{12,10},{14,8},{1,7},{3,5},... | collective-permute-start | bytes 393224 | tf_op jit(solution)/shard_map/ppermute | solution.py:193
  85.1 16.0 %collective-permute-start.15 = (bf16[4,128,128]{2,1,0:T(8,128)(2,1)S(1)}, bf16[4,128,128]{2,1,0:T(8,128)(2,1)S(1)}, u32[]{:S(2)}, u32[]{:S(2)}) collective-permute-start(bf16[4,128,128]{2,1,0:T(8,128)(2,1)S(1)} %get-tuple-element.102), channel_id=1, source_target_pairs={{0,12},{2,14},{4,8},{6,10},{8,4},{10,6},{12,0},{14,2},{1,13},{3,15... | collective-permute-start | bytes 393224 | tf_op jit(solution)/shard_map/ppermute | solution.py:193
  86.2 17.2 %collective-permute-start.16 = (bf16[4,128,128]{2,1,0:T(8,128)(2,1)S(1)}, bf16[4,128,128]{2,1,0:T(8,128)(2,1)S(1)}, u32[]{:S(2)}, u32[]{:S(2)}) collective-permute-start(bf16[4,128,128]{2,1,0:T(8,128)(2,1)S(1)} %get-tuple-element.103), channel_id=1, source_target_pairs={{0,14},{2,12},{4,10},{6,8},{8,6},{10,4},{12,2},{14,0},{1,15},{3,13... | collective-permute-start | bytes 393224 | tf_op jit(solution)/shard_map/ppermute | solution.py:193

commit v5 on v4

--- a/solution.py
+++ b/solution.py
@@ -341,14 +341,12 @@
     if sides:
         sides, queries, outs = refs[:2], refs[2 : 2 + count], refs[2 + count : 2 + 2 * count]
         kv, sem = refs[-2:]
-        for slot in range(kv.shape[0]):
-            for at, side in enumerate(sides):
-                target = kv.at[slot, place[1] ^ at]
-                loads.append(pltpu.make_async_copy(side.at[:, :, slot], target, sem.at[slot, at]))
-                loads[-1].start()
+        for at, side in enumerate(sides):
+            loads.append(pltpu.make_async_copy(side, kv.at[place[1] ^ at], sem.at[at]))
+            loads[-1].start()
     else:
         kv, queries, outs = refs[0], refs[1 : 1 + count], refs[1 + count :]
-    heads, width = kv.shape[0], kv.shape[-1]
+    heads, width = kv.shape[3], kv.shape[-1]
     scaling = width ** (-0.5) * LOG2_E
     all_heads, n_vert, n_slash = sizes
     vert_cnt = all_heads * n_vert
@@ -360,7 +358,7 @@
 
     def tile(block, tensor, slot):
         span = block // n_seq
-        return kv[slot, span % 2, (span // 2) * n_seq + block % n_seq, tensor]
+        return kv[span % 2, (span // 2) * n_seq + block % n_seq, tensor, slot]
 
     def unit(query, out, slot, block):
         head = place[0] * heads + slot
@@ -408,9 +406,9 @@
     sides, count = isinstance(kv, (tuple, list)), len(masks)
     if sides:
         spots, _, heads, tokens, width = kv[0].shape
-        whole = jax.ShapeDtypeStruct((heads, 2, spots, 2, tokens, width), jnp.bfloat16)
+        whole = jax.ShapeDtypeStruct((2, spots, 2, heads, tokens, width), jnp.bfloat16)
     else:
-        heads, _, _, _, tokens, width = kv.shape
+        _, _, _, heads, tokens, width = kv.shape
     outs = pl.pallas_call(
         functools.partial(
             attend_kernel,
@@ -424,7 +422,7 @@
         + ([whole] if sides else []),
         in_specs=[SMEM] * 2 + ([ANY] * 2 if sides else [VMEM]) + [VMEM] * count,
         out_specs=[VMEM] * (count + sides),
-        scratch_shapes=[pltpu.SemaphoreType.DMA((heads, 2))] if sides else [],
+        scratch_shapes=[pltpu.SemaphoreType.DMA((2,))] if sides else [],
         compiler_params=pltpu.CompilerParams(vmem_limit_bytes=12 * MIB),
         cost_estimate=pl.CostEstimate(flops=1, bytes_accessed=1, transcendentals=0),
         name="attend",

time: 105 us -> 105 us (level)
  no operation moved by 1% of the time
where the time goes in v5:
time: 105 us
  waiting for transfers between devices  54 us (51%)
  starting transfers between devices  30 us (29%)
  Pallas kernels  20.4 us (19%)
    ppermute x19, waiting for transfers between devices, swap_with(): lax.ppermute(value, axes, [(source, source ^ mask) for source in range(co...  54 us
    ppermute x19, starting transfers between devices, swap_with(): lax.ppermute(value, axes, [(source, source ^ mask) for source in range(co...  30 us
    pallas_call x2, Pallas kernels, attend(): pl.pallas_call(functools.partial(attend_kernel, masks=masks, sizes=sizes,...  8.92 us
    pallas_call x2, Pallas kernels, regroup(): pl.pallas_call(functools.partial(regroup_kernel, tensors=len(tensors), ta...  6.62 us
    pallas_call x2, Pallas kernels, ungroup(): pl.pallas_call(functools.partial(ungroup_kernel, masks=masks, groups=grou...  2.9 us
  transfers between devices with their start and end apart: 19, of which 10 were waited for; matrix products, arithmetic and copies ran while one was open for 0% of the time, Pallas kernels for 15%

profile of v5, /device:TPU:12, one launch (start us, length us, event | category | flops | bytes accessed | tf_op | source)
XLA Modules:
  0.0 104.9 jit_solution(4077361658923264625)
XLA Ops:
  0.1 2.8 %regroup.3 = (bf16[2,4,128,128]{3,2,1,0:T(8,128)(2,1)}, bf16[2,4,128,128]{3,2,1,0:T(8,128)(2,1)}, bf16[2,4,128,128]{3,2,1,0:T(8,128)(2,1)}, bf16[2,4,128,128]{3,2,1,0:T(8,128)(2,1)}) custom-call(s32[2]{0:T(128)S(1)} %pad_add_fusion.1.place, bf16[128,32,128]{2,1,0:T(8,128)(2,1)} %bitcast.10, bf16[128,32,128]{2,1,0:T(8,128)(2,1)} %bitcast.12), custom_call_target="tpu_custom_call" | custom-call | flops 1 | bytes 1 | tf_op jit(solution)/shard_map/regroup/pallas_call | solution.py:235
  2.9 2.7 %collective-permute-start.5 = (bf16[2,4,128,128]{3,2,1,0:T(8,128)(2,1)}, bf16[2,4,128,128]{3,2,1,0:T(8,128)(2,1)S(1)}, u32[]{:S(2)}, u32[]{:S(2)}) collective-permute-start(bf16[2,4,128,128]{3,2,1,0:T(8,128)(2,1)} %get-tuple-element.89), channel_id=1, source_target_pairs={{0,8},{2,10},{4,12},{6,14},{8,0},{10,2},{12,4},{14,6},{1,9},{3,11}... | collective-permute-start | bytes 786440 | tf_op jit(solution)/shard_map/ppermute | solution.py:193
  5.6 1.3 %collective-permute-start.6 = (bf16[2,4,128,128]{3,2,1,0:T(8,128)(2,1)}, bf16[2,4,128,128]{3,2,1,0:T(8,128)(2,1)S(1)}, u32[]{:S(2)}, u32[]{:S(2)}) collective-permute-start(bf16[2,4,128,128]{3,2,1,0:T(8,128)(2,1)} %get-tuple-element.90), channel_id=1, source_target_pairs={{0,10},{2,8},{4,14},{6,12},{8,2},{10,0},{12,6},{14,4},{1,11},{3,9}... | collective-permute-start | bytes 786440 | tf_op jit(solution)/shard_map/ppermute | solution.py:193
  7.1 3.8 %regroup.2 = (bf16[3,4,128,128]{3,2,1,0:T(8,128)(2,1)S(1)}, bf16[3,4,128,128]{3,2,1,0:T(8,128)(2,1)}, bf16[3,4,128,128]{3,2,1,0:T(8,128)(2,1)}, bf16[3,4,128,128...) custom-call(s32[2]{0:T(128)S(1)} %pad_add_fusion.1.place, ...), custom_call_target="tpu_custom_call" | custom-call | flops 1 | bytes 1 | tf_op jit(solution)/shard_map/regroup/pallas_call | solution.py:235
  10.9 0.6 collective-permute-start.2
  12.0 2.5 %collective-permute-start.4 = (bf16[3,4,128,128]{3,2,1,0:T(8,128)(2,1)}, bf16[3,4,128,128]{3,2,1,0:T(8,128)(2,1)S(1)}, u32[]{:S(2)}, u32[]{:S(2)}) collective-permute-start(bf16[3,4,128,128]{3,2,1,0:T(8,128)(2,1)} %get-tuple-element.88), channel_id=1, source_target_pairs={{0,6},{2,4},{4,2},{6,0},{8,14},{10,12},{12,10},{14,8},{1,7},{3,5},... | collective-permute-start | bytes 1179656 | tf_op jit(solution)/shard_map/ppermute | solution.py:193
  14.5 8.2 %collective-permute-done.5 = bf16[2,4,128,128]{3,2,1,0:T(8,128)(2,1)S(1)} collective-permute-done((bf16[2,4,128,128]{3,2,1,0:T(8,128)(2,1)}, bf16[2,4,128,128]{3,2,1,0:T(8,128)(2,1)S(1)}, u32[]{:S(2)}, u32[]{:S(2)}) %collective-permute-start.5) | collective-permute-done | bytes 262176 | tf_op jit(solution)/shard_map/ppermute | solution.py:193
  23.2 5.1 %collective-permute-done.6 = bf16[2,4,128,128]{3,2,1,0:T(8,128)(2,1)S(1)} collective-permute-done((bf16[2,4,128,128]{3,2,1,0:T(8,128)(2,1)}, bf16[2,4,128,128]{3,2,1,0:T(8,128)(2,1)S(1)}, u32[]{:S(2)}, u32[]{:S(2)}) %collective-permute-start.6) | collective-permute-done | bytes 262176 | tf_op jit(solution)/shard_map/ppermute | solution.py:193
  28.3 1.4 %collective-permute-start.8 = (bf16[2,4,128,128]{3,2,1,0:T(8,128)(2,1)S(1)}, bf16[2,4,128,128]{3,2,1,0:T(8,128)(2,1)S(1)}, u32[]{:S(2)}, u32[]{:S(2)}) collective-permute-start(bf16[2,4,128,128]{3,2,1,0:T(8,128)(2,1)S(1)} %copy-done.2), channel_id=1, source_target_pairs={{0,14},{2,12},{4,10},{6,8},{8,6},{10,4},{12,2},{14,0},{1,15},{3,13... | collective-permute-start | bytes 786440 | tf_op jit(solution)/shard_map/ppermute | solution.py:193
  29.7 6.2 %collective-permute-done.7 = bf16[2,4,128,128]{3,2,1,0:T(8,128)(2,1)S(1)} collective-permute-done((bf16[2,4,128,128]{3,2,1,0:T(8,128)(2,1)S(1)}, bf16[2,4,128,128]{3,2,1,0:T(8,128)(2,1)S(1)}, u32[]{:S(2)}, u32[]{:S(2)}) %collective-permute-start.7) | collective-permute-done | bytes 262176 | tf_op jit(solution)/shard_map/ppermute | solution.py:193
  35.9 8.2 %collective-permute-start.9 = (bf16[1,4,128,128]{3,2,1,0:T(8,128)(2,1)}, bf16[1,4,128,128]{3,2,1,0:T(8,128)(2,1)S(1)}, u32[]{:S(2)}, u32[]{:S(2)}) collective-permute-start(bf16[1,4,128,128]{3,2,1,0:T(8,128)(2,1)} %get-tuple-element.95), channel_id=1, source_target_pairs={{0,8},{2,10},{4,12},{6,14},{8,0},{10,2},{12,4},{14,6},{1,9},{3,11}... | collective-permute-start | bytes 393224 | tf_op jit(solution)/shard_map/ppermute | solution.py:193
  44.1 11.3 %collective-permute-done.8 = bf16[2,4,128,128]{3,2,1,0:T(8,128)(2,1)S(1)} collective-permute-done((bf16[2,4,128,128]{3,2,1,0:T(8,128)(2,1)S(1)}, bf16[2,4,128,128]{3,2,1,0:T(8,128)(2,1)S(1)}, u32[]{:S(2)}, u32[]{:S(2)}) %collective-permute-start.8) | collective-permute-done | bytes 262176 | tf_op jit(solution)/shard_map/ppermute | solution.py:193
  55.4 1.6 %collective-permute-start.13 = (bf16[1,4,128,128]{3,2,1,0:T(8,128)(2,1)}, bf16[1,4,128,128]{3,2,1,0:T(8,128)(2,1)S(1)}, u32[]{:S(2)}, u32[]{:S(2)}) collective-permute-start(bf16[1,4,128,128]{3,2,1,0:T(8,128)(2,1)} %get-tuple-element.100), channel_id=1, source_target_pairs={{0,12},{2,14},{4,8},{6,10},{8,4},{10,6},{12,0},{14,2},{1,13},{3,15... | collective-permute-start | bytes 393224 | tf_op jit(solution)/shard_map/ppermute | solution.py:193
  57.5 6.5 %conditional.1 = (bf16[8,2,4,128,128]{4,3,2,1,0:T(8,128)(2,1)}, bf16[8,2,4,128,128]{4,3,2,1,0:T(8,128)(2,1)}) conditional(s32[]{:T(128)} %bitcast.4, (s32[2]{0:T(128)S(1)}, bf16[3,4,128,128]{3,2,1,0:T(8,128)(2,1)S(1)}, bf16[3,4,128,128]{3,2,1,0:T(8,128)(2,1)S(1)}, bf16[3,4,128,128]{3,2,1,0:T(8,128)(2,1)S(1)}, bf16[3,4,128,128]{3,2,1,0:T(8,128)(2,1)S(1)}, ...), branch_computations={%region_0.0_spmd, %region_1.0_spmd} | conditional | flops 1 | bytes 8388665 | solution.py:465
  57.5 1.9 %gather.3 = bf16[8,2,4,128,128]{4,3,2,1,0:T(8,128)(2,1)} custom-call(s32[2]{0:T(128)S(1)} %get-tuple-element.51.place, bf16[3,4,128,128]{3,2,1,0:T(8,128)(2,1)S(1)} %get-tuple-element.52.refs_0_, bf16[3,4,128,128]{3,2,1,0:T(8,128)(2,1)S(1)} %get-tuple-element.53.refs_1_, bf16[3,4,128,128]{3,2,1,0:T(8,128)(2,1)S(1)} %get-tuple-element.54.refs_2_, ...), custom_call_target="tpu_custom_call" | custom-call | flops 1 | bytes 1 | tf_op jit(solution)/shard_map/cond/branch_1_fun/gather/pallas_call | solution.py:321
  59.5 4.5 %collective-permute-done.1 = bf16[8,2,4,128,128]{4,3,2,1,0:T(8,128)(2,1)} collective-permute-done((bf16[8,2,4,128,128]{4,3,2,1,0:T(8,128)(2,1)}, bf16[8,2,4,128,128]{4,3,2,1,0:T(8,128)(2,1)}, u32[]{:S(2)}, u32[]{:S(2)}) %collective-permute-start.1) | collective-permute-done | bytes 2097184 | tf_op jit(solution)/shard_map/cond/branch_1_fun/ppermute | solution.py:193
  64.0 4.1 %collective-permute-done.10.refs_7_ = bf16[1,4,128,128]{3,2,1,0:T(8,128)(2,1)S(1)} collective-permute-done((bf16[1,4,128,128]{3,2,1,0:T(8,128)(2,1)}, bf16[1,4,128,128]{3,2,1,0:T(8,128)(2,1)S(1)}, u32[]{:S(2)}, u32[]{:S(2)}) %collective-permute-start.10) | collective-permute-done | bytes 131104 | tf_op jit(solution)/shard_map/ppermute | solution.py:193
  68.0 6.8 %attend.2 = (bf16[4,128,128]{2,1,0:T(8,128)(2,1)S(1)}, bf16[4,128,128]{2,1,0:T(8,128)(2,1)S(1)}, bf16[4,128,128]{2,1,0:T(8,128)(2,1)S(1)}, bf16[4,128,128]{2,1,0...) custom-call(s32[2]{0:T(128)S(1)} %pad_add_fusion.1.place, ...), custom_call_target="tpu_custom_call" | custom-call | flops 1 | bytes 1 | tf_op jit(solution)/shard_map/attend/pallas_call | solution.py:412
  74.9 1.2 %collective-permute-start.17 = (bf16[4,128,128]{2,1,0:T(8,128)(2,1)S(1)}, bf16[4,128,128]{2,1,0:T(8,128)(2,1)S(1)}, u32[]{:S(2)}, u32[]{:S(2)}) collective-permute-start(bf16[4,128,128]{2,1,0:T(8,128)(2,1)S(1)} %get-tuple-element.105), channel_id=1, source_target_pairs={{0,2},{2,0},{4,6},{6,4},{8,10},{10,8},{12,14},{14,12},{1,3},{3,1},... | collective-permute-start | bytes 393224 | tf_op jit(solution)/shard_map/ppermute | solution.py:193
  76.0 3.2 %collective-permute-start.18 = (bf16[4,128,128]{2,1,0:T(8,128)(2,1)S(1)}, bf16[4,128,128]{2,1,0:T(8,128)(2,1)S(1)}, u32[]{:S(2)}, u32[]{:S(2)}) collective-permute-start(bf16[4,128,128]{2,1,0:T(8,128)(2,1)S(1)} %get-tuple-element.106), channel_id=1, source_target_pairs={{0,4},{2,6},{4,0},{6,2},{8,12},{10,14},{12,8},{14,10},{1,5},{3,7},... | collective-permute-start | bytes 393224 | tf_op jit(solution)/shard_map/ppermute | solution.py:193
  79.2 0.5 collective-permute-start.11
  79.7 2.4 %collective-permute-start.12 = (bf16[4,128,128]{2,1,0:T(8,128)(2,1)S(1)}, bf16[4,128,128]{2,1,0:T(8,128)(2,1)S(1)}, u32[]{:S(2)}, u32[]{:S(2)}) collective-permute-start(bf16[4,128,128]{2,1,0:T(8,128)(2,1)S(1)} %get-tuple-element.98), channel_id=1, source_target_pairs={{0,10},{2,8},{4,14},{6,12},{8,2},{10,0},{12,6},{14,4},{1,11},{3,9}... | collective-permute-start | bytes 393224 | tf_op jit(solution)/shard_map/ppermute | solution.py:193
  82.1 0.9 collective-permute-start.19
  83.0 2.1 %attend.3 = (bf16[4,128,128]{2,1,0:T(8,128)(2,1)S(1)}, bf16[4,128,128]{2,1,0:T(8,128)(2,1)S(1)}) custom-call(s32[2]{0:T(128)S(1)} %pad_add_fusion.1.place, s32[192]{0:T(256)S(1)} %pad_add_fusion.tables, bf16[2,8,2,4,128,128]{5,4,3,2,1,0:T(8,128)(2,1)S(1)} %get-tuple-element.99.refs_0_, bf16[1,4,128,128]{3,2,1,0:T(8,128)(2,1)S(1)} %collective-permute-done.13.refs_1_, ...), custom_call_target="tpu_custom_call" | custom-call | flops 1 | bytes 1 | tf_op jit(solution)/shard_map/attend/pallas_call | solution.py:412
  85.1 1.1 %collective-permute-start.15 = (bf16[4,128,128]{2,1,0:T(8,128)(2,1)S(1)}, bf16[4,128,128]{2,1,0:T(8,128)(2,1)S(1)}, u32[]{:S(2)}, u32[]{:S(2)}) collective-permute-start(bf16[4,128,128]{2,1,0:T(8,128)(2,1)S(1)} %get-tuple-element.102), channel_id=1, source_target_pairs={{0,12},{2,14},{4,8},{6,10},{8,4},{10,6},{12,0},{14,2},{1,13},{3,15... | collective-permute-start | bytes 393224 | tf_op jit(solution)/shard_map/ppermute | solution.py:193
  86.3 1.1 %collective-permute-start.16 = (bf16[4,128,128]{2,1,0:T(8,128)(2,1)S(1)}, bf16[4,128,128]{2,1,0:T(8,128)(2,1)S(1)}, u32[]{:S(2)}, u32[]{:S(2)}) collective-permute-start(bf16[4,128,128]{2,1,0:T(8,128)(2,1)S(1)} %get-tuple-element.103), channel_id=1, source_target_pairs={{0,14},{2,12},{4,10},{6,8},{8,6},{10,4},{12,2},{14,0},{1,15},{3,13... | collective-permute-start | bytes 393224 | tf_op jit(solution)/shard_map/ppermute | solution.py:193
  87.3 4.9 %collective-permute-done.19.refs_3_ = bf16[4,128,128]{2,1,0:T(8,128)(2,1)S(1)} collective-permute-done((bf16[4,128,128]{2,1,0:T(8,128)(2,1)S(1)}, bf16[4,128,128]{2,1,0:T(8,128)(2,1)S(1)}, u32[]{:S(2)}, u32[]{:S(2)}) %collective-permute-start.19) | collective-permute-done | bytes 131104 | tf_op jit(solution)/shard_map/ppermute | solution.py:193
  92.3 1.4 %ungroup.2.refs_4_ = bf16[128,32,128]{2,1,0:T(8,128)(2,1)} custom-call(s32[2]{0:T(128)S(1)} %pad_add_fusion.1.place, bf16[4,128,128]{2,1,0:T(8,128)(2,1)S(1)} %get-tuple-element.104.refs_0_, bf16[4,128,128]{2,1,0:T(8,128)(2,1)S(1)} %collective-permute-done.17.refs_1_, bf16[4,128,128]{2,1,0:T(8,128)(2,1)S(1)} %collective-permute-done.18.refs_2_, ...), custom_call_target="tpu_custom_call" | custom-call | flops 1 | bytes 1 | tf_op jit(solution)/shard_map/ungroup/pallas_call | solution.py:280
  93.7 3.4 %collective-permute-done.12.refs_1_ = bf16[4,128,128]{2,1,0:T(8,128)(2,1)S(1)} collective-permute-done((bf16[4,128,128]{2,1,0:T(8,128)(2,1)S(1)}, bf16[4,128,128]{2,1,0:T(8,128)(2,1)S(1)}, u32[]{:S(2)}, u32[]{:S(2)}) %collective-permute-start.12) | collective-permute-done | bytes 131104 | tf_op jit(solution)/shard_map/ppermute | solution.py:193
  97.2 4.0 %collective-permute-done.15.refs_2_ = bf16[4,128,128]{2,1,0:T(8,128)(2,1)S(1)} collective-permute-done((bf16[4,128,128]{2,1,0:T(8,128)(2,1)S(1)}, bf16[4,128,128]{2,1,0:T(8,128)(2,1)S(1)}, u32[]{:S(2)}, u32[]{:S(2)}) %collective-permute-start.15) | collective-permute-done | bytes 131104 | tf_op jit(solution)/shard_map/ppermute | solution.py:193
  101.2 2.3 %collective-permute-done.16.refs_3_ = bf16[4,128,128]{2,1,0:T(8,128)(2,1)S(1)} collective-permute-done((bf16[4,128,128]{2,1,0:T(8,128)(2,1)S(1)}, bf16[4,128,128]{2,1,0:T(8,128)(2,1)S(1)}, u32[]{:S(2)}, u32[]{:S(2)}) %collective-permute-start.16) | collective-permute-done | bytes 131104 | tf_op jit(solution)/shard_map/ppermute | solution.py:193
  103.5 1.4 %ungroup.3 = bf16[128,32,128]{2,1,0:T(8,128)(2,1)} custom-call(s32[2]{0:T(128)S(1)} %pad_add_fusion.1.place, bf16[4,128,128]{2,1,0:T(8,128)(2,1)S(1)} %collective-permute-done.11.refs_0_, bf16[4,128,128]{2,1,0:T(8,128)(2,1)S(1)} %collective-permute-done.12.refs_1_, ...), custom_call_target="tpu_custom_call", output_to_operand_aliasing={{}: (5, {})} | custom-call | flops 1 | bytes 1 | tf_op jit(solution)/shard_map/ungroup/pallas_call | solution.py:280
  (30 shorter events, 1.8 us)
Async XLA Ops:
  0.0 6.8 %copy-start.4 = (s32[32,2]{0,1:T(2,128)S(1)}, s32[32,2]{0,1:T(2,128)}, u32[]{:S(2)}) copy-start(s32[32,2]{0,1:T(2,128)} %param.12) | copy-start | bytes 772
  0.0 6.9 %copy-start.5 = (s32[32,2]{0,1:T(2,128)S(1)}, s32[32,2]{0,1:T(2,128)}, u32[]{:S(2)}) copy-start(s32[32,2]{0,1:T(2,128)} %param.14) | copy-start | bytes 772
  0.0 7.0 %copy-start.1 = (s32[32]{0:T(128)S(1)}, s32[32]{0:T(128)}, u32[]{:S(2)}) copy-start(s32[32]{0:T(128)} %param.13) | copy-start | bytes 388
  0.0 7.0 %copy-start = (s32[32]{0:T(128)S(1)}, s32[32]{0:T(128)}, u32[]{:S(2)}) copy-start(s32[32]{0:T(128)} %param.15) | copy-start | bytes 388
  2.9 19.8 %copy-start.3 = (bf16[2,4,128,128]{3,2,1,0:T(8,128)(2,1)S(1)}, bf16[2,4,128,128]{3,2,1,0:T(8,128)(2,1)}, u32[]{:S(2)}) copy-start(bf16[2,4,128,128]{3,2,1,0:T(8,128)(2,1)} %get-tuple-element.91) | copy-start | bytes 786436
  2.9 25.4 %copy-start.2 = (bf16[2,4,128,128]{3,2,1,0:T(8,128)(2,1)S(1)}, bf16[2,4,128,128]{3,2,1,0:T(8,128)(2,1)}, u32[]{:S(2)}) copy-start(bf16[2,4,128,128]{3,2,1,0:T(8,128)(2,1)} %get-tuple-element.92) | copy-start | bytes 786436
  2.9 19.8 %collective-permute-start.5 = (bf16[2,4,128,128]{3,2,1,0:T(8,128)(2,1)}, bf16[2,4,128,128]{3,2,1,0:T(8,128)(2,1)S(1)}, u32[]{:S(2)}, u32[]{:S(2)}) collective-permute-start(bf16[2,4,128,128]{3,2,1,0:T(8,128)(2,1)} %get-tuple-element.89), channel_id=1, source_target_pairs={{0,8},{2,10},{4,12},{6,14},{8,0},{10,2},{12,4},{14,6},{1,9},{3,11}... | collective-permute-start | bytes 786440 | tf_op jit(solution)/shard_map/ppermute | solution.py:193
  5.6 22.8 %collective-permute-start.6 = (bf16[2,4,128,128]{3,2,1,0:T(8,128)(2,1)}, bf16[2,4,128,128]{3,2,1,0:T(8,128)(2,1)S(1)}, u32[]{:S(2)}, u32[]{:S(2)}) collective-permute-start(bf16[2,4,128,128]{3,2,1,0:T(8,128)(2,1)} %get-tuple-element.90), channel_id=1, source_target_pairs={{0,10},{2,8},{4,14},{6,12},{8,2},{10,0},{12,6},{14,4},{1,11},{3,9}... | collective-permute-start | bytes 786440 | tf_op jit(solution)/shard_map/ppermute | solution.py:193
  10.9 44.5 %collective-permute-start.2 = (bf16[3,4,128,128]{3,2,1,0:T(8,128)(2,1)}, bf16[3,4,128,128]{3,2,1,0:T(8,128)(2,1)S(1)}, u32[]{:S(2)}, u32[]{:S(2)}) collective-permute-start(bf16[3,4,128,128]{3,2,1,0:T(8,128)(2,1)} %get-tuple-element.86), channel_id=1, source_target_pairs={{0,2},{2,0},{4,6},{6,4},{8,10},{10,8},{12,14},{14,12},{1,3},{3,1},... | collective-permute-start | bytes 1179656 | tf_op jit(solution)/shard_map/ppermute | solution.py:193
  11.5 45.5 %collective-permute-start.3 = (bf16[3,4,128,128]{3,2,1,0:T(8,128)(2,1)}, bf16[3,4,128,128]{3,2,1,0:T(8,128)(2,1)S(1)}, u32[]{:S(2)}, u32[]{:S(2)}) collective-permute-start(bf16[3,4,128,128]{3,2,1,0:T(8,128)(2,1)} %get-tuple-element.87), channel_id=1, source_target_pairs={{0,4},{2,6},{4,0},{6,2},{8,12},{10,14},{12,8},{14,10},{1,5},{3,7},... | collective-permute-start | bytes 1179656 | tf_op jit(solution)/shard_map/ppermute | solution.py:193
  12.0 45.5 %collective-permute-start.4 = (bf16[3,4,128,128]{3,2,1,0:T(8,128)(2,1)}, bf16[3,4,128,128]{3,2,1,0:T(8,128)(2,1)S(1)}, u32[]{:S(2)}, u32[]{:S(2)}) collective-permute-start(bf16[3,4,128,128]{3,2,1,0:T(8,128)(2,1)} %get-tuple-element.88), channel_id=1, source_target_pairs={{0,6},{2,4},{4,2},{6,0},{8,14},{10,12},{12,10},{14,8},{1,7},{3,5},... | collective-permute-start | bytes 1179656 | tf_op jit(solution)/shard_map/ppermute | solution.py:193
  22.7 13.2 %collective-permute-start.7 = (bf16[2,4,128,128]{3,2,1,0:T(8,128)(2,1)S(1)}, bf16[2,4,128,128]{3,2,1,0:T(8,128)(2,1)S(1)}, u32[]{:S(2)}, u32[]{:S(2)}) collective-permute-start(bf16[2,4,128,128]{3,2,1,0:T(8,128)(2,1)S(1)} %copy-done.3), channel_id=1, source_target_pairs={{0,12},{2,14},{4,8},{6,10},{8,4},{10,6},{12,0},{14,2},{1,13},{3,15... | collective-permute-start | bytes 786440 | tf_op jit(solution)/shard_map/ppermute | solution.py:193
  28.3 27.0 %collective-permute-start.8 = (bf16[2,4,128,128]{3,2,1,0:T(8,128)(2,1)S(1)}, bf16[2,4,128,128]{3,2,1,0:T(8,128)(2,1)S(1)}, u32[]{:S(2)}, u32[]{:S(2)}) collective-permute-start(bf16[2,4,128,128]{3,2,1,0:T(8,128)(2,1)S(1)} %copy-done.2), channel_id=1, source_target_pairs={{0,14},{2,12},{4,10},{6,8},{8,6},{10,4},{12,2},{14,0},{1,15},{3,13... | collective-permute-start | bytes 786440 | tf_op jit(solution)/shard_map/ppermute | solution.py:193
  35.9 28.1 %collective-permute-start.9 = (bf16[1,4,128,128]{3,2,1,0:T(8,128)(2,1)}, bf16[1,4,128,128]{3,2,1,0:T(8,128)(2,1)S(1)}, u32[]{:S(2)}, u32[]{:S(2)}) collective-permute-start(bf16[1,4,128,128]{3,2,1,0:T(8,128)(2,1)} %get-tuple-element.95), channel_id=1, source_target_pairs={{0,8},{2,10},{4,12},{6,14},{8,0},{10,2},{12,4},{14,6},{1,9},{3,11}... | collective-permute-start | bytes 393224 | tf_op jit(solution)/shard_map/ppermute | solution.py:193
  55.3 12.7 %collective-permute-start.10 = (bf16[1,4,128,128]{3,2,1,0:T(8,128)(2,1)}, bf16[1,4,128,128]{3,2,1,0:T(8,128)(2,1)S(1)}, u32[]{:S(2)}, u32[]{:S(2)}) collective-permute-start(bf16[1,4,128,128]{3,2,1,0:T(8,128)(2,1)} %get-tuple-element.96), channel_id=1, source_target_pairs={{0,10},{2,8},{4,14},{6,12},{8,2},{10,0},{12,6},{14,4},{1,11},{3,9}... | collective-permute-start | bytes 393224 | tf_op jit(solution)/shard_map/ppermute | solution.py:193
  55.4 24.3 %collective-permute-start.13 = (bf16[1,4,128,128]{3,2,1,0:T(8,128)(2,1)}, bf16[1,4,128,128]{3,2,1,0:T(8,128)(2,1)S(1)}, u32[]{:S(2)}, u32[]{:S(2)}) collective-permute-start(bf16[1,4,128,128]{3,2,1,0:T(8,128)(2,1)} %get-tuple-element.100), channel_id=1, source_target_pairs={{0,12},{2,14},{4,8},{6,10},{8,4},{10,6},{12,0},{14,2},{1,13},{3,15... | collective-permute-start | bytes 393224 | tf_op jit(solution)/shard_map/ppermute | solution.py:193
  57.0 25.1 %collective-permute-start.14 = (bf16[1,4,128,128]{3,2,1,0:T(8,128)(2,1)}, bf16[1,4,128,128]{3,2,1,0:T(8,128)(2,1)S(1)}, u32[]{:S(2)}, u32[]{:S(2)}) collective-permute-start(bf16[1,4,128,128]{3,2,1,0:T(8,128)(2,1)} %get-tuple-element.101), channel_id=1, source_target_pairs={{0,14},{2,12},{4,10},{6,8},{8,6},{10,4},{12,2},{14,0},{1,15},{3,13... | collective-permute-start | bytes 393224 | tf_op jit(solution)/shard_map/ppermute | solution.py:193
  59.4 4.6 %collective-permute-start.1 = (bf16[8,2,4,128,128]{4,3,2,1,0:T(8,128)(2,1)}, bf16[8,2,4,128,128]{4,3,2,1,0:T(8,128)(2,1)}, u32[]{:S(2)}, u32[]{:S(2)}) collective-permute-start(bf16[8,2,4,128,128]{4,3,2,1,0:T(8,128)(2,1)} %gather.3), channel_id=1, source_target_pairs={{0,1},{1,0},{2,3},{3,2},{4,5},{5,4},{6,7},{7,6},{8,9},{9,8},{10,11... | collective-permute-start | bytes 6291464 | tf_op jit(solution)/shard_map/cond/branch_1_fun/ppermute | solution.py:193
  74.9 10.3 %collective-permute-start.17 = (bf16[4,128,128]{2,1,0:T(8,128)(2,1)S(1)}, bf16[4,128,128]{2,1,0:T(8,128)(2,1)S(1)}, u32[]{:S(2)}, u32[]{:S(2)}) collective-permute-start(bf16[4,128,128]{2,1,0:T(8,128)(2,1)S(1)} %get-tuple-element.105), channel_id=1, source_target_pairs={{0,2},{2,0},{4,6},{6,4},{8,10},{10,8},{12,14},{14,12},{1,3},{3,1},... | collective-permute-start | bytes 393224 | tf_op jit(solution)/shard_map/ppermute | solution.py:193
  76.0 10.2 %collective-permute-start.18 = (bf16[4,128,128]{2,1,0:T(8,128)(2,1)S(1)}, bf16[4,128,128]{2,1,0:T(8,128)(2,1)S(1)}, u32[]{:S(2)}, u32[]{:S(2)}) collective-permute-start(bf16[4,128,128]{2,1,0:T(8,128)(2,1)S(1)} %get-tuple-element.106), channel_id=1, source_target_pairs={{0,4},{2,6},{4,0},{6,2},{8,12},{10,14},{12,8},{14,10},{1,5},{3,7},... | collective-permute-start | bytes 393224 | tf_op jit(solution)/shard_map/ppermute | solution.py:193
  79.2 14.5 %collective-permute-start.11 = (bf16[4,128,128]{2,1,0:T(8,128)(2,1)S(1)}, bf16[4,128,128]{2,1,0:T(8,128)(2,1)S(1)}, u32[]{:S(2)}, u32[]{:S(2)}) collective-permute-start(bf16[4,128,128]{2,1,0:T(8,128)(2,1)S(1)} %get-tuple-element.97), channel_id=1, source_target_pairs={{0,8},{2,10},{4,12},{6,14},{8,0},{10,2},{12,4},{14,6},{1,9},{3,11}... | collective-permute-start | bytes 393224 | tf_op jit(solution)/shard_map/ppermute | solution.py:193
  79.7 17.5 %collective-permute-start.12 = (bf16[4,128,128]{2,1,0:T(8,128)(2,1)S(1)}, bf16[4,128,128]{2,1,0:T(8,128)(2,1)S(1)}, u32[]{:S(2)}, u32[]{:S(2)}) collective-permute-start(bf16[4,128,128]{2,1,0:T(8,128)(2,1)S(1)} %get-tuple-element.98), channel_id=1, source_target_pairs={{0,10},{2,8},{4,14},{6,12},{8,2},{10,0},{12,6},{14,4},{1,11},{3,9}... | collective-permute-start | bytes 393224 | tf_op jit(solution)/shard_map/ppermute | solution.py:193
  82.1 10.2 %collective-permute-start.19 = (bf16[4,128,128]{2,1,0:T(8,128)(2,1)S(1)}, bf16[4,128,128]{2,1,0:T(8,128)(2,1)S(1)}, u32[]{:S(2)}, u32[]{:S(2)}) collective-permute-start(bf16[4,128,128]{2,1,0:T(8,128)(2,1)S(1)} %get-tuple-element.107), channel_id=1, source_target_pairs={{0,6},{2,4},{4,2},{6,0},{8,14},{10,12},{12,10},{14,8},{1,7},{3,5},... | collective-permute-start | bytes 393224 | tf_op jit(solution)/shard_map/ppermute | solution.py:193
  85.1 16.0 %collective-permute-start.15 = (bf16[4,128,128]{2,1,0:T(8,128)(2,1)S(1)}, bf16[4,128,128]{2,1,0:T(8,128)(2,1)S(1)}, u32[]{:S(2)}, u32[]{:S(2)}) collective-permute-start(bf16[4,128,128]{2,1,0:T(8,128)(2,1)S(1)} %get-tuple-element.102), channel_id=1, source_target_pairs={{0,12},{2,14},{4,8},{6,10},{8,4},{10,6},{12,0},{14,2},{1,13},{3,15... | collective-permute-start | bytes 393224 | tf_op jit(solution)/shard_map/ppermute | solution.py:193
  86.3 17.2 %collective-permute-start.16 = (bf16[4,128,128]{2,1,0:T(8,128)(2,1)S(1)}, bf16[4,128,128]{2,1,0:T(8,128)(2,1)S(1)}, u32[]{:S(2)}, u32[]{:S(2)}) collective-permute-start(bf16[4,128,128]{2,1,0:T(8,128)(2,1)S(1)} %get-tuple-element.103), channel_id=1, source_target_pairs={{0,14},{2,12},{4,10},{6,8},{8,6},{10,4},{12,2},{14,0},{1,15},{3,13... | collective-permute-start | bytes 393224 | tf_op jit(solution)/shard_map/ppermute | solution.py:193
